TPU v7x, 32 devices: a whole 2x2x4 slice. The times are simulated.
32 devices in a mesh: dp: 16 (over z, y, x), tensor: 2 (over core).
Axes of the slice: x: 2, y: 2, z: 4, core: 2. Of those that a mesh axis runs over, the one named last changes fastest.
Arguments:
- latents: bfloat16 [65536, 512], P('dp'), may hold values from -6 to 6
- scene_len: int32 [128], P('dp'), may hold values from 65 to 512, as said below
- attn_gain: bfloat16 [512], replicated, may hold values from 0.25 to 1.75
- attn_shift: bfloat16 [512], replicated, may hold values from -1.75 to 1.75
- qkv_weight: bfloat16 [3, 512, 512], P(None, 'tensor'), may hold values from -0.25 to 0.25
- out_weight: bfloat16 [512, 512], P('tensor'), may hold values from -1 to 1
- out_bias: bfloat16 [512], replicated, may hold values from -1.75 to 1.75
- mlp_gain: bfloat16 [512], replicated, may hold values from 0.25 to 1.75
- mlp_shift: bfloat16 [512], replicated, may hold values from -1.75 to 1.75
- up_weight: bfloat16 [2048, 512], P('tensor'), may hold values from -0.25 to 0.25
- up_bias: bfloat16 [2048], P('tensor'), may hold values from -3 to 3
- down_weight: bfloat16 [2048, 512], P('tensor'), may hold values from -0.1875 to 0.1875
- down_bias: bfloat16 [512], replicated, may hold values from -1.75 to 1.75
- cotangent: bfloat16 [65536, 512], P('dp'), may hold values from -6 to 6
Outputs:
- block_out: bfloat16 [65536, 512], P(('dp', 'tensor'))
- grad_latents: float32 [65536, 512], P(('dp', 'tensor'))
- grad_attn_gain: float32 [512], replicated
- grad_attn_shift: float32 [512], replicated
- grad_qkv: float32 [3, 512, 512], P(None, 'tensor')
- grad_out_weight: float32 [512, 512], P('tensor')
- grad_out_bias: float32 [512], replicated
- grad_mlp_gain: float32 [512], replicated
- grad_mlp_shift: float32 [512], replicated
- grad_up_weight: float32 [2048, 512], P('tensor')
- grad_up_bias: float32 [2048], P('tensor')
- grad_down_weight: float32 [2048, 512], P('tensor')
- grad_down_bias: float32 [512], replicated
Inputs may be any that keep to these rules, and one draw needn't show every extreme that they name: `scene_len`: count of valid latents of each scene; the scene's key mask keeps keys below it and masks those at or beyond it, queries are not masked. Some scene has all 512 valid.
All inputs are finite; a program needn't handle non-finite values.
Results may differ from a plain program's by a relative error of at most 0.011.
Values may be sent and summed in bfloat16 or wider, within the bound.
No kernel may reach another device: no remote copies, remote signals or barrier semaphores. Data moves between devices by JAX's collectives and lax.ppermute only.
A program may use at most 192 MiB of HBM per device.

v0:
```python
import jax
import jax.numpy as jnp
from jax import lax
from jax.sharding import PartitionSpec as P

HD = 64
LAT = 512


EPS = 1e-05
NEG = -1e30


def layer_norm(values, gain_row, shift_row):
    values = values.astype(jnp.float32)
    centre = jnp.mean(values, -1, keepdims=True)
    centred = values - centre
    spread = jnp.mean(centred * centred, -1, keepdims=True)
    return centred * lax.rsqrt(spread + EPS) * gain_row + shift_row


def exact_gelu(values):
    return jax.nn.gelu(values, approximate=False)


def masked_scores(q_rows, k_rows, length):
    scores = jnp.einsum(
        "qhd,khd->hqk", q_rows, k_rows, preferred_element_type=jnp.float32
    ) * HD ** (-0.5)
    allowed = jnp.arange(scores.shape[-1]) < length
    return jnp.where(allowed[None, None, :], scores, NEG)


def attend_forward(q_all, k_all, v_all, lengths):
    layout = (lengths.shape[0], LAT, q_all.shape[1] // HD, HD)

    def one_scene(pieces):
        q_rows, k_rows, v_rows, length = pieces
        scores = masked_scores(q_rows, k_rows, length)
        highest = jnp.max(scores, -1, keepdims=True)
        exponent = jnp.exp(scores - highest)
        partition = jnp.sum(exponent, -1, keepdims=True)
        prob_low = (exponent / partition).astype(jnp.bfloat16)
        output = jnp.einsum("hqk,khd->qhd", prob_low, v_rows, preferred_element_type=jnp.float32)
        return (output.astype(jnp.bfloat16), (highest + jnp.log(partition))[..., 0])

    outputs, logsums = lax.map(
        one_scene, (q_all.reshape(layout), k_all.reshape(layout), v_all.reshape(layout), lengths)
    )
    return (outputs.reshape(q_all.shape), logsums)


def attend_back(q_all, k_all, v_all, grad_all, logsums, lengths):
    layout = (lengths.shape[0], LAT, q_all.shape[1] // HD, HD)
    factor = HD ** (-0.5)

    def one_scene(pieces):
        q_rows, k_rows, v_rows, grad_rows, logsum, length = pieces
        prob_rows = jnp.exp(masked_scores(q_rows, k_rows, length) - logsum[..., None])
        grad_probs = jnp.einsum(
            "qhd,khd->hqk", grad_rows, v_rows, preferred_element_type=jnp.float32
        )
        row_inner = jnp.sum(prob_rows * grad_probs, -1, keepdims=True)
        grad_scores = (prob_rows * (grad_probs - row_inner)).astype(jnp.bfloat16)
        grad_query = (
            jnp.einsum("hqk,khd->qhd", grad_scores, k_rows, preferred_element_type=jnp.float32)
            * factor
        )
        grad_keys = (
            jnp.einsum("hqk,qhd->khd", grad_scores, q_rows, preferred_element_type=jnp.float32)
            * factor
        )
        grad_values = jnp.einsum(
            "hqk,qhd->khd",
            prob_rows.astype(jnp.bfloat16),
            grad_rows,
            preferred_element_type=jnp.float32,
        )
        return jnp.stack([grad_query, grad_keys, grad_values]).astype(jnp.bfloat16)

    grad_parts = lax.map(
        one_scene,
        (
            q_all.reshape(layout),
            k_all.reshape(layout),
            v_all.reshape(layout),
            grad_all.reshape(layout),
            logsums,
            lengths,
        ),
    )
    return jnp.moveaxis(grad_parts, 1, 0).reshape(3, q_all.shape[0], q_all.shape[1])


def run_layer(rows_in, own_rows, cot_in, cot_own, lengths, params, reducers, collect):
    (
        attn_gain,
        attn_shift,
        qkv_weight,
        out_weight,
        out_bias,
        mlp_gain,
        mlp_shift,
        up_weight,
        up_bias,
        down_weight,
        down_bias,
    ) = params
    gain_one = attn_gain.astype(jnp.float32)
    shift_one = attn_shift.astype(jnp.float32)
    gain_two = mlp_gain.astype(jnp.float32)
    shift_two = mlp_shift.astype(jnp.float32)
    normed_one = layer_norm(rows_in, gain_one, shift_one).astype(jnp.bfloat16)
    projected = jnp.einsum(
        "rd,thd->trh", normed_one, qkv_weight, preferred_element_type=jnp.float32
    ).astype(jnp.bfloat16)
    attended, logsums = attend_forward(projected[0], projected[1], projected[2], lengths)

    def attn_term(start, count):
        return jnp.dot(attended, out_weight, preferred_element_type=jnp.float32)

    own_float = own_rows.astype(jnp.float32)
    hidden_one = own_float + reducers[0](attn_term) + out_bias.astype(jnp.float32)
    normed_two, norm_two_pull = jax.vjp(layer_norm, hidden_one, gain_two, shift_two)
    mlp_input = collect[0](normed_two.astype(jnp.bfloat16))
    pre_act = jnp.einsum(
        "rd,fd->rf", mlp_input, up_weight, preferred_element_type=jnp.float32
    ) + up_bias.astype(jnp.float32)
    activated, gelu_pull = jax.vjp(exact_gelu, pre_act)
    act_low = activated.astype(jnp.bfloat16)

    def mlp_term(start, count):
        return jnp.dot(act_low, down_weight, preferred_element_type=jnp.float32)

    block_out = (hidden_one + reducers[1](mlp_term) + down_bias.astype(jnp.float32)).astype(
        jnp.bfloat16
    )
    grad_down = jnp.einsum("rf,rd->fd", act_low, cot_in, preferred_element_type=jnp.float32)
    grad_act = jnp.einsum("rd,fd->rf", cot_in, down_weight, preferred_element_type=jnp.float32)
    grad_pre = gelu_pull(grad_act)[0].astype(jnp.bfloat16)
    grad_up_bias = jnp.sum(grad_pre, 0, dtype=jnp.float32)
    grad_up = jnp.einsum("rf,rd->fd", grad_pre, mlp_input, preferred_element_type=jnp.float32)

    def mlp_back_term(start, count):
        return jnp.dot(grad_pre, up_weight, preferred_element_type=jnp.float32)

    grad_normed_two = reducers[2](mlp_back_term)
    grad_from_norm, grad_mlp_gain, grad_mlp_shift = norm_two_pull(grad_normed_two)
    cot_float = cot_own.astype(jnp.float32)
    grad_hidden = cot_float + grad_from_norm
    grad_branch = collect[1](grad_hidden.astype(jnp.bfloat16))
    grad_out = jnp.einsum("rh,rd->hd", attended, grad_branch, preferred_element_type=jnp.float32)
    grad_attended = jnp.einsum(
        "rd,hd->rh", grad_branch, out_weight, preferred_element_type=jnp.float32
    ).astype(jnp.bfloat16)
    grad_projected = attend_back(
        projected[0], projected[1], projected[2], grad_attended, logsums, lengths
    )
    grad_qkv = jnp.einsum(
        "trh,rd->thd", grad_projected, normed_one, preferred_element_type=jnp.float32
    )

    def attn_back_term(start, count):
        return jnp.einsum(
            "trh,thd->rd", grad_projected, qkv_weight, preferred_element_type=jnp.float32
        )

    grad_normed_one = reducers[3](attn_back_term)
    unused_value, norm_one_pull = jax.vjp(layer_norm, own_float, gain_one, shift_one)
    grad_from_first, grad_attn_gain, grad_attn_shift = norm_one_pull(grad_normed_one)
    grad_latents = grad_hidden + grad_from_first
    local_grads = (grad_qkv, grad_out, grad_up, grad_up_bias, grad_down)
    shared = (
        grad_attn_gain,
        grad_attn_shift,
        jnp.sum(grad_hidden, 0),
        grad_mlp_gain,
        grad_mlp_shift,
        jnp.sum(cot_float, 0),
    )
    return (block_out, grad_latents, local_grads, shared)


def body(
    latents,
    scene_len,
    attn_gain,
    attn_shift,
    qkv_weight,
    out_weight,
    out_bias,
    mlp_gain,
    mlp_shift,
    up_weight,
    up_bias,
    down_weight,
    down_bias,
    cotangent,
):
    pieces_count = lax.axis_size("tensor")
    own_count = latents.shape[0] // pieces_count
    own_start = lax.axis_index("tensor") * own_count
    own_rows = lax.dynamic_slice_in_dim(latents, own_start, own_count, 0)
    cot_own = lax.dynamic_slice_in_dim(cotangent, own_start, own_count, 0)
    params = (
        attn_gain,
        attn_shift,
        qkv_weight,
        out_weight,
        out_bias,
        mlp_gain,
        mlp_shift,
        up_weight,
        up_bias,
        down_weight,
        down_bias,
    )
    reducers = (
        lambda term_fn: lax.psum_scatter(
            term_fn(jnp.int32(0), own_count * lax.axis_size("tensor")),
            "tensor",
            scatter_dimension=0,
            tiled=True,
        ),
        lambda term_fn: lax.psum_scatter(
            term_fn(jnp.int32(0), own_count * lax.axis_size("tensor")).astype(jnp.bfloat16),
            "tensor",
            scatter_dimension=0,
            tiled=True,
        ).astype(jnp.float32),
        lambda term_fn: lax.psum_scatter(
            term_fn(jnp.int32(0), own_count * lax.axis_size("tensor")),
            "tensor",
            scatter_dimension=0,
            tiled=True,
        ),
        lambda term_fn: lax.psum_scatter(
            term_fn(jnp.int32(0), own_count * lax.axis_size("tensor")),
            "tensor",
            scatter_dimension=0,
            tiled=True,
        ),
    )
    collect = (
        lambda values: lax.all_gather(values, "tensor", axis=0, tiled=True),
        lambda values: lax.all_gather(values, "tensor", axis=0, tiled=True),
    )
    block_out, grad_latents, local_grads, shared = run_layer(
        latents, own_rows, cotangent, cot_own, scene_len, params, reducers, collect
    )
    local_grads = lax.psum(
        (local_grads[0], local_grads[1], local_grads[2], local_grads[3], local_grads[4]), "dp"
    )
    shared = lax.psum(
        (shared[0], shared[1], shared[2], shared[3], shared[4], shared[5]), ("dp", "tensor")
    )
    return (
        block_out,
        grad_latents,
        shared[0],
        shared[1],
        local_grads[0],
        local_grads[1],
        shared[2],
        shared[3],
        shared[4],
        local_grads[2],
        local_grads[3],
        local_grads[4],
        shared[5],
    )


def solution(mesh):
    placed = (
        P("dp", None),
        P("dp"),
        P(),
        P(),
        P(None, "tensor", None),
        P("tensor", None),
        P(),
        P(),
        P(),
        P("tensor", None),
        P("tensor"),
        P("tensor", None),
        P(),
        P("dp", None),
    )
    return jax.shard_map(
        body,
        mesh=mesh,
        in_specs=placed,
        out_specs=(
            P(("dp", "tensor"), None),
            P(("dp", "tensor"), None),
            P(),
            P(),
            P(None, "tensor", None),
            P("tensor", None),
            P(),
            P(),
            P(),
            P("tensor", None),
            P("tensor"),
            P("tensor", None),
            P(),
        ),
        check_vma=False,
    )
```

profile of v0, /device:TPU:0, one launch (start us, length us, event | category | flops | bytes accessed | tf_op | source)
XLA Modules:
  0.0 710.7 jit_solution(14364615661905591841)
XLA Ops:
  14.5 4.9 fusion.70
  21.8 7.1 reshape.202
  28.9 6.9 copy.46
  39.0 5.6 copy.47
  44.5 7.1 reshape.204
  51.6 6.9 copy.48
  58.6 74.2 %while.22 = (s32[]{:T(128)}, bf16[8,512,4,64]{1,3,2,0:T(8,128)(2,1)}, f32[8,4,512]{2,1,0:T(4,128)}, bf16[8,512,4,64]{1,3,2,0:T(8,128)(2,1)}, s32[8]{0:T(128)S(1)...) while((s32[]{:T(128)}, bf16[8,512,4,64]{1,3,2,0:T(8,128)(2,1)}, ...), condition=%wide.region_5.6_spmd, body=%wide.region_2.5_spmd.sunk | while | flops 281147904 | bytes 13701733 | solution.py:47
  138.6 4.5 fusion.90
  143.8 19.0 %reduce-scatter.5.cloned.1.call-done = f32[2048,512]{1,0:T(8,128)} async-done(((f32[4096,512]{1,0:T(8,128)}), f32[2048,512]{1,0:T(8,128)}) %reduce-scatter.5.cloned.1.call-update) | async-done | bytes 4194320 | tf_op jit(solution)/shard_map/reduce_scatter | solution.py:219
  162.8 4.6 fusion.87
  171.9 15.0 %all-gather.3.cloned.1.call-done = bf16[4096,512]{1,0:T(8,128)(2,1)} async-done(((bf16[2048,512]{1,0:T(8,128)(2,1)}), bf16[4096,512]{1,0:T(8,128)(2,1)}) %all-gather.3.cloned.1.call-update) | async-done | bytes 4194320 | tf_op jit(solution)/shard_map/all_gather | solution.py:245
  187.0 6.5 fusion.91
  193.5 44.3 %convert_reduce_fusion = (f32[1024]{0:T(1024)S(1)}, bf16[4096,1024]{1,0:T(8,128)(2,1)}, f32[4096,1024]{1,0:T(8,128)}) fusion(f32[4096,1024]{1,0:T(8,128)S(1)} %fusion.91, f32[1024]{0:T(1024)S(1)} %convert_element_type.100, bf16[4096,512]{1,0:T(8,128)(2,1)S(1)} %copy-done.13, bf16[1024,512]{1,0:T(8,128)(2,1)S(1)} %copy-done), kind=kOutput, calls=%fused_computation.64 | convolution fusion | flops 4609539072 | bytes 47194112 | tf_op jit(solution)/shard_map/rd,fd->rf/dot_general | solution.py:139
  237.9 10.2 %fusion.92 = f32[4096,512]{1,0:T(8,128)} fusion(bf16[4096,1024]{1,0:T(8,128)(2,1)} %get-tuple-element.177, bf16[1024,512]{1,0:T(8,128)(2,1)S(1)} %copy-done.45), kind=kOutput, calls=%fused_computation.137 | convolution fusion | flops 4294967296 | bytes 17825792 | tf_op jit(solution)/shard_map/dot_general | solution.py:145
  248.1 13.8 %multiply_convert_fusion.1 = bf16[4096,1024]{1,0:T(8,128)(2,1)S(1)} fusion(f32[4096,1024]{1,0:T(8,128)} %get-tuple-element.178, f32[4096,1024]{1,0:T(8,128)} %copy-done.9, f32[1024]{0:T(1024)S(1)} %convert_element_type.100), kind=kLoop, calls=%fused_computation.66 | loop fusion | flops 16777216 | bytes 41947136 | tf_op jit(solution)/shard_map/convert_element_type | solution.py:130
  265.9 6.1 convolution_convert_fusion.1
  277.0 8.3 %reduce-scatter.7.cloned.1.call-done = bf16[2048,512]{1,0:T(8,128)(2,1)} async-done(((bf16[4096,512]{1,0:T(8,128)(2,1)}), bf16[2048,512]{1,0:T(8,128)(2,1)}) %reduce-scatter.7.cloned.1.call-update) | async-done | bytes 2097168 | tf_op jit(solution)/shard_map/reduce_scatter | solution.py:225
  285.3 6.0 fusion.86
  295.3 15.1 %all-gather.5.cloned.1.call-done = bf16[4096,512]{1,0:T(8,128)(2,1)} async-done(((bf16[2048,512]{1,0:T(8,128)(2,1)}), bf16[4096,512]{1,0:T(8,128)(2,1)}) %all-gather.5.cloned.1.call-update) | async-done | bytes 4194320 | tf_op jit(solution)/shard_map/all_gather | solution.py:246
  317.5 5.6 copy.53
  323.1 102.5 %while.23 = (s32[]{:T(128)}, bf16[8,3,512,4,64]{2,4,3,1,0:T(8,128)(2,1)}, bf16[8,512,4,64]{1,3,2,0:T(8,128)(2,1)}, s32[8]{0:T(128)S(1)}, bf16[8,512,4,64]{1,3,2,...) while((s32[]{:T(128)}, ...), condition=%wide.region_15.16_spmd, body=%wide.region_13.15_spmd.sunk | while | flops 689830400 | bytes 35714676 | solution.py:81
  425.6 9.6 %copy.55 = bf16[3,8,512,4,64]{2,1,4,3,0:T(8,128)(2,1)} copy(bf16[3,8,512,4,64]{2,4,3,0,1:T(8,128)(2,1)} %bitcast.21) | data formatting | bytes 12582912 | tf_op jit(solution)/shard_map/transpose | solution.py:92
  435.2 10.5 %reshape.198 = bf16[3,4096,256]{1,2,0:T(8,128)(2,1)} reshape(bf16[3,8,512,4,64]{2,1,4,3,0:T(8,128)(2,1)} %copy.55) | data formatting | bytes 12582912 | tf_op jit(solution)/shard_map/reshape | solution.py:92
  445.7 8.7 %convolution_bitcast_fusion = f32[4096,512]{1,0:T(8,128)} fusion(bf16[3,4096,256]{1,2,0:T(8,128)(2,1)} %reshape.198, bf16[3,256,512]{2,1,0:T(8,128)(2,1)S(1)} %copy-done.47), kind=kOutput, calls=%fused_computation.89 | convolution fusion | flops 3221225472 | bytes 15466496 | tf_op jit(solution)/shard_map/trh,thd->rd/dot_general | solution.py:164
  454.5 10.6 %fusion.95 = f32[1024,512]{1,0:T(8,128)} fusion(bf16[4096,1024]{1,0:T(8,128)(2,1)} %copy-done.12, bf16[4096,512]{1,0:T(8,128)(2,1)} %param.31), kind=kOutput, calls=%fused_computation.140 | convolution fusion | flops 4294967296 | bytes 14680064 | tf_op jit(solution)/shard_map/rf,rd->fd/dot_general | solution.py:138
  465.0 9.4 %fusion.94 = f32[1024,512]{1,0:T(8,128)} fusion(bf16[4096,1024]{1,0:T(8,128)(2,1)} %get-tuple-element.177, bf16[4096,512]{1,0:T(8,128)(2,1)S(1)} %copy-done.42), kind=kOutput, calls=%fused_computation.139 | convolution fusion | flops 4294967296 | bytes 14680064 | tf_op jit(solution)/shard_map/rf,rd->fd/dot_general | solution.py:142
  476.7 4.7 fusion.77
  482.1 44.8 %psum.85 = f32[1024]{0:T(1024)} all-reduce(f32[1024]{0:T(1024)S(1)} %get-tuple-element.176), channel_id=1, replica_groups=mesh['dp'=16,'tensor'=2] {'dp'}, use_global_device_ids=true, to_apply=%region_35.36 | all-reduce | flops 1024 | bytes 8192 | tf_op jit(solution)/shard_map/psum | solution.py:251
  531.0 4.3 fusion.74
  535.4 5.3 convert_reduce_fusion.3
  540.7 37.9 %all-reduce = (f32[512]{0:T(512)}, f32[512]{0:T(512)}, f32[512]{0:T(512)}, f32[512]{0:T(512)}, f32[512]{0:T(512)}, /*index=5*/f32[512]{0:T(512)}) all-reduce(f32[512]{0:T(512)S(1)} %get-tuple-element.126, f32[512]{0:T(512)S(1)} %get-tuple-element.132, ...), channel_id=1, replica_groups=mesh['dp'=16,'tensor'=2] {'dp','tensor'}, use_global_device_ids=true, to_apply=%region_22.23 | all-reduce | flops 3072 | bytes 24576 | tf_op jit(solution)/shard_map/psum | solution.py:254
  578.6 117.7 %all-reduce.4.cloned.1.call-done = (f32[3,256,512]{2,1,0:T(8,128)}, f32[256,512]{1,0:T(8,128)}, f32[1024,512]{1,0:T(8,128)}, f32[1024,512]{1,0:T(8,128)}) async-done(((f32[3,256,512]{2,1,0:T(8,128)}, f32[256,512]{1,0:T(8,128)}, f32[1024,512]{1,0:T(8,128)}, f32[1024,512]{1,0:T(8,128)}), (f32[3,256,512]{2,1,0:T(8,128)}, f32[256,512]{1,0:T(8,128)}, f32[1024,512]{1,0:T(8,128)}, ...) | async-done | bytes 6291472 | tf_op jit(solution)/shard_map/psum | solution.py:251
  (286 shorter events, 221.2 us)
Async XLA Ops:
  7.2 186.3 %copy-start = (bf16[1024,512]{1,0:T(8,128)(2,1)S(1)}, bf16[1024,512]{1,0:T(8,128)(2,1)}, u32[]{:S(2)}) copy-start(bf16[1024,512]{1,0:T(8,128)(2,1)} %param.29) | copy-start | bytes 3145732
  7.2 155.6 %reduce-scatter.5.cloned.1.call-start = ((), (), s32[]{:S(2)}) async-start(), calls=%async_computation.4 | async-start | bytes 12582912 | tf_op jit(solution)/shard_map/reduce_scatter | solution.py:219
  8.1 5.2 copy-start.30
  8.1 5.2 copy-start.37
  8.1 6.4 copy-start.46
  51.6 6.9 copy-start.48
  132.8 4.5 copy-start.8
  132.8 5.8 copy-start.17
  143.1 43.8 %all-gather.3.cloned.1.call-start = ((), (), s32[]{:S(2)}) async-start(), calls=%async_computation.5 | async-start | bytes 6291456 | tf_op jit(solution)/shard_map/all_gather | solution.py:245
  143.8 25.6 %copy-start.27 = (f32[512]{0:T(512)}, f32[512]{0:T(512)S(1)}, u32[]{:S(2)}) copy-start(f32[512]{0:T(512)S(1)} %convert_element_type.97) | copy-start | bytes 6148
  170.1 16.9 %copy-start.44 = (bf16[1024,512]{1,0:T(8,128)(2,1)S(1)}, bf16[1024,512]{1,0:T(8,128)(2,1)}, u32[]{:S(2)}) copy-start(bf16[1024,512]{1,0:T(8,128)(2,1)} %param.27) | copy-start | bytes 3145732
  171.8 100.8 %reduce-scatter.9.cloned.1.call-start = ((), (), s32[]{:S(2)}) async-start(), calls=%async_computation.7 | async-start | bytes 12582912 | tf_op jit(solution)/shard_map/reduce_scatter | solution.py:231
  186.9 6.6 copy-start.13
  193.5 44.4 %copy-start.9 = (f32[4096,1024]{1,0:T(8,128)}, f32[4096,1024]{1,0:T(8,128)S(1)}, u32[]{:S(2)}) copy-start(f32[4096,1024]{1,0:T(8,128)S(1)} %fusion.91) | copy-start | bytes 50331652
  193.5 44.4 %copy-start.45 = (bf16[1024,512]{1,0:T(8,128)(2,1)S(1)}, bf16[1024,512]{1,0:T(8,128)(2,1)}, u32[]{:S(2)}) copy-start(bf16[1024,512]{1,0:T(8,128)(2,1)} %param.27) | copy-start | bytes 3145732
  248.1 37.2 %reduce-scatter.7.cloned.1.call-start = ((), (), s32[]{:S(2)}) async-start(), calls=%async_computation.6 | async-start | bytes 6291456 | tf_op jit(solution)/shard_map/reduce_scatter | solution.py:225
  272.0 38.4 %all-gather.5.cloned.1.call-start = ((), (), s32[]{:S(2)}) async-start(), calls=%async_computation.8 | async-start | bytes 6291456 | tf_op jit(solution)/shard_map/all_gather | solution.py:246
  285.3 8.0 %copy-start.14 = (bf16[4096,512]{1,0:T(8,128)(2,1)S(1)}, bf16[4096,512]{1,0:T(8,128)(2,1)}, u32[]{:S(2)}) copy-start(bf16[4096,512]{1,0:T(8,128)(2,1)} %param.31) | copy-start | bytes 12582916
  293.3 17.1 %copy-start.18 = (bf16[256,512]{1,0:T(8,128)(2,1)S(1)}, bf16[256,512]{1,0:T(8,128)(2,1)}, u32[]{:S(2)}) copy-start(bf16[256,512]{1,0:T(8,128)(2,1)} %param.23) | copy-start | bytes 786436
  295.2 231.6 %reduce-scatter.11.cloned.1.call-start = ((), (), s32[]{:S(2)}) async-start(), calls=%async_computation.9 | async-start | bytes 12582912 | tf_op jit(solution)/shard_map/reduce_scatter | solution.py:237
  317.5 5.6 copy-start.49
  435.2 10.5 %copy-start.47 = (bf16[3,256,512]{2,1,0:T(8,128)(2,1)S(1)}, bf16[3,256,512]{2,1,0:T(8,128)(2,1)}, u32[]{:S(2)}) copy-start(bf16[3,256,512]{2,1,0:T(8,128)(2,1)} %param.22) | copy-start | bytes 2359300
  454.4 241.9 %all-reduce.4.cloned.1.call-start = ((), (), s32[]{:S(2)}) async-start(), calls=%async_computation.10 | async-start | bytes 12582912 | tf_op jit(solution)/shard_map/psum | solution.py:251
  454.4 10.6 %copy-start.42 = (bf16[4096,512]{1,0:T(8,128)(2,1)S(1)}, bf16[4096,512]{1,0:T(8,128)(2,1)}, u32[]{:S(2)}) copy-start(bf16[4096,512]{1,0:T(8,128)(2,1)} %all-gather.3.cloned.1.call-done) | copy-start | bytes 12582916
  454.4 22.2 %slice-start = ((s8[6291456]{0:T(1024)(128)(4,1)}), s8[4194304]{0:T(1024)(128)(4,1)S(1)}, s32[]{:S(2)}) async-start(s8[6291456]{0:T(1024)(128)(4,1)} %bitcast.144), calls=%async_computation.11 | async-start | bytes 8388608
  465.0 9.5 %copy-start.11 = (bf16[32,8,8,512]{3,1,2,0:T(8,128)(2,1)S(1)}, bf16[32,8,8,512]{3,1,2,0:T(8,128)(2,1)}, u32[]{:S(2)}) copy-start(bf16[32,8,8,512]{3,1,2,0:T(8,128)(2,1)} %copy-done.10) | copy-start | bytes 6291460
  465.0 9.5 %copy-start.43 = (bf16[4096,512]{1,0:T(8,128)(2,1)S(1)}, bf16[4096,512]{1,0:T(8,128)(2,1)}, u32[]{:S(2)}) copy-start(bf16[4096,512]{1,0:T(8,128)(2,1)} %all-gather.5.cloned.1.call-done) | copy-start | bytes 12582916
  465.0 11.6 %slice-start.1 = ((s8[6291456]{0:T(1024)(128)(4,1)}), s8[2097152]{0:T(1024)(128)(4,1)S(1)}, s32[]{:S(2)}) async-start(s8[6291456]{0:T(1024)(128)(4,1)} %bitcast.144), calls=%async_computation.12 | async-start | bytes 4194304
  526.8 8.6 %copy-start.7 = (f32[2048,512]{1,0:T(8,128)S(1)}, f32[2048,512]{1,0:T(8,128)}, u32[]{:S(2)}) copy-start(f32[2048,512]{1,0:T(8,128)} %reduce-scatter.11.cloned.1.call-done) | copy-start | bytes 12582916
  530.8 4.6 copy-start.6
  696.3 4.7 copy-start.16
  696.3 6.0 copy-start.15
  (27 other events, 47.1 us)
Sparse Core Ops, SparseCore 0:
  143.3 19.4 reduce-scatter.4
  172.0 14.9 all-gather.2
  248.2 17.9 reduce-scatter.8
  272.1 13.1 reduce-scatter.6
  295.3 14.9 all-gather.4
  454.5 17.9 reduce-scatter.10
  481.5 214.7 all-reduce.3
where the time goes:
time: 715 us; the launch traced here: 711 us
  matrix products  222 us (31%)
  waiting for transfers between devices  175 us (24%)
  local copies, waits for them, and re-layouts  108 us (15%)
  other arithmetic  94.5 us (13%)
  blocking collectives  82.6 us (12%)
  between operations  14.9 us (2%)
  loops' own time  13.6 us (2%)
    psum x1, waiting for transfers between devices, body(): lax.psum((local_grads[0], local_grads[1], local_grads[2], local_grads[3],...  118 us
    psum x1, blocking collectives, body(): lax.psum((local_grads[0], local_grads[1], local_grads[2], local_grads[3],...  44.8 us
    dot_general x1, matrix products, run_layer(): jnp.einsum('rd,fd->rf', cot_in, down_weight, preferred_element_type=jnp.f...  44.3 us
    psum x1, blocking collectives, body(): lax.psum((shared[0], shared[1], shared[2], shared[3], shared[4], shared[5...  37.9 us
    all_gather x2, waiting for transfers between devices, body(): lax.all_gather(values, 'tensor', axis=0, tiled=True)  30.1 us
    dot_general x16, matrix products, masked_scores(): jnp.einsum('qhd,khd->hqk', q_rows, k_rows, preferred_element_type=jnp.flo...  30.1 us
    reduce_scatter x4, waiting for transfers between devices, body(): lax.psum_scatter(term_fn(jnp.int32(0), own_count * lax.axis_size('tensor'...  27.2 us
    dot_general x8, matrix products, one_scene(): jnp.einsum('hqk,khd->qhd', prob_low, v_rows, preferred_element_type=jnp.f...  23 us
  transfers between devices with their start and end apart: 7, of which 5 were waited for; matrix products, arithmetic and copies ran while one was open for 9% of the time, Pallas kernels for 0%

commit v1 on v0

v1 whole, which is shorter than its diff:
```python
import jax
import jax.numpy as jnp
from jax import lax
from jax.experimental import pallas as pl
from jax.experimental.pallas import tpu as pltpu
from jax.sharding import PartitionSpec as P

D = 512
HD = 64
LAT = 512
AUG = 16
EPS = 1e-05
NEG = -1e30
BF = jnp.bfloat16
F32 = jnp.float32
VMEM_LIMIT = 58 * 2**20
SWAP = [(0, 1), (1, 0)]


def _dot(a, b, ca, cb):
    return lax.dot_general(a, b, (((ca,), (cb,)), ((), ())), preferred_element_type=F32)


def nn(a, b):
    return _dot(a, b, 1, 0)


def nt(a, b):
    return _dot(a, b, 1, 1)


def tn(a, b):
    return _dot(a, b, 0, 0)


def normalised(v):
    c = v - jnp.mean(v, -1, keepdims=True)
    r = lax.rsqrt(jnp.mean(c * c, -1, keepdims=True) + EPS)
    return c * r, r


def norm_back(e, xh, r):
    return r * (e - jnp.mean(e, -1, keepdims=True) - xh * jnp.mean(e * xh, -1, keepdims=True))


def forward_kernel(
    tens, lens, x_ref, vecs, wq_own, wq_oth, wo_own, wo_oth,
    n1_ref, qkv_ref, p_ref, att_ref, rl_ref, h1_ref, n2_ref,
):
    scenes = pl.num_programs(0)
    length = lens[tens[0] * scenes + pl.program_id(0)]
    x = x_ref[...].astype(F32)
    n1 = (normalised(x)[0] * vecs[0:1] + vecs[1:2]).astype(BF)
    n1_ref[...] = n1
    half = wo_own.shape[0]
    for side, w in enumerate((wq_own, wq_oth)):
        for t in range(3):
            part = nt(w[t * half:(t + 1) * half], n1)
            if t == 0:
                part = part * HD**-0.5
            qkv_ref[0, side, t] = part.astype(BF)
    heads = wo_own.shape[0] // HD
    key_at = lax.broadcasted_iota(jnp.int32, (AUG, LAT), 1)
    row_at = lax.broadcasted_iota(jnp.int32, (AUG, LAT), 0)
    bias = jnp.where((key_at >= length) & (row_at == 0), NEG, 0.0).astype(BF)
    ones = jnp.ones((AUG, LAT), BF)
    for side in range(2):
        for h in range(heads):
            at = pl.ds(h * HD, HD)
            ka = jnp.concatenate([qkv_ref[0, side, 1, at], bias], 0)
            qa = jnp.concatenate([qkv_ref[0, side, 0, at], ones], 0)
            va = jnp.concatenate([qkv_ref[0, side, 2, at], ones], 0)
            hh = side * heads + h
            for qb in range(2):
                cols = slice(qb * 256, qb * 256 + 256)
                s = tn(ka, qa[:, cols])
                p = jnp.exp(s - jnp.max(s, 0, keepdims=True)).astype(BF)
                p_ref[0, hh, :, cols] = p
                o = nn(va, p)
                rl = 1.0 / o[HD:HD + 1]
                rl_ref[0, hh:hh + 1, cols] = rl
                att_ref[0, hh * HD:hh * HD + HD, cols] = (o[:HD] * rl).astype(BF)
    h1 = x + (tn(att_ref[0, :half], wo_own[...]) + tn(att_ref[0, half:], wo_oth[...])) + vecs[2:3]
    h1_ref[...] = h1
    n2_ref[...] = (normalised(h1)[0] * vecs[3:4] + vecs[4:5]).astype(BF)


def whole(shape, row=0):
    at = (row,) + (0,) * (len(shape) - 1)
    return pl.BlockSpec(shape, lambda i, *_: at, pipeline_mode=pl.Buffered(1))


def params():
    return pltpu.CompilerParams(vmem_limit_bytes=VMEM_LIMIT, dimension_semantics=("arbitrary",))


def vecs_spec():
    return whole((6, D))


def attention_forward(tens, lens, x, vecs, wq_own, theirs, wo_own, rows):
    scenes = rows // LAT
    rowblock = pl.BlockSpec((LAT, D), lambda i, *_: (i, 0))
    half = wo_own.shape[0]
    return pl.pallas_call(
        forward_kernel,
        grid_spec=pltpu.PrefetchScalarGridSpec(
            num_scalar_prefetch=2,
            grid=(scenes,),
            in_specs=[
                pl.BlockSpec((LAT, D), lambda i, tens, lens: (tens[0] * scenes + i, 0)),
                vecs_spec(), whole((3 * half, D)), whole((3 * half, D)), whole((half, D)), whole((half, D), 3),
            ],
            out_specs=[
                rowblock,
                pl.BlockSpec((1, 2, 3, half, LAT), lambda i, *_: (i, 0, 0, 0, 0)),
                pl.BlockSpec((1, 2 * half // HD, LAT, LAT), lambda i, *_: (i, 0, 0, 0)),
                pl.BlockSpec((1, D, LAT), lambda i, *_: (i, 0, 0)),
                pl.BlockSpec((1, 2 * half // HD, LAT), lambda i, *_: (i, 0, 0)),
                rowblock,
                rowblock,
            ],
        ),
        out_shape=[
            jax.ShapeDtypeStruct((rows, D), BF),
            jax.ShapeDtypeStruct((scenes, 2, 3, half, LAT), BF),
            jax.ShapeDtypeStruct((scenes, 2 * half // HD, LAT, LAT), BF),
            jax.ShapeDtypeStruct((scenes, D, LAT), BF),
            jax.ShapeDtypeStruct((scenes, 2 * half // HD, LAT), F32),
            jax.ShapeDtypeStruct((rows, D), F32),
            jax.ShapeDtypeStruct((rows, D), BF),
        ],
        compiler_params=params(),
        name="attention_forward",
    )(tens, lens, x, vecs, wq_own, theirs, wo_own, theirs)


ERF_P = 0.3275911 / 2**0.5
ERF_A = tuple(0.5 * a for a in (0.254829592, -0.284496736, 1.421413741, -1.453152027, 1.061405429))
LOG2E = 1.4426950408889634


def gelu_parts(z):
    t = 1.0 / (1.0 + ERF_P * jnp.abs(z))
    density = jnp.exp2(z * z * (-0.5 * LOG2E))
    poly = t * (ERF_A[0] + t * (ERF_A[1] + t * (ERF_A[2] + t * (ERF_A[3] + t * ERF_A[4]))))
    tail = poly * density
    cdf = jnp.where(z >= 0, 1.0 - tail, tail)
    return z * cdf, cdf + z * (density * 0.3989422804014327)


SUB = 256


def mlp_step(n2, cot, up, ub, down, acc_up, acc_down, acc_ub):
    out, back = 0.0, 0.0
    first = pl.program_id(0) == 0

    @pl.when(first)
    def _():
        acc_up[...] = jnp.zeros_like(acc_up)
        acc_down[...] = jnp.zeros_like(acc_down)
        acc_ub[...] = jnp.zeros_like(acc_ub)

    for j in range(up.shape[0] // SUB):
        at = slice(j * SUB, j * SUB + SUB)
        u, d = up[at], down[at]
        pre = nt(n2, u) + ub[:, at].astype(F32)
        act, slope = gelu_parts(pre)
        act = act.astype(BF)
        dpre = (nt(cot, d) * slope).astype(BF)
        out += nn(act, d)
        back += nn(dpre, u)
        acc_down[at] += tn(act, cot)
        acc_up[at] += tn(dpre, n2)
        acc_ub[:, at] += jnp.sum(dpre.astype(F32), 0, keepdims=True)
    return out, back


def mlp_first_kernel(
    tens, n2_ref, cot_ref, up, ub, down, h1_ref, vecs,
    out_ref, back_ref, grads_ref, acc_up, acc_down, acc_ub,
):
    out, back = mlp_step(n2_ref[...], cot_ref[...], up, ub, down, acc_up, acc_down, acc_ub)
    out_ref[...] = out + h1_ref[...] + vecs[5:6]
    back_ref[...] = back

    @pl.when(pl.program_id(0) == pl.num_programs(0) - 1)
    def _():
        units = acc_up.shape[0]
        put_slabs(grads_ref, 0, acc_up)
        put_slabs(grads_ref, 4 * units, acc_down)
        put_row(grads_ref, 8 * units, acc_ub, 16)


def put_slabs(out, at, values):
    n = values.shape[0]
    for c in range(D // 128):
        out[at + c * n:at + (c + 1) * n] = values[:, c * 128:c * 128 + 128].astype(out.dtype)


def put_row(out, at, row, count):
    parts = [row[:, c * 128:c * 128 + 128] for c in range(row.shape[1] // 128)]
    parts += [jnp.zeros((1, 128), F32)] * (count - len(parts))
    out[at:at + count] = jnp.concatenate(parts, 0).astype(out.dtype)


def mlp_second_kernel(
    tens, n2_ref, cot_ref, up, ub, down, h1_ref, out_in, back_in, vecs, att_ref, rl_ref, wo_own, wo_oth,
    block_ref, gh_ref, doa_ref, grads_ref, wo_oth_ref, cols_ref, acc_up, acc_down, acc_ub, acc_wo,
):
    cot = cot_ref[...]
    out, back = mlp_step(n2_ref[...], cot, up, ub, down, acc_up, acc_down, acc_ub)
    block_ref[...] = (out + out_in[...]).astype(BF)
    g = back + back_in[...]
    xh, r = normalised(h1_ref[...])
    cot32 = cot.astype(F32)
    gh = cot32 + norm_back(g * vecs[3:4], xh, r)
    gh_ref[...] = gh
    gb = gh.astype(BF)
    half = wo_own.shape[0]
    heads = half // HD
    zeros = jnp.zeros((AUG - 3, LAT), F32)
    for side, w in enumerate((wo_own, wo_oth)):
        do = nt(w[...], gb)
        for h in range(heads):
            hh = side * heads + h
            scaled = (do[h * HD:h * HD + HD] * rl_ref[0, hh:hh + 1]).astype(BF)
            doa_ref[0, hh, :HD] = scaled
            delta = -jnp.sum(scaled.astype(F32) * att_ref[0, hh * HD:hh * HD + HD].astype(F32), 0, keepdims=True)
            high = delta.astype(BF).astype(F32)
            low = (delta - high).astype(BF).astype(F32)
            doa_ref[0, hh, HD:] = jnp.concatenate([high, low, delta - high - low, zeros], 0).astype(BF)
    wo_term = nn(att_ref[0], gb)
    sums = jnp.concatenate(
        [jnp.sum(v, 0, keepdims=True) for v in (g * xh, g, gh, cot32)] + [jnp.zeros((4, D), F32)], 0
    )

    @pl.when(pl.program_id(0) == 0)
    def _():
        acc_wo[...] = wo_term
        cols_ref[...] = sums

    @pl.when(pl.program_id(0) > 0)
    def _():
        acc_wo[...] += wo_term
        cols_ref[...] += sums

    @pl.when(pl.program_id(0) == pl.num_programs(0) - 1)
    def _():
        units = acc_up.shape[0]
        put_slabs(grads_ref, 0, acc_up)
        put_slabs(grads_ref, 4 * units, acc_down)
        put_slabs(grads_ref, 8 * units, acc_wo.at[:half])
        put_slabs(wo_oth_ref, 0, acc_wo.at[half:])
        base = 8 * units + 4 * half
        put_row(grads_ref, base, acc_ub, 8)
        grads_ref[base + 8:] = jnp.zeros((grads_ref.shape[0] - base - 8, 128), F32)


def mlp_first(tens, n2, cot, theirs, ub, h1, vecs):
    rows = n2.shape[0]
    scenes = rows // LAT
    units = ub.shape[1]
    rowblock = pl.BlockSpec((LAT, D), lambda i, *_: (i, 0))
    cotblock = pl.BlockSpec((LAT, D), lambda i, tens: (tens[0] * scenes + i, 0))
    return pl.pallas_call(
        mlp_first_kernel,
        grid_spec=pltpu.PrefetchScalarGridSpec(
            num_scalar_prefetch=1,
            grid=(scenes,),
            in_specs=[
                rowblock, cotblock, whole((units, D)), whole((1, units)), whole((units, D), 1), rowblock, vecs_spec(),
            ],
            out_specs=[rowblock, rowblock, whole((8 * units + 16, 128))],
            scratch_shapes=[pltpu.VMEM((units, D), F32), pltpu.VMEM((units, D), F32), pltpu.VMEM((1, units), F32)],
        ),
        out_shape=[
            jax.ShapeDtypeStruct((rows, D), F32),
            jax.ShapeDtypeStruct((rows, D), F32),
            jax.ShapeDtypeStruct((8 * units + 16, 128), BF),
        ],
        compiler_params=params(),
        name="mlp_first",
    )(tens, n2, cot, theirs, ub, theirs, h1, vecs)


def mlp_second(tens, n2, cot, up, ub, down, h1, out_in, back_in, vecs, att, rl, wo_own, theirs, total_rows):
    rows = n2.shape[0]
    scenes = rows // LAT
    units = up.shape[0]
    half = wo_own.shape[0]
    heads = 2 * half // HD
    rowblock = pl.BlockSpec((LAT, D), lambda i, *_: (i, 0))
    cotblock = pl.BlockSpec((LAT, D), lambda i, tens: (tens[0] * scenes + i, 0))
    return pl.pallas_call(
        mlp_second_kernel,
        grid_spec=pltpu.PrefetchScalarGridSpec(
            num_scalar_prefetch=1,
            grid=(scenes,),
            in_specs=[
                rowblock, cotblock, whole((units, D)), whole((1, units)), whole((units, D)), rowblock, rowblock, rowblock,
                vecs_spec(),
                pl.BlockSpec((1, D, LAT), lambda i, *_: (i, 0, 0)),
                pl.BlockSpec((1, heads, LAT), lambda i, *_: (i, 0, 0)),
                whole((half, D)), whole((half, D), 3),
            ],
            out_specs=[
                rowblock, rowblock,
                pl.BlockSpec((1, heads, HD + AUG, LAT), lambda i, *_: (i, 0, 0, 0)),
                whole((total_rows, 128)), whole((4 * half, 128)), whole((8, D)),
            ],
            scratch_shapes=[
                pltpu.VMEM((units, D), F32), pltpu.VMEM((units, D), F32), pltpu.VMEM((1, units), F32),
                pltpu.VMEM((2 * half, D), F32),
            ],
        ),
        out_shape=[
            jax.ShapeDtypeStruct((rows, D), BF),
            jax.ShapeDtypeStruct((rows, D), F32),
            jax.ShapeDtypeStruct((scenes, heads, HD + AUG, LAT), BF),
            jax.ShapeDtypeStruct((total_rows, 128), F32),
            jax.ShapeDtypeStruct((4 * half, 128), BF),
            jax.ShapeDtypeStruct((8, D), F32),
        ],
        compiler_params=params(),
        name="mlp_second",
    )(tens, n2, cot, up, ub, down, h1, out_in, back_in, vecs, att, rl, wo_own, theirs)


def back_head_kernel(tens, p_ref, doa_ref, qkv_ref, n1_ref, *refs):
    dqkv_ref, dw_ref, dw_acc = refs[-3:]
    ones = jnp.ones((AUG, LAT), BF)
    q, k = qkv_ref[0, 0, 0], qkv_ref[0, 0, 1]
    va = jnp.concatenate([qkv_ref[0, 0, 2], ones], 0)
    doa = doa_ref[0, 0]
    p = p_ref[0, 0]
    ds = (p.astype(F32) * tn(va, doa)).astype(BF)
    dqkv_ref[0, 0, 0] = (nn(k, ds) * HD**-0.5).astype(BF)
    dqkv_ref[0, 0, 1] = nt(q, ds).astype(BF)
    dqkv_ref[0, 0, 2] = nt(doa[:HD], p).astype(BF)
    term = nn(dqkv_ref[...].reshape(3 * HD, LAT), n1_ref[...])

    @pl.when(pl.program_id(0) == 0)
    def _():
        dw_acc[...] = term

    @pl.when(pl.program_id(0) > 0)
    def _():
        dw_acc[...] += term

    @pl.when(pl.program_id(0) == pl.num_programs(0) - 1)
    def _():
        put_slabs(dw_ref.at[0], 0, dw_acc)


def back_head(tens, p, doa, qkv, n1, dqkv, dw, side, h):
    scenes, heads = p.shape[0], p.shape[1] // 2
    hh = side * heads + h
    head_at = lambda i, *_: (i, side, 0, h, 0)
    carried = [v for v in (dqkv, dw) if v is not None]
    places = [j for j, v in enumerate((dqkv, dw)) if v is not None]
    return pl.pallas_call(
        back_head_kernel,
        grid_spec=pltpu.PrefetchScalarGridSpec(
            num_scalar_prefetch=1,
            grid=(scenes,),
            in_specs=[
                pl.BlockSpec((1, 1, LAT, LAT), lambda i, *_: (i, hh, 0, 0)),
                pl.BlockSpec((1, 1, HD + AUG, LAT), lambda i, *_: (i, hh, 0, 0)),
                pl.BlockSpec((1, 1, 3, HD, LAT), head_at),
                pl.BlockSpec((LAT, D), lambda i, *_: (i, 0)),
            ] + [pl.BlockSpec(memory_space=pl.ANY)] * len(carried),
            out_specs=[
                pl.BlockSpec((1, 1, 3, HD, LAT), head_at),
                pl.BlockSpec((1, 12 * HD, 128), lambda i, *_: (h, 0, 0)),
            ],
            scratch_shapes=[pltpu.VMEM((3 * HD, D), F32)],
        ),
        out_shape=[
            jax.ShapeDtypeStruct(qkv.shape, BF),
            jax.ShapeDtypeStruct((heads, 12 * HD, 128), BF if side else F32),
        ],
        input_output_aliases={5 + n: j for n, j in enumerate(places)},
        compiler_params=params(),
        name="attention_back",
    )(tens, p, doa, qkv, n1, *carried)


def norm_one_back_kernel(tens, dqkv, wq_own, wq_oth, x_ref, vecs, gh_ref, gl_ref, cols_ref):
    feats = wq_own.shape[0]
    g = tn(dqkv[0, 0].reshape(feats, LAT), wq_own[...]) + tn(dqkv[0, 1].reshape(feats, LAT), wq_oth[...])
    xh, r = normalised(x_ref[...].astype(F32))
    gl_ref[...] = gh_ref[...] + norm_back(g * vecs[0:1], xh, r)
    sums = jnp.concatenate([jnp.sum(v, 0, keepdims=True) for v in (g * xh, g)] + [jnp.zeros((6, D), F32)], 0)

    @pl.when(pl.program_id(0) == 0)
    def _():
        cols_ref[...] = sums

    @pl.when(pl.program_id(0) > 0)
    def _():
        cols_ref[...] += sums


def norm_one_back(tens, dqkv, wq_own, theirs, x, vecs, gh):
    scenes, half = dqkv.shape[0], dqkv.shape[3]
    rowblock = pl.BlockSpec((LAT, D), lambda i, *_: (i, 0))
    return pl.pallas_call(
        norm_one_back_kernel,
        grid_spec=pltpu.PrefetchScalarGridSpec(
            num_scalar_prefetch=1,
            grid=(scenes,),
            in_specs=[
                pl.BlockSpec((1, 2, 3, half, LAT), lambda i, *_: (i, 0, 0, 0, 0)),
                whole((3 * half, D)), whole((3 * half, D)),
                pl.BlockSpec((LAT, D), lambda i, tens: (tens[0] * scenes + i, 0)),
                vecs_spec(),
                rowblock,
            ],
            out_specs=[rowblock, whole((8, D))],
        ),
        out_shape=[jax.ShapeDtypeStruct((scenes * LAT, D), F32), jax.ShapeDtypeStruct((8, D), F32)],
        compiler_params=params(),
        name="norm_one_back",
    )(tens, dqkv, wq_own, theirs, x, vecs, gh)


def tie(value, *after):
    return lax.optimization_barrier((value, *after))[0]


def swap(v):
    return lax.ppermute(v, "tensor", SWAP)


class Cube:
    def __init__(self):
        self.count = lax.axis_size("dp")
        self.steps = self.count.bit_length() - 1
        assert 1 << self.steps == self.count
        first = list(range(self.steps))
        second = [b ^ 1 if b ^ 1 < self.steps else b for b in first]
        self.order = (first, second)
        self.at = lax.axis_index("dp")
        self.core = lax.axis_index("tensor")

    def bit(self, s):
        which = jnp.where(self.core == 0, self.order[0][s], self.order[1][s])
        return (jnp.right_shift(self.at, which) & 1).astype(jnp.int32)

    def exchange(self, v, s):
        pairs = []
        for i in range(self.count):
            for t in range(2):
                pairs.append((i * 2 + t, (i ^ (1 << self.order[t][s])) * 2 + t))
        return lax.ppermute(v, ("dp", "tensor"), pairs)


def small_call(kernel, out_shape, name, scalars, *arrays, scratch=()):
    return pl.pallas_call(
        kernel,
        in_specs=[pl.BlockSpec(memory_space=pltpu.SMEM)] + [pl.BlockSpec(memory_space=pltpu.VMEM)] * len(arrays),
        out_specs=[pl.BlockSpec(memory_space=pltpu.VMEM)] * len(out_shape),
        out_shape=out_shape,
        scratch_shapes=list(scratch),
        compiler_params=pltpu.CompilerParams(vmem_limit_bytes=VMEM_LIMIT),
        name=name,
    )(scalars, *arrays)


def halves(bit, m):
    return pl.ds(pl.multiple_of(bit * m, 16), m), pl.ds(pl.multiple_of((1 - bit) * m, 16), m)


def split_kernel(bits, keep, recv, keep_out, send_out):
    m = keep_out.shape[0]
    mine, other = halves(bits[0], m)
    send_out[...] = (keep[other] + recv[other].astype(F32)).astype(BF)
    keep_out[...] = keep[mine] + recv[mine].astype(F32)


def split(keep, recv, bits):
    m = keep.shape[0] // 2
    return small_call(
        split_kernel, [jax.ShapeDtypeStruct((m, 128), F32), jax.ShapeDtypeStruct((m, 128), BF)], "split", bits, keep, recv
    )


def settle_kernel(bits, keep, recv, out):
    out[...] = (keep[...] + recv[...].astype(F32)).astype(BF)


def settle(keep, recv, bits):
    return small_call(settle_kernel, [jax.ShapeDtypeStruct(keep.shape, BF)], "settle", bits, keep, recv)[0]


def join_kernel(bits, own, recv, out):
    mine, other = halves(bits[0], own.shape[0])
    out[mine] = own[...]
    out[other] = recv[...]


def join(own, recv, bits):
    return small_call(
        join_kernel, [jax.ShapeDtypeStruct((2 * own.shape[0], 128), BF)], "join", bits, own, recv
    )[0]


def split_mlp_kernel(bits, own, recv, recv_wo, keep_out, send_out, full):
    big, wo = recv.shape[0] - 16, recv_wo.shape[0]
    ub = big // 1024
    full[...] = own[...]
    full[:big] += recv[:big].astype(F32)
    full[big:big + wo] += recv_wo[...].astype(F32)
    full[big + wo:big + wo + ub] += recv[big:big + ub].astype(F32)
    m = keep_out.shape[0]
    mine, other = halves(bits[0], m)
    send_out[...] = full[other].astype(BF)
    keep_out[...] = full[mine]


def split_mlp(own, recv, recv_wo, bits):
    m = own.shape[0] // 2
    return small_call(
        split_mlp_kernel, [jax.ShapeDtypeStruct((m, 128), F32), jax.ShapeDtypeStruct((m, 128), BF)], "split_mlp",
        bits, own, recv, recv_wo, scratch=[pltpu.VMEM(own.shape, F32)],
    )


def finish_mlp_kernel(bits, own, recv, dup, ddown, dwo, dub, full):
    mine, other = halves(bits[0], own.shape[0])
    full[mine] = own[...]
    full[other] = recv[...]
    units, half = dup.shape[0], dwo.shape[0]
    for c in range(D // 128):
        at = slice(c * 128, c * 128 + 128)
        dup[:, at] = full[c * units:(c + 1) * units].astype(F32)
        ddown[:, at] = full[(4 + c) * units:(5 + c) * units].astype(F32)
        dwo[:, at] = full[8 * units + c * half:8 * units + (c + 1) * half].astype(F32)
    base = 8 * units + 4 * half
    dub[...] = full[base:base + dub.shape[0]].astype(F32)


def finish_mlp(own, recv, bits, units, half):
    return small_call(
        finish_mlp_kernel,
        [
            jax.ShapeDtypeStruct((units, D), F32), jax.ShapeDtypeStruct((units, D), F32),
            jax.ShapeDtypeStruct((half, D), F32), jax.ShapeDtypeStruct((units // 128, 128), F32),
        ],
        "finish_mlp", bits, own, recv, scratch=[pltpu.VMEM((2 * own.shape[0], 128), BF)],
    )


def finish_qkv_kernel(bits, own, recv, out, full):
    mine, other = halves(bits[0], own.shape[0])
    full[mine] = own[...]
    full[other] = recv[...]
    for h in range(out.shape[1] // HD):
        for c in range(D // 128):
            for t in range(3):
                row = h * 12 * HD + c * 3 * HD + t * HD
                out[t, h * HD:h * HD + HD, c * 128:c * 128 + 128] = full[row:row + HD].astype(F32)


def finish_qkv(own, recv, bits, half):
    return small_call(
        finish_qkv_kernel, [jax.ShapeDtypeStruct((3, half, D), F32)], "finish_qkv", bits, own, recv,
        scratch=[pltpu.VMEM((2 * own.shape[0], 128), BF)],
    )[0]


def body(
    latents, scene_len, attn_gain, attn_shift, qkv_weight, out_weight, out_bias, mlp_gain, mlp_shift,
    up_weight, up_bias, down_weight, down_bias, cotangent,
):
    rows = latents.shape[0] // lax.axis_size("tensor")
    units, half = up_weight.shape[0], out_weight.shape[0]
    heads = half // HD
    tens = lax.axis_index("tensor").astype(jnp.int32).reshape(1)
    cube = Cube()
    bits = [cube.bit(s).reshape(1) for s in range(cube.steps)]

    ours = jnp.concatenate([qkv_weight.reshape(3 * half, D), out_weight], 0)
    theirs = swap(ours)
    wq_oth, wo_oth = theirs, theirs
    vecs = jnp.stack([attn_gain, attn_shift, out_bias, mlp_gain, mlp_shift, down_bias]).astype(F32)
    ours_mlp = jnp.concatenate([up_weight, down_weight, jnp.pad(up_bias.reshape(units // D, D), ((0, 16 - units // D), (0, 0)))], 0)
    theirs_mlp = swap(ours_mlp)

    n1, qkv, p, att, rl, h1, n2 = attention_forward(
        tens, scene_len, latents, vecs, qkv_weight.reshape(3 * half, D), theirs, out_weight, rows
    )
    ub_oth = theirs_mlp[2 * units:2 * units + units // D].reshape(1, units)
    out_part, back_part, grads_oth = mlp_first(tens, n2, cotangent, theirs_mlp, ub_oth, h1, vecs)
    from_peer = swap(grads_oth)
    count = cube.count
    need = 8 * units + 4 * half + units // 128
    total_rows = -(-need // (16 * count)) * 16 * count
    block_out, gh, doa, grads_own, wo_oth_grad, cols_two = mlp_second(
        tens, n2, cotangent, up_weight, up_bias.reshape(1, units), down_weight, h1, out_part, back_part, vecs, att, rl,
        out_weight, theirs, total_rows,
    )
    keep, send = split_mlp(grads_own, from_peer, swap(wo_oth_grad), bits[0])

    queue = []
    state = {"keep": keep, "send": send, "recv": None}

    def reduce_steps(keep, send):
        for s in range(cube.steps):
            recv = cube.exchange(send, s)
            token = yield send
            recv = tie(recv, token)
            if s + 1 < cube.steps:
                keep, send = split(keep, recv, bits[s + 1])
            else:
                have = settle(keep, recv, bits[s])
        for s in range(cube.steps - 1, -1, -1):
            recv = cube.exchange(have, s)
            token = yield have
            recv = tie(recv, token)
            if s:
                have = join(have, recv, bits[s])
        return have, recv

    def advance(steps, token):
        try:
            return steps.send(token), None
        except StopIteration as end:
            return None, end.value

    mlp_steps = reduce_steps(keep, send)
    token = next(mlp_steps)
    mlp_result = None
    dqkv, dw_oth, dw_own = None, None, None
    calls = 0
    for side in (1, 0):
        for h in range(heads):
            dw = dw_oth if side else dw_own
            dqkv, dw = back_head(tie(tens, token), p, doa, qkv, n1, dqkv, dw, side, h)
            if side:
                dw_oth = dw
            else:
                dw_own = dw
            calls += 1
            if mlp_result is None and calls != 1:
                token, mlp_result = advance(mlp_steps, dw)
                if mlp_result is not None:
                    token = dw
            else:
                token = dw
        if side:
            qkv_peer = swap(dw_oth.reshape(heads * 12 * HD, 128))
    keep, send = split(tie(dw_own.reshape(heads * 12 * HD, 128), token), qkv_peer, bits[0])
    qkv_steps = reduce_steps(keep, send)
    token = next(qkv_steps)
    grad_latents, cols_one = norm_one_back(tie(tens, token), dqkv, qkv_weight.reshape(3 * half, D), theirs, latents, vecs, gh)
    cols = jnp.concatenate([cols_one[:2], cols_two[:4]], 0).reshape(24, 128)
    qkv_result = None
    token = cols
    todo = [lambda v: swap(v)] + [lambda v, s=s: cube.exchange(v, s) for s in range(cube.steps)]
    while qkv_result is None:
        _, qkv_result = advance(qkv_steps, token)
        if todo:
            cols = cols + todo.pop(0)(cols)
            token = cols
        if mlp_result is None:
            token, mlp_result = advance(mlp_steps, token)
            token = cols
    while todo:
        cols = cols + todo.pop(0)(cols)
    while mlp_result is None:
        _, mlp_result = advance(mlp_steps, cols)
    dup, ddown, dwo, dub = finish_mlp(*mlp_result, bits[0], units, half)
    dwq = finish_qkv(*qkv_result, bits[0], half)
    shared = cols.reshape(6, D)
    return (
        block_out, grad_latents, shared[0], shared[1], dwq, dwo, shared[4],
        shared[2], shared[3], dup, dub.reshape(units), ddown, shared[5],
    )


def solution(mesh):
    placed = (
        P("dp", None), P("dp"), P(), P(), P(None, "tensor", None), P("tensor", None), P(), P(), P(),
        P("tensor", None), P("tensor"), P("tensor", None), P(), P("dp", None),
    )
    return jax.shard_map(
        body,
        mesh=mesh,
        in_specs=placed,
        out_specs=(
            P(("dp", "tensor"), None), P(("dp", "tensor"), None), P(), P(), P(None, "tensor", None),
            P("tensor", None), P(), P(), P(), P("tensor", None), P("tensor"), P("tensor", None), P(),
        ),
        check_vma=False,
    )
```

time: 715 us -> 300 us (0.42)
  matrix products: 222 us -> 0 us
  Pallas kernels: 0 us -> 204 us
  waiting for transfers between devices: 175 us -> 32.7 us
  other arithmetic: 94.5 us -> 4.8 us
  local copies, waits for them, and re-layouts: 108 us -> 19.2 us
  blocking collectives: 82.6 us -> 0 us
  starting transfers between devices: 0.29 us -> 37.5 us
  between operations: 14.9 us -> 0.92 us
  loops' own time: 13.6 us -> 0 us
    dot_general x68 -> x0, matrix products: 222 us -> none  [the longest x1 44.3 us: run_layer(): jnp.einsum('rd,fd->rf', cot_in, down_weight, preferred_element_type=jnp.f...]
    pallas_call x0 -> x30, Pallas kernels: none -> 204 us  [the longest x8 52.8 us: back_head(): pl.pallas_call(back_head_kernel, grid_spec=pltpu.PrefetchScalarGridSpec(n...]
    psum x1 -> x0, waiting for transfers between devices: 118 us -> none  [body(): lax.psum((local_grads[0], local_grads[1], local_grads[2], local_grads[3],...]
    psum x2 -> x0, blocking collectives: 82.6 us -> none  [the longest x1 44.8 us: body(): lax.psum((local_grads[0], local_grads[1], local_grads[2], local_grads[3],...]
    reduce_sum x17 -> x0, other arithmetic: 41.7 us -> none  [the longest x2 8.62 us: layer_norm(): return centred * lax.rsqrt(spread + EPS) * gain_row + shift_row]
    ppermute x0 -> x26, starting transfers between devices: none -> 37.5 us  [the longest x20 36.4 us: exchange(): return lax.ppermute(v, ('dp', 'tensor'), pairs)]
    ppermute x0 -> x26, waiting for transfers between devices: none -> 32.7 us  [the longest x20 26.2 us: exchange(): return lax.ppermute(v, ('dp', 'tensor'), pairs)]
    all_gather x2 -> x0, waiting for transfers between devices: 30.1 us -> none  [body(): lax.all_gather(values, 'tensor', axis=0, tiled=True)]
  transfers between devices with their start and end apart: 7 -> 26, of which waited for: 5 -> 16; matrix products, arithmetic and copies ran while one was open for 9% -> 1% of each run, Pallas kernels for 0% -> 52%
where the time goes in v1:
time: 300 us; the launch traced here: 299 us
  Pallas kernels  204 us (68%)
  starting transfers between devices  37.5 us (12%)
  waiting for transfers between devices  32.7 us (11%)
  local copies, waits for them, and re-layouts  19.2 us (6%)
  other arithmetic  4.8 us (2%)
    pallas_call x8, Pallas kernels, back_head(): pl.pallas_call(back_head_kernel, grid_spec=pltpu.PrefetchScalarGridSpec(n...  52.8 us
    pallas_call x18, Pallas kernels, small_call(): pl.pallas_call(kernel, in_specs=[pl.BlockSpec(memory_space=pltpu.SMEM)] +...  43 us
    pallas_call x1, Pallas kernels, attention_forward(): pl.pallas_call(forward_kernel, grid_spec=pltpu.PrefetchScalarGridSpec(num...  37.1 us
    ppermute x20, starting transfers between devices, exchange(): return lax.ppermute(v, ('dp', 'tensor'), pairs)  36.4 us
    pallas_call x1, Pallas kernels, mlp_second(): pl.pallas_call(mlp_second_kernel, grid_spec=pltpu.PrefetchScalarGridSpec(...  34.1 us
    pallas_call x1, Pallas kernels, mlp_first(): pl.pallas_call(mlp_first_kernel, grid_spec=pltpu.PrefetchScalarGridSpec(n...  26.6 us
    ppermute x20, waiting for transfers between devices, exchange(): return lax.ppermute(v, ('dp', 'tensor'), pairs)  26.2 us
    unnamed x68, local copies, waits for them, and re-layouts  16.4 us
  transfers between devices with their start and end apart: 26, of which 16 were waited for; matrix products, arithmetic and copies ran while one was open for 1% of the time, Pallas kernels for 52%

profile of v1, /device:TPU:0, one launch (start us, length us, event | category | flops | bytes accessed | tf_op | source)
XLA Modules:
  0.0 298.8 jit_solution(14364309610668839203)
XLA Ops:
  1.5 3.1 %fusion.1 = bf16[2064,512]{1,0:T(8,128)(2,1)} fusion(bf16[2,512]{1,0:T(2,128)(2,1)S(1)} %reshape.83, bf16[1024,512]{1,0:T(8,128)(2,1)} %down.1, bf16[1024,512]{1,0:T(8,128)(2,1)} %up.1), kind=kLoop, calls=%fused_computation.2 | loop fusion | flops 8454144 | bytes 4212736 | tf_op jit(solution)/shard_map/concatenate | solution.py:589
  6.9 3.7 %collective-permute-done.wq_oth.wo_oth = bf16[1024,512]{1,0:T(8,128)(2,1)S(1)} collective-permute-done((bf16[1024,512]{1,0:T(8,128)(2,1)}, bf16[1024,512]{1,0:T(8,128)(2,1)S(1)}, u32[]{:S(2)}, u32[]{:S(2)}) %collective-permute-start) | collective-permute-done | bytes 1048608 | tf_op jit(solution)/shard_map/ppermute | solution.py:434
  11.6 37.1 %attention_forward.1 = (bf16[2048,512]{1,0:T(8,128)(2,1)}, bf16[4,2,3,256,512]{4,3,2,1,0:T(8,128)(2,1)}, bf16[4,8,512,512]{3,2,1,0:T(8,128)(2,1)}, bf16[4,512,51...) custom-call(s32[1]{0:T(128)} %bitcast.tens, s32[8]{0:T(128)} %lens.1, ...), custom_call_target="tpu_custom_call" | custom-call | tf_op jit(solution)/shard_map/attention_forward/pallas_call | solution.py:105
  50.0 26.6 %mlp_first.1 = (f32[2048,512]{1,0:T(8,128)}, f32[2048,512]{1,0:T(8,128)}, bf16[8208,128]{1,0:T(8,128)(2,1)}) custom-call(s32[1]{0:T(128)} %bitcast.tens, bf16[2048,512]{1,0:T(8,128)(2,1)} %get-tuple-element.93.n2_ref, bf16[4096,512]{1,0:T(8,128)(2,1)} %cot_ref.3, bf16[2064,512]{1,0:T(8,128)(2,1)} %copy-done.1, bf16[1,1024]{1,0:T(2,128)(2,1)} %bitcast.30, ...), custom_call_target="tpu_custom_call" | custom-call | tf_op jit(solution)/shard_map/mlp_first/pallas_call | solution.py:267
  77.6 34.1 %mlp_second.1 = (bf16[2048,512]{1,0:T(8,128)(2,1)}, f32[2048,512]{1,0:T(8,128)}, bf16[4,8,80,512]{3,2,1,0:T(8,128)(2,1)}, f32[9472,128]{1,0:T(8,128)}, bf16[1024,128]{1,0:T(8,128)(2,1)}, /*index=5*/f32[8,512]{1,0:T(8,128)}) custom-call(s32[1]{0:T(128)} %bitcast.tens, bf16[2048,512]{1,0:T(8,128)(2,1)} %get-tuple-element.93.n2_ref, bf16[4096,512]{1,0:T(8,128)(2,1)} %cot_ref.3, ...), custom_call_target="tpu_custom_call" | custom-call | tf_op jit(solution)/shard_map/mlp_second/pallas_call | solution.py:296
  114.9 6.0 %split_mlp.1 = (f32[4736,128]{1,0:T(8,128)}, bf16[4736,128]{1,0:T(8,128)(2,1)}) custom-call(s32[1]{0:T(128)} %bitcast.2.bits, f32[9472,128]{1,0:T(8,128)} %get-tuple-element.100.own, bf16[8208,128]{1,0:T(8,128)(2,1)} %copy-done.6, bf16[1024,128]{1,0:T(8,128)(2,1)} %copy-done.16), custom_call_target="tpu_custom_call" | custom-call | tf_op jit(solution)/shard_map/split_mlp/pallas_call | solution.py:461
  120.9 2.6 collective-permute-start.4
  123.6 6.5 %attention_back.8 = (bf16[4,2,3,256,512]{4,3,2,1,0:T(8,128)(2,1)}, bf16[4,768,128]{2,1,0:T(8,128)(2,1)}) custom-call(s32[1]{0:T(128)} %bitcast.tens, bf16[4,8,512,512]{3,2,1,0:T(8,128)(2,1)} %get-tuple-element.106.p_ref, bf16[4,8,80,512]{3,2,1,0:T(8,128)(2,1)} %get-tuple-element.107.doa_ref, bf16[4,2,3,256,512]{4,3,2,1,0:T(8,128)(2,1)} %get-tuple-element.108.qkv_ref, ...), custom_call_target="tpu_custom_call" | custom-call | tf_op jit(solution)/shard_map/attention_back/pallas_call | solution.py:363
  130.1 6.5 %attention_back.9 = (bf16[4,2,3,256,512]{4,3,2,1,0:T(8,128)(2,1)}, bf16[4,768,128]{2,1,0:T(8,128)(2,1)}) custom-call(s32[1]{0:T(128)} %bitcast.tens, bf16[4,8,512,512]{3,2,1,0:T(8,128)(2,1)} %get-tuple-element.106.p_ref, bf16[4,8,80,512]{3,2,1,0:T(8,128)(2,1)} %get-tuple-element.107.doa_ref, ...), custom_call_target="tpu_custom_call", output_to_operand_aliasing={{0}: (5, {}), {1}: (6, {})} | custom-call | tf_op jit(solution)/shard_map/attention_back/pallas_call | solution.py:363
  139.3 3.4 %split.7 = (f32[2368,128]{1,0:T(8,128)}, bf16[2368,128]{1,0:T(8,128)(2,1)}) custom-call(s32[1]{0:T(128)} %bitcast.5.bits, f32[4736,128]{1,0:T(8,128)} %get-tuple-element.103.keep, bf16[4736,128]{1,0:T(8,128)(2,1)} %copy-done.8), custom_call_target="tpu_custom_call" | custom-call | tf_op jit(solution)/shard_map/split/pallas_call | solution.py:461
  144.8 6.5 %attention_back.10 = (bf16[4,2,3,256,512]{4,3,2,1,0:T(8,128)(2,1)}, bf16[4,768,128]{2,1,0:T(8,128)(2,1)}) custom-call(s32[1]{0:T(128)} %bitcast.tens, bf16[4,8,512,512]{3,2,1,0:T(8,128)(2,1)} %get-tuple-element.106.p_ref, bf16[4,8,80,512]{3,2,1,0:T(8,128)(2,1)} %get-tuple-element.107.doa_ref, ...), custom_call_target="tpu_custom_call", output_to_operand_aliasing={{0}: (5, {}), {1}: (6, {})} | custom-call | tf_op jit(solution)/shard_map/attention_back/pallas_call | solution.py:363
  153.9 2.5 split.8
  158.4 6.5 %attention_back.11 = (bf16[4,2,3,256,512]{4,3,2,1,0:T(8,128)(2,1)}, bf16[4,768,128]{2,1,0:T(8,128)(2,1)}) custom-call(s32[1]{0:T(128)} %bitcast.tens, bf16[4,8,512,512]{3,2,1,0:T(8,128)(2,1)} %get-tuple-element.106.p_ref, bf16[4,8,80,512]{3,2,1,0:T(8,128)(2,1)} %get-tuple-element.107.doa_ref, ...), custom_call_target="tpu_custom_call", output_to_operand_aliasing={{0}: (5, {}), {1}: (6, {})} | custom-call | tf_op jit(solution)/shard_map/attention_back/pallas_call | solution.py:363
  167.7 3.8 %collective-permute-start.7 = (bf16[592,128]{1,0:T(8,128)(2,1)}, bf16[592,128]{1,0:T(8,128)(2,1)S(1)}, u32[]{:S(2)}, u32[]{:S(2)}) collective-permute-start(bf16[592,128]{1,0:T(8,128)(2,1)} %get-tuple-element.128), channel_id=1, source_target_pairs={{0,16},{1,9},{2,18},{3,11},{4,20},{5,13},{6,22},{7,15},{8,24},{9,1... | collective-permute-start | bytes 454664 | tf_op jit(solution)/shard_map/ppermute | solution.py:457
  171.5 6.6 %attention_back.12 = (bf16[4,2,3,256,512]{4,3,2,1,0:T(8,128)(2,1)}, f32[4,768,128]{2,1,0:T(8,128)}) custom-call(s32[1]{0:T(128)} %bitcast.tens, bf16[4,8,512,512]{3,2,1,0:T(8,128)(2,1)} %get-tuple-element.106.p_ref, bf16[4,8,80,512]{3,2,1,0:T(8,128)(2,1)} %get-tuple-element.107.doa_ref, ...), custom_call_target="tpu_custom_call", output_to_operand_aliasing={{0}: (5, {})} | custom-call | tf_op jit(solution)/shard_map/attention_back/pallas_call | solution.py:363
  180.4 6.8 %attention_back.13 = (bf16[4,2,3,256,512]{4,3,2,1,0:T(8,128)(2,1)}, f32[4,768,128]{2,1,0:T(8,128)}) custom-call(s32[1]{0:T(128)} %bitcast.tens, bf16[4,8,512,512]{3,2,1,0:T(8,128)(2,1)} %get-tuple-element.106.p_ref, bf16[4,8,80,512]{3,2,1,0:T(8,128)(2,1)} %get-tuple-element.107.doa_ref, ...), custom_call_target="tpu_custom_call", output_to_operand_aliasing={{0}: (5, {}), {1}: (6, {})} | custom-call | tf_op jit(solution)/shard_map/attention_back/pallas_call | solution.py:363
  189.7 2.6 collective-permute-start.9
  192.3 6.6 %attention_back.14 = (bf16[4,2,3,256,512]{4,3,2,1,0:T(8,128)(2,1)}, f32[4,768,128]{2,1,0:T(8,128)}) custom-call(s32[1]{0:T(128)} %bitcast.tens, bf16[4,8,512,512]{3,2,1,0:T(8,128)(2,1)} %get-tuple-element.106.p_ref, bf16[4,8,80,512]{3,2,1,0:T(8,128)(2,1)} %get-tuple-element.107.doa_ref, ...), custom_call_target="tpu_custom_call", output_to_operand_aliasing={{0}: (5, {}), {1}: (6, {})} | custom-call | tf_op jit(solution)/shard_map/attention_back/pallas_call | solution.py:363
  203.8 6.6 %attention_back.15 = (bf16[4,2,3,256,512]{4,3,2,1,0:T(8,128)(2,1)}, f32[4,768,128]{2,1,0:T(8,128)}) custom-call(s32[1]{0:T(128)} %bitcast.tens, bf16[4,8,512,512]{3,2,1,0:T(8,128)(2,1)} %get-tuple-element.106.p_ref, bf16[4,8,80,512]{3,2,1,0:T(8,128)(2,1)} %get-tuple-element.107.doa_ref, ...), custom_call_target="tpu_custom_call", output_to_operand_aliasing={{0}: (5, {}), {1}: (6, {})} | custom-call | tf_op jit(solution)/shard_map/attention_back/pallas_call | solution.py:363
  213.1 2.4 join.8.own
  216.5 2.7 split.10
  221.2 10.1 %norm_one_back.1 = (f32[2048,512]{1,0:T(8,128)}, f32[8,512]{1,0:T(8,128)}) custom-call(s32[1]{0:T(128)} %bitcast.tens, bf16[4,2,3,256,512]{4,3,2,1,0:T(8,128)(2,1)} %get-tuple-element.148.dqkv, bf16[768,512]{1,0:T(8,128)(2,1)} %bitcast.27, bf16[1024,512]{1,0:T(8,128)(2,1)} %copy-done, bf16[4096,512]{1,0:T(8,128)(2,1)} %x_ref.3, ...), custom_call_target="tpu_custom_call" | custom-call | tf_op jit(solution)/shard_map/norm_one_back/pallas_call | solution.py:409
  232.9 2.1 split.11
  237.9 3.0 collective-permute-done.18.recv
  245.0 2.2 collective-permute-done.13
  251.5 3.4 %collective-permute-start.20 = (bf16[192,128]{1,0:T(8,128)(2,1)}, bf16[192,128]{1,0:T(8,128)(2,1)S(1)}, u32[]{:S(2)}, u32[]{:S(2)}) collective-permute-start(bf16[192,128]{1,0:T(8,128)(2,1)} %get-tuple-element.162), channel_id=1, source_target_pairs={{0,16},{1,9},{2,18},{3,11},{4,20},{5,13},{6,22},{7,15},{8,24},{9,1... | collective-permute-start | bytes 147464 | tf_op jit(solution)/shard_map/ppermute | solution.py:457
  256.4 2.2 collective-permute-done.14
  263.8 2.2 collective-permute-done.15
  269.8 3.4 %collective-permute-start.16 = (f32[24,128]{1,0:T(8,128)S(1)}, f32[24,128]{1,0:T(8,128)S(1)}, u32[]{:S(2)}, u32[]{:S(2)}) collective-permute-start(f32[24,128]{1,0:T(8,128)S(1)} %add.20), channel_id=1, source_target_pairs={{0,16},{1,9},{2,18},{3,11},{4,20},{5,13},{6,22},{7,15},{8,24},{9,1... | collective-permute-start | bytes 36872 | tf_op jit(solution)/shard_map/ppermute | solution.py:457
  278.6 6.5 %collective-permute-done.23.recv = bf16[768,128]{1,0:T(8,128)(2,1)S(1)} collective-permute-done((bf16[768,128]{1,0:T(8,128)(2,1)}, bf16[768,128]{1,0:T(8,128)(2,1)S(1)}, u32[]{:S(2)}, u32[]{:S(2)}) %collective-permute-start.23) | collective-permute-done | bytes 196640 | tf_op jit(solution)/shard_map/ppermute | solution.py:457
  290.7 4.3 %finish_mlp.1 = (f32[1024,512]{1,0:T(8,128)}, f32[1024,512]{1,0:T(8,128)}, f32[256,512]{1,0:T(8,128)}, f32[8,128]{1,0:T(8,128)}) custom-call(s32[1]{0:T(128)} %bitcast.2.bits, bf16[4736,128]{1,0:T(8,128)(2,1)} %join.8.own, bf16[4736,128]{1,0:T(8,128)(2,1)} %copy-done.7), custom_call_target="tpu_custom_call" | custom-call | tf_op jit(solution)/shard_map/finish_mlp/pallas_call | solution.py:461
  296.3 2.5 finish_qkv.1
  (140 shorter events, 72.8 us)
Async XLA Ops:
  1.5 4.8 %copy-start.31 = (bf16[512]{0:T(512)(128)(2,1)S(1)}, bf16[512]{0:T(512)(128)(2,1)}, u32[]{:S(2)}) copy-start(bf16[512]{0:T(512)(128)(2,1)} %param.22) | copy-start | bytes 3076
  1.5 4.8 %copy-start.32 = (bf16[512]{0:T(512)(128)(2,1)S(1)}, bf16[512]{0:T(512)(128)(2,1)}, u32[]{:S(2)}) copy-start(bf16[512]{0:T(512)(128)(2,1)} %param.26) | copy-start | bytes 3076
  4.6 44.1 %collective-permute-start.1 = (bf16[2064,512]{1,0:T(8,128)(2,1)}, bf16[2064,512]{1,0:T(8,128)(2,1)S(1)}, u32[]{:S(2)}, u32[]{:S(2)}) collective-permute-start(bf16[2064,512]{1,0:T(8,128)(2,1)} %fusion.1), channel_id=1, source_target_pairs={{0,1},{1,0},{2,3},{3,2},{4,5},{5,4},{6,7},{7,6},{8,9},{9,8},{10,11... | collective-permute-start | bytes 6340616 | tf_op jit(solution)/shard_map/ppermute | solution.py:434
  6.1 4.5 %collective-permute-start = (bf16[1024,512]{1,0:T(8,128)(2,1)}, bf16[1024,512]{1,0:T(8,128)(2,1)S(1)}, u32[]{:S(2)}, u32[]{:S(2)}) collective-permute-start(bf16[1024,512]{1,0:T(8,128)(2,1)} %pad_maximum_fusion), channel_id=1, source_target_pairs={{0,1},{1,0},{2,3},{3,2},{4,5},{5,4},{6,7},{7,6},{8,9},{9,8},{10,11... | collective-permute-start | bytes 3145736 | tf_op jit(solution)/shard_map/ppermute | solution.py:434
  50.0 27.0 %copy-start.25 = (bf16[1024]{0:T(1024)(128)(2,1)S(1)}, bf16[1024]{0:T(1024)(128)(2,1)}, u32[]{:S(2)}) copy-start(bf16[1024]{0:T(1024)(128)(2,1)} %param.24) | copy-start | bytes 6148
  76.6 37.0 %collective-permute-start.2 = (bf16[8208,128]{1,0:T(8,128)(2,1)}, bf16[8208,128]{1,0:T(8,128)(2,1)S(1)}, u32[]{:S(2)}, u32[]{:S(2)}) collective-permute-start(bf16[8208,128]{1,0:T(8,128)(2,1)} %get-tuple-element.101), channel_id=1, source_target_pairs={{0,1},{1,0},{2,3},{3,2},{4,5},{5,4},{6,7},{7,6},{8,9},{9,8},{10,11... | collective-permute-start | bytes 6303752 | tf_op jit(solution)/shard_map/ppermute | solution.py:434
  111.7 1.8 collective-permute-start.3
  120.9 17.4 %collective-permute-start.4 = (bf16[4736,128]{1,0:T(8,128)(2,1)}, bf16[4736,128]{1,0:T(8,128)(2,1)S(1)}, u32[]{:S(2)}, u32[]{:S(2)}) collective-permute-start(bf16[4736,128]{1,0:T(8,128)(2,1)} %get-tuple-element.104), channel_id=1, source_target_pairs={{0,2},{1,5},{2,0},{3,7},{4,6},{5,1},{6,4},{7,3},{8,10},{9,13},{10,... | collective-permute-start | bytes 3637256 | tf_op jit(solution)/shard_map/ppermute | solution.py:457
  142.7 10.3 %collective-permute-start.5 = (bf16[2368,128]{1,0:T(8,128)(2,1)}, bf16[2368,128]{1,0:T(8,128)(2,1)S(1)}, u32[]{:S(2)}, u32[]{:S(2)}) collective-permute-start(bf16[2368,128]{1,0:T(8,128)(2,1)} %get-tuple-element.116), channel_id=1, source_target_pairs={{0,4},{1,3},{2,6},{3,1},{4,0},{5,7},{6,2},{7,5},{8,12},{9,11},{10,... | collective-permute-start | bytes 1818632 | tf_op jit(solution)/shard_map/ppermute | solution.py:457
  156.3 8.7 %collective-permute-start.6 = (bf16[1184,128]{1,0:T(8,128)(2,1)}, bf16[1184,128]{1,0:T(8,128)(2,1)S(1)}, u32[]{:S(2)}, u32[]{:S(2)}) collective-permute-start(bf16[1184,128]{1,0:T(8,128)(2,1)} %get-tuple-element.122), channel_id=1, source_target_pairs={{0,8},{1,17},{2,10},{3,19},{4,12},{5,21},{6,14},{7,23},{8,0},{9,25... | collective-permute-start | bytes 909320 | tf_op jit(solution)/shard_map/ppermute | solution.py:457
  167.7 10.4 %collective-permute-start.7 = (bf16[592,128]{1,0:T(8,128)(2,1)}, bf16[592,128]{1,0:T(8,128)(2,1)S(1)}, u32[]{:S(2)}, u32[]{:S(2)}) collective-permute-start(bf16[592,128]{1,0:T(8,128)(2,1)} %get-tuple-element.128), channel_id=1, source_target_pairs={{0,16},{1,9},{2,18},{3,11},{4,20},{5,13},{6,22},{7,15},{8,24},{9,1... | collective-permute-start | bytes 454664 | tf_op jit(solution)/shard_map/ppermute | solution.py:457
  180.4 6.9 %collective-permute-start.8 = (bf16[592,128]{1,0:T(8,128)(2,1)}, bf16[592,128]{1,0:T(8,128)(2,1)S(1)}, u32[]{:S(2)}, u32[]{:S(2)}) collective-permute-start(bf16[592,128]{1,0:T(8,128)(2,1)} %settle.2.own), channel_id=1, source_target_pairs={{0,16},{1,9},{2,18},{3,11},{4,20},{5,13},{6,22},{7,15},{8,24},{9,1... | collective-permute-start | bytes 454664 | tf_op jit(solution)/shard_map/ppermute | solution.py:457
  180.4 11.8 %copy-start.3 = (bf16[4,768,128]{2,1,0:T(8,128)(2,1)S(1)}, bf16[4,768,128]{2,1,0:T(8,128)(2,1)}, u32[]{:S(2)}) copy-start(bf16[4,768,128]{2,1,0:T(8,128)(2,1)} %get-tuple-element.125) | copy-start | bytes 2359300
  189.7 9.8 %collective-permute-start.9 = (bf16[1184,128]{1,0:T(8,128)(2,1)}, bf16[1184,128]{1,0:T(8,128)(2,1)S(1)}, u32[]{:S(2)}, u32[]{:S(2)}) collective-permute-start(bf16[1184,128]{1,0:T(8,128)(2,1)} %join.6.own), channel_id=1, source_target_pairs={{0,8},{1,17},{2,10},{3,19},{4,12},{5,21},{6,14},{7,23},{8,0},{9,25... | collective-permute-start | bytes 909320 | tf_op jit(solution)/shard_map/ppermute | solution.py:457
  192.3 23.3 %collective-permute-start.11 = (bf16[3072,128]{1,0:T(8,128)(2,1)S(1)}, bf16[3072,128]{1,0:T(8,128)(2,1)S(1)}, u32[]{:S(2)}, u32[]{:S(2)}) collective-permute-start(bf16[3072,128]{1,0:T(8,128)(2,1)S(1)} %bitcast.29), channel_id=1, source_target_pairs={{0,1},{1,0},{2,3},{3,2},{4,5},{5,4},{6,7},{7,6},{8,9},{9,8},{10,11... | collective-permute-start | bytes 2359304 | tf_op jit(solution)/shard_map/ppermute | solution.py:434
  202.0 10.3 %collective-permute-start.10 = (bf16[2368,128]{1,0:T(8,128)(2,1)}, bf16[2368,128]{1,0:T(8,128)(2,1)S(1)}, u32[]{:S(2)}, u32[]{:S(2)}) collective-permute-start(bf16[2368,128]{1,0:T(8,128)(2,1)} %join.7.own), channel_id=1, source_target_pairs={{0,4},{1,3},{2,6},{3,1},{4,0},{5,7},{6,2},{7,5},{8,12},{9,11},{10,... | collective-permute-start | bytes 1818632 | tf_op jit(solution)/shard_map/ppermute | solution.py:457
  213.1 8.1 %copy-start.26 = (f32[8,512]{1,0:T(8,128)S(1)}, f32[8,512]{1,0:T(8,128)}, u32[]{:S(2)}) copy-start(f32[8,512]{1,0:T(8,128)} %get-tuple-element.152) | copy-start | bytes 49156
  215.6 5.3 %copy-start.4 = (bf16[4736,128]{1,0:T(8,128)(2,1)S(1)}, bf16[4736,128]{1,0:T(8,128)(2,1)}, u32[]{:S(2)}) copy-start(bf16[4736,128]{1,0:T(8,128)(2,1)} %join.8.own) | copy-start | bytes 3637252
  219.2 12.9 %collective-permute-start.17 = (bf16[1536,128]{1,0:T(8,128)(2,1)}, bf16[1536,128]{1,0:T(8,128)(2,1)S(1)}, u32[]{:S(2)}, u32[]{:S(2)}) collective-permute-start(bf16[1536,128]{1,0:T(8,128)(2,1)} %get-tuple-element.146), channel_id=1, source_target_pairs={{0,2},{1,5},{2,0},{3,7},{4,6},{5,1},{6,4},{7,3},{8,10},{9,13},{10,... | collective-permute-start | bytes 1179656 | tf_op jit(solution)/shard_map/ppermute | solution.py:457
  220.9 68.8 %collective-permute-start.25 = (bf16[4736,128]{1,0:T(8,128)(2,1)S(1)}, bf16[4736,128]{1,0:T(8,128)(2,1)S(1)}, u32[]{:S(2)}, u32[]{:S(2)}) collective-permute-start(bf16[4736,128]{1,0:T(8,128)(2,1)S(1)} %copy-done.4), channel_id=1, source_target_pairs={{0,2},{1,5},{2,0},{3,7},{4,6},{5,1},{6,4},{7,3},{8,10},{9,13},{10,... | collective-permute-start | bytes 3637256 | tf_op jit(solution)/shard_map/ppermute | solution.py:457
  235.0 5.9 %collective-permute-start.18 = (bf16[768,128]{1,0:T(8,128)(2,1)}, bf16[768,128]{1,0:T(8,128)(2,1)S(1)}, u32[]{:S(2)}, u32[]{:S(2)}) collective-permute-start(bf16[768,128]{1,0:T(8,128)(2,1)} %get-tuple-element.156), channel_id=1, source_target_pairs={{0,4},{1,3},{2,6},{3,1},{4,0},{5,7},{6,2},{7,5},{8,12},{9,11},{10,... | collective-permute-start | bytes 589832 | tf_op jit(solution)/shard_map/ppermute | solution.py:457
  236.7 1.2 collective-permute-start.12
  243.3 5.9 %collective-permute-start.19 = (bf16[384,128]{1,0:T(8,128)(2,1)}, bf16[384,128]{1,0:T(8,128)(2,1)S(1)}, u32[]{:S(2)}, u32[]{:S(2)}) collective-permute-start(bf16[384,128]{1,0:T(8,128)(2,1)} %get-tuple-element.159), channel_id=1, source_target_pairs={{0,8},{1,17},{2,10},{3,19},{4,12},{5,21},{6,14},{7,23},{8,0},{9,25... | collective-permute-start | bytes 294920 | tf_op jit(solution)/shard_map/ppermute | solution.py:457
  243.5 3.7 %collective-permute-start.13 = (f32[24,128]{1,0:T(8,128)S(1)}, f32[24,128]{1,0:T(8,128)S(1)}, u32[]{:S(2)}, u32[]{:S(2)}) collective-permute-start(f32[24,128]{1,0:T(8,128)S(1)} %add.17), channel_id=1, source_target_pairs={{0,2},{1,5},{2,0},{3,7},{4,6},{5,1},{6,4},{7,3},{8,10},{9,13},{10,... | collective-permute-start | bytes 36872 | tf_op jit(solution)/shard_map/ppermute | solution.py:457
  251.5 7.1 %collective-permute-start.20 = (bf16[192,128]{1,0:T(8,128)(2,1)}, bf16[192,128]{1,0:T(8,128)(2,1)S(1)}, u32[]{:S(2)}, u32[]{:S(2)}) collective-permute-start(bf16[192,128]{1,0:T(8,128)(2,1)} %get-tuple-element.162), channel_id=1, source_target_pairs={{0,16},{1,9},{2,18},{3,11},{4,20},{5,13},{6,22},{7,15},{8,24},{9,1... | collective-permute-start | bytes 147464 | tf_op jit(solution)/shard_map/ppermute | solution.py:457
  254.8 3.7 %collective-permute-start.14 = (f32[24,128]{1,0:T(8,128)S(1)}, f32[24,128]{1,0:T(8,128)S(1)}, u32[]{:S(2)}, u32[]{:S(2)}) collective-permute-start(f32[24,128]{1,0:T(8,128)S(1)} %add.18), channel_id=1, source_target_pairs={{0,4},{1,3},{2,6},{3,1},{4,0},{5,7},{6,2},{7,5},{8,12},{9,11},{10,... | collective-permute-start | bytes 36872 | tf_op jit(solution)/shard_map/ppermute | solution.py:457
  260.7 5.3 %collective-permute-start.21 = (bf16[192,128]{1,0:T(8,128)(2,1)}, bf16[192,128]{1,0:T(8,128)(2,1)S(1)}, u32[]{:S(2)}, u32[]{:S(2)}) collective-permute-start(bf16[192,128]{1,0:T(8,128)(2,1)} %settle.3.own), channel_id=1, source_target_pairs={{0,16},{1,9},{2,18},{3,11},{4,20},{5,13},{6,22},{7,15},{8,24},{9,1... | collective-permute-start | bytes 147464 | tf_op jit(solution)/shard_map/ppermute | solution.py:457
  262.3 3.7 %collective-permute-start.15 = (f32[24,128]{1,0:T(8,128)S(1)}, f32[24,128]{1,0:T(8,128)S(1)}, u32[]{:S(2)}, u32[]{:S(2)}) collective-permute-start(f32[24,128]{1,0:T(8,128)S(1)} %add.19), channel_id=1, source_target_pairs={{0,8},{1,17},{2,10},{3,19},{4,12},{5,21},{6,14},{7,23},{8,0},{9,25... | collective-permute-start | bytes 36872 | tf_op jit(solution)/shard_map/ppermute | solution.py:457
  268.1 6.7 %collective-permute-start.22 = (bf16[384,128]{1,0:T(8,128)(2,1)}, bf16[384,128]{1,0:T(8,128)(2,1)S(1)}, u32[]{:S(2)}, u32[]{:S(2)}) collective-permute-start(bf16[384,128]{1,0:T(8,128)(2,1)} %join.9.own), channel_id=1, source_target_pairs={{0,8},{1,17},{2,10},{3,19},{4,12},{5,21},{6,14},{7,23},{8,0},{9,25... | collective-permute-start | bytes 294920 | tf_op jit(solution)/shard_map/ppermute | solution.py:457
  269.8 5.0 %collective-permute-start.16 = (f32[24,128]{1,0:T(8,128)S(1)}, f32[24,128]{1,0:T(8,128)S(1)}, u32[]{:S(2)}, u32[]{:S(2)}) collective-permute-start(f32[24,128]{1,0:T(8,128)S(1)} %add.20), channel_id=1, source_target_pairs={{0,16},{1,9},{2,18},{3,11},{4,20},{5,13},{6,22},{7,15},{8,24},{9,1... | collective-permute-start | bytes 36872 | tf_op jit(solution)/shard_map/ppermute | solution.py:457
  277.1 8.0 %collective-permute-start.23 = (bf16[768,128]{1,0:T(8,128)(2,1)}, bf16[768,128]{1,0:T(8,128)(2,1)S(1)}, u32[]{:S(2)}, u32[]{:S(2)}) collective-permute-start(bf16[768,128]{1,0:T(8,128)(2,1)} %join.10.own), channel_id=1, source_target_pairs={{0,4},{1,3},{2,6},{3,1},{4,0},{5,7},{6,2},{7,5},{8,12},{9,11},{10,... | collective-permute-start | bytes 589832 | tf_op jit(solution)/shard_map/ppermute | solution.py:457
  287.6 8.0 %collective-permute-start.24 = (bf16[1536,128]{1,0:T(8,128)(2,1)}, bf16[1536,128]{1,0:T(8,128)(2,1)S(1)}, u32[]{:S(2)}, u32[]{:S(2)}) collective-permute-start(bf16[1536,128]{1,0:T(8,128)(2,1)} %join.11.own), channel_id=1, source_target_pairs={{0,2},{1,5},{2,0},{3,7},{4,6},{5,1},{6,4},{7,3},{8,10},{9,13},{10,... | collective-permute-start | bytes 1179656 | tf_op jit(solution)/shard_map/ppermute | solution.py:457
  (27 other events, 44.9 us)

commit v2 on v1

v2 whole, which is shorter than its diff:
```python
import functools

import jax
import jax.numpy as jnp
from jax import lax
from jax.experimental import pallas as pl
from jax.experimental.pallas import tpu as pltpu
from jax.sharding import PartitionSpec as P

D = 512
HD = 64
LAT = 512
AUG = 16
EPS = 1e-05
NEG = -1e30
BF = jnp.bfloat16
F32 = jnp.float32
MIB = 2**20
SWAP = [(0, 1), (1, 0)]
GO_ON = (1, 2, 3)
BACK_SCENES = 2


def _dot(a, b, ca, cb):
    return lax.dot_general(a, b, (((ca,), (cb,)), ((), ())), preferred_element_type=F32)


def hbm(*values):
    return tuple(pltpu.with_memory_space_constraint(v, pltpu.HBM) for v in values)


def nn(a, b):
    return _dot(a, b, 1, 0)


def nt(a, b):
    return _dot(a, b, 1, 1)


def tn(a, b):
    return _dot(a, b, 0, 0)


def normalised(v):
    c = v - jnp.mean(v, -1, keepdims=True)
    r = lax.rsqrt(jnp.mean(c * c, -1, keepdims=True) + EPS)
    return c * r, r


def norm_back(e, xh, r):
    return r * (e - jnp.mean(e, -1, keepdims=True) - xh * jnp.mean(e * xh, -1, keepdims=True))


def forward_kernel(
    tens, lens, x_ref, vecs, wq_own, wq_oth, wo_own, wo_oth,
    n1_ref, qkv_ref, p_ref, att_ref, rl_ref, h1_ref, n2_ref,
):
    scenes = pl.num_programs(0)
    length = lens[tens[0] * scenes + pl.program_id(0)]
    x = x_ref[...].astype(F32)
    n1 = (normalised(x)[0] * vec(vecs, 0) + vec(vecs, 1)).astype(BF)
    n1_ref[...] = n1
    half = wo_own.shape[0]
    heads = half // HD

    def project(side, t):
        part = nt((wq_own, wq_oth)[side][t * half:(t + 1) * half], n1)
        if t == 0:
            part = part * HD**-0.5
        qkv_ref[0, side, t] = part.astype(BF)

    key_at = lax.broadcasted_iota(jnp.int32, (AUG, LAT), 1)
    row_at = lax.broadcasted_iota(jnp.int32, (AUG, LAT), 0)
    bias = jnp.where((key_at >= length) & (row_at == 0), NEG, 0.0).astype(BF)
    ones = jnp.ones((AUG, LAT), BF)

    def part_of(t, h):
        return qkv_ref[0, h // heads, t, h % heads * HD:h % heads * HD + HD]

    def scores(h):
        return tn(jnp.concatenate([part_of(1, h), bias], 0), jnp.concatenate([part_of(0, h), ones], 0))

    def weights(h, s):
        p = jnp.exp(s - jnp.max(s, 0, keepdims=True)).astype(BF)
        p_ref[0, h] = p
        return p

    def attend(h, p):
        o = nn(jnp.concatenate([part_of(2, h), ones], 0), p)
        rl = 1.0 / o[HD:HD + 1]
        rl_ref[0, h:h + 1] = rl
        att_ref[0, h * HD:h * HD + HD] = (o[:HD] * rl).astype(BF)

    for t in (1, 0, 2):
        project(0, t)
    scored, weighed = [], []
    total = None
    for h in range(2 * heads + 2):
        if h < 2 * heads:
            scored.append(scores(h))
        if h in (1, 2, 3):
            project(1, (1, 0, 2)[h - 1])
        if h >= 2:
            attend(h - 2, weighed.pop(0))
        if 1 <= h <= 2 * heads:
            weighed.append(weights(h - 1, scored.pop(0)))
        if h == heads + 2:
            total = tn(att_ref[0, :half], wo_own[...])
    h1 = x + (total + tn(att_ref[0, half:], wo_oth[...])) + vec(vecs, 2)
    h1_ref[...] = h1
    n2_ref[...] = (normalised(h1)[0] * vec(vecs, 3) + vec(vecs, 4)).astype(BF)


def whole(shape, row=0):
    at = (row,) + (0,) * (len(shape) - 1)
    return pl.BlockSpec(shape, lambda i, *_: at, pipeline_mode=pl.Buffered(1))


def params(mib):
    return pltpu.CompilerParams(vmem_limit_bytes=mib * MIB, dimension_semantics=("arbitrary",))


def vec(vecs, i):
    return vecs[i:i + 1].astype(F32)


def vecs_spec(row=0):
    return whole((16, D), row)


def attention_forward(tens, lens, x, vecs, wq_own, theirs, wo_own, rows):
    scenes = rows // LAT
    rowblock = pl.BlockSpec((LAT, D), lambda i, *_: (i, 0))
    half = wo_own.shape[0]
    return pl.pallas_call(
        forward_kernel,
        grid_spec=pltpu.PrefetchScalarGridSpec(
            num_scalar_prefetch=2,
            grid=(scenes,),
            in_specs=[
                pl.BlockSpec((LAT, D), lambda i, tens, lens: (tens[0] * scenes + i, 0)),
                vecs_spec(), whole((3 * half, D)), whole((3 * half, D)), whole((half, D)), whole((half, D), 3),
            ],
            out_specs=[
                rowblock,
                pl.BlockSpec((1, 2, 3, half, LAT), lambda i, *_: (i, 0, 0, 0, 0)),
                pl.BlockSpec((1, 2 * half // HD, LAT, LAT), lambda i, *_: (i, 0, 0, 0)),
                pl.BlockSpec((1, D, LAT), lambda i, *_: (i, 0, 0)),
                pl.BlockSpec((1, 2 * half // HD, LAT), lambda i, *_: (i, 0, 0)),
                rowblock,
                rowblock,
            ],
        ),
        out_shape=[
            pltpu.HBM((rows, D), BF),
            pltpu.HBM((scenes, 2, 3, half, LAT), BF),
            pltpu.HBM((scenes, 2 * half // HD, LAT, LAT), BF),
            pltpu.HBM((scenes, D, LAT), BF),
            pltpu.HBM((scenes, 2 * half // HD, LAT), F32),
            pltpu.HBM((rows, D), F32),
            pltpu.HBM((rows, D), BF),
        ],
        compiler_params=params(40),
        name="attention_forward",
    )(tens, lens, *hbm(x, vecs, wq_own, theirs, wo_own, theirs))


LOG2E = 1.4426950408889634
SUB = 256


def gelu_parts(z):
    cdf = 0.5 + 0.5 * lax.erf(z * 0.7071067811865476)
    return z * cdf, cdf + z * (0.3989422804014327 * jnp.exp2(z * z * (-0.5 * LOG2E)))


def put_slabs(out, at, values):
    n = values.shape[0]
    for c in range(D // 128):
        out[at + c * n:at + (c + 1) * n] = values[:, c * 128:c * 128 + 128].astype(out.dtype)


def put_row(out, at, row, count):
    parts = [row[:, c * 128:c * 128 + 128] for c in range(row.shape[1] // 128)]
    parts += [jnp.zeros((1, 128), F32)] * (count - len(parts))
    out[at:at + count] = jnp.concatenate(parts, 0).astype(out.dtype)


def mlp_kernel(
    tens, n2_ref, cot_ref, up_own, down_own, up_oth, down_oth, vecs_oth, vecs, h1_ref, att_ref, rl_ref, wo_own, wo_oth,
    block_ref, gh_ref, doa_ref, own_ref, oth_ref, cols_ref, acc_up, acc_down, acc_ub, acc_wo,
):
    @pl.when(pl.program_id(0) == 0)
    def _():
        acc_up[...] = jnp.zeros_like(acc_up)
        acc_down[...] = jnp.zeros_like(acc_down)
        acc_ub[...] = jnp.zeros_like(acc_ub)
        acc_wo[...] = jnp.zeros_like(acc_wo)
        cols_ref[...] = jnp.zeros_like(cols_ref)

    n2, cot = n2_ref[...], cot_ref[...]
    units = up_own.shape[0]
    per = units // SUB

    def place(j):
        side, at = divmod(j, per)
        ups, downs, rows = ((up_own, down_own, vecs), (up_oth, down_oth, vecs_oth))[side]
        at = slice(at * SUB, at * SUB + SUB)
        first = at.start // D
        return ups[at], downs[at], vec(rows, 6 + first)[:, at.start - first * D:at.stop - first * D]

    def before(j):
        u, d, b = place(j)
        return nt(n2, u) + b, nt(cot, d)

    def between(pre, grad_act):
        act, slope = gelu_parts(pre)
        return act.astype(BF), (grad_act * slope).astype(BF)

    def after(j, act, dpre):
        u, d, _ = place(j)
        at = slice(j * SUB, j * SUB + SUB)
        acc_down[at] += tn(act, cot)
        acc_up[at] += tn(dpre, n2)
        acc_ub[:, at] += jnp.sum(dpre.astype(F32), 0, keepdims=True)
        return nn(act, d), nn(dpre, u)

    out, back = 0.0, 0.0
    first, second = [], []
    for j in range(2 * per + 2):
        if j < 2 * per:
            first.append(before(j))
        if j >= 2:
            o, b = after(j - 2, *second.pop(0))
            out, back = out + o, back + b
        if 1 <= j <= 2 * per:
            second.append(between(*first.pop(0)))
    h1 = h1_ref[...]
    block_ref[...] = (h1 + out + vec(vecs, 5)).astype(BF)
    xh, r = normalised(h1)
    cot32 = cot.astype(F32)
    gh = cot32 + norm_back(back * vec(vecs, 3), xh, r)
    gh_ref[...] = gh
    gb = gh.astype(BF)
    half = wo_own.shape[0]
    heads = half // HD
    zeros = jnp.zeros((AUG - 3, LAT), F32)
    for side, w in enumerate((wo_own, wo_oth)):
        do = nt(w[...], gb)
        for h in range(heads):
            hh = side * heads + h
            scaled = (do[h * HD:h * HD + HD] * rl_ref[0, hh:hh + 1]).astype(BF)
            doa_ref[0, hh, :HD] = scaled
            delta = -jnp.sum(scaled.astype(F32) * att_ref[0, hh * HD:hh * HD + HD].astype(F32), 0, keepdims=True)
            high = delta.astype(BF).astype(F32)
            low = (delta - high).astype(BF).astype(F32)
            doa_ref[0, hh, HD:] = jnp.concatenate([high, low, delta - high - low, zeros], 0).astype(BF)
    acc_wo[...] += nn(att_ref[0], gb)
    cols_ref[...] += jnp.concatenate(
        [jnp.sum(v, 0, keepdims=True) for v in (back * xh, back, gh, cot32)] + [jnp.zeros((4, D), F32)], 0
    )

    @pl.when(pl.program_id(0) == pl.num_programs(0) - 1)
    def _():
        base = 8 * units + 4 * half
        for side, ref in enumerate((own_ref, oth_ref)):
            put_slabs(ref, 0, acc_up.at[side * units:(side + 1) * units])
            put_slabs(ref, 4 * units, acc_down.at[side * units:(side + 1) * units])
            put_slabs(ref, 8 * units, acc_wo.at[side * half:(side + 1) * half])
            put_row(ref, base, acc_ub[:, side * units:(side + 1) * units], 16)
            if ref.shape[0] > base + 16:
                ref[base + 16:] = jnp.zeros((ref.shape[0] - base - 16, 128), ref.dtype)


def mlp(tens, n2, cot, up, down, up_oth, down_oth, theirs, vecs, h1, att, rl, wo, total_rows):
    rows = n2.shape[0]
    scenes = rows // LAT
    units, half = up.shape[0], wo.shape[0]
    heads = 2 * half // HD
    rowblock = pl.BlockSpec((LAT, D), lambda i, *_: (i, 0))
    weights = whole((units, D))
    return pl.pallas_call(
        mlp_kernel,
        grid_spec=pltpu.PrefetchScalarGridSpec(
            num_scalar_prefetch=1,
            grid=(scenes,),
            in_specs=[
                rowblock,
                pl.BlockSpec((LAT, D), lambda i, tens: (tens[0] * scenes + i, 0)),
                weights, weights, weights, weights, vecs_spec(theirs.shape[0] // 16 - 1), vecs_spec(), rowblock,
                pl.BlockSpec((1, D, LAT), lambda i, *_: (i, 0, 0)),
                pl.BlockSpec((1, heads, LAT), lambda i, *_: (i, 0, 0)),
                whole((half, D)), whole((half, D), 3),
            ],
            out_specs=[
                rowblock, rowblock,
                pl.BlockSpec((1, heads, HD + AUG, LAT), lambda i, *_: (i, 0, 0, 0)),
                whole((total_rows, 128)), whole((total_rows, 128)), whole((8, D)),
            ],
            scratch_shapes=[
                pltpu.VMEM((2 * units, D), F32), pltpu.VMEM((2 * units, D), F32), pltpu.VMEM((1, 2 * units), F32),
                pltpu.VMEM((2 * half, D), F32),
            ],
        ),
        out_shape=[
            pltpu.HBM((rows, D), BF),
            pltpu.HBM((rows, D), F32),
            pltpu.HBM((scenes, heads, HD + AUG, LAT), BF),
            pltpu.HBM((total_rows, 128), BF),
            pltpu.HBM((total_rows, 128), BF),
            pltpu.HBM((8, D), F32),
        ],
        compiler_params=params(56),
        name="mlp",
    )(tens, *hbm(n2, cot, up, down, up_oth, down_oth, theirs, vecs, h1, att, rl, wo, theirs))


def back_kernel(tens, p_ref, doa_ref, qkv_ref, n1_ref, *refs, ends):
    starts, stops = ends
    dqkv_ref, dw_ref, acc = refs[-3:]
    groups = acc.shape[0]
    ones = jnp.ones((AUG, LAT), BF)
    count = p_ref.shape[1]

    @pl.when((pl.program_id(0) == 0) & (pl.program_id(1) == 0))
    def _():
        if starts:
            acc[...] = jnp.zeros_like(acc)
        else:
            acc[...] = refs[0][...]

    def part_of(t, h):
        return qkv_ref[0, 0, t, h * HD:h * HD + HD]

    def first(h):
        return tn(jnp.concatenate([part_of(2, h), ones], 0), doa_ref[0, h])

    def second(h, grad):
        return (p_ref[0, h].astype(F32) * grad).astype(BF)

    def third(h, ds):
        at = slice(h * HD, h * HD + HD)
        dqkv_ref[0, 0, 0, at] = (nn(part_of(1, h), ds) * HD**-0.5).astype(BF)
        dqkv_ref[0, 0, 1, at] = nt(part_of(0, h), ds).astype(BF)

    def values(h):
        dqkv_ref[0, 0, 2, h * HD:h * HD + HD] = nt(doa_ref[0, h, :HD], p_ref[0, h]).astype(BF)

    grads, scores = [], []
    for h in range(count + 1):
        if h < count:
            grads.append(first(h))
            values(h)
        if h >= 1:
            third(h - 1, scores.pop(0))
        if h < count:
            scores.append(second(h, grads.pop(0)))
    feats = count * HD
    group = pl.program_id(1)
    term = nn(dqkv_ref[0, 0].reshape(3 * feats, LAT), n1_ref[...])
    acc[group] += term.reshape(3, feats, D)

    @pl.when((pl.program_id(0) == pl.num_programs(0) - 1) & (pl.program_id(1) == groups - 1))
    def _():
        if not stops:
            dw_ref[...] = acc[...]
            return
        for c in range(D // 128):
            for t in range(3):
                for g in range(groups):
                    row = ((c * 3 + t) * groups + g) * feats
                    dw_ref[row:row + feats] = acc[g, t, :, c * 128:c * 128 + 128].astype(dw_ref.dtype)
        used = 12 * groups * feats
        if used < dw_ref.shape[0]:
            dw_ref[used:] = jnp.zeros((dw_ref.shape[0] - used, 128), dw_ref.dtype)


BACK_HEADS = 2


def attention_back(tens, p, doa, qkv, n1, dqkv, partial, side, first, count, total_rows):
    scenes, heads = p.shape[0], p.shape[1] // 2
    steps = heads // BACK_HEADS
    feats = BACK_HEADS * HD
    block = lambda i, j, *_: (first + i, side, 0, j, 0)
    head_block = lambda i, j, *_: (first + i, side * steps + j, 0, 0)
    ends = (first == 0, first + count == scenes)
    sums = (steps, 3, feats, D)
    zeros = lambda i, j, *_: (0, 0, 0, 0)
    carried, specs, aliases = [], [], {}
    if not ends[0]:
        carried.append(partial)
        specs.append(pl.BlockSpec(sums, zeros, pipeline_mode=pl.Buffered(1)))
    if dqkv is not None:
        aliases = {5 + len(carried): 0}
        carried.append(dqkv)
        specs.append(pl.BlockSpec(memory_space=pl.ANY))
    if ends[1]:
        dw = jax.ShapeDtypeStruct((total_rows, 128), BF if side else F32)
        dw_spec = pl.BlockSpec((total_rows, 128), lambda i, j, *_: (0, 0), pipeline_mode=pl.Buffered(1))
    else:
        dw = pltpu.HBM(sums, F32)
        dw_spec = pl.BlockSpec(sums, zeros, pipeline_mode=pl.Buffered(1))
    return pl.pallas_call(
        functools.partial(back_kernel, ends=ends),
        grid_spec=pltpu.PrefetchScalarGridSpec(
            num_scalar_prefetch=1,
            grid=(count, steps),
            in_specs=[
                pl.BlockSpec((1, BACK_HEADS, LAT, LAT), head_block),
                pl.BlockSpec((1, BACK_HEADS, HD + AUG, LAT), head_block),
                pl.BlockSpec((1, 1, 3, feats, LAT), block),
                pl.BlockSpec((LAT, D), lambda i, j, *_: (first + i, 0)),
            ] + specs,
            out_specs=[pl.BlockSpec((1, 1, 3, feats, LAT), block), dw_spec],
            scratch_shapes=[pltpu.VMEM(sums, F32)],
        ),
        out_shape=[pltpu.HBM(qkv.shape, BF), dw],
        input_output_aliases=aliases,
        compiler_params=pltpu.CompilerParams(vmem_limit_bytes=24 * MIB, dimension_semantics=("arbitrary", "arbitrary")),
        name="attention_back",
    )(tens, *hbm(p, doa, qkv, n1, *carried))


def norm_one_back_kernel(tens, dqkv, wq_own, wq_oth, x_ref, vecs, gh_ref, gl_ref, cols_ref):
    feats = wq_own.shape[0]
    g = tn(dqkv[0, 0].reshape(feats, LAT), wq_own[...]) + tn(dqkv[0, 1].reshape(feats, LAT), wq_oth[...])
    xh, r = normalised(x_ref[...].astype(F32))
    gl_ref[...] = gh_ref[...] + norm_back(g * vec(vecs, 0), xh, r)
    sums = jnp.concatenate([jnp.sum(v, 0, keepdims=True) for v in (g * xh, g)] + [jnp.zeros((6, D), F32)], 0)

    @pl.when(pl.program_id(0) == 0)
    def _():
        cols_ref[...] = sums

    @pl.when(pl.program_id(0) > 0)
    def _():
        cols_ref[...] += sums


def norm_one_back(tens, dqkv, wq_own, theirs, x, vecs, gh):
    scenes, half = dqkv.shape[0], dqkv.shape[3]
    rowblock = pl.BlockSpec((LAT, D), lambda i, *_: (i, 0))
    return pl.pallas_call(
        norm_one_back_kernel,
        grid_spec=pltpu.PrefetchScalarGridSpec(
            num_scalar_prefetch=1,
            grid=(scenes,),
            in_specs=[
                pl.BlockSpec((1, 2, 3, half, LAT), lambda i, *_: (i, 0, 0, 0, 0)),
                whole((3 * half, D)), whole((3 * half, D)),
                pl.BlockSpec((LAT, D), lambda i, tens: (tens[0] * scenes + i, 0)),
                vecs_spec(),
                rowblock,
            ],
            out_specs=[rowblock, whole((8, D))],
        ),
        out_shape=[pltpu.HBM((scenes * LAT, D), F32), pltpu.HBM((8, D), F32)],
        compiler_params=params(28),
        name="norm_one_back",
    )(tens, *hbm(dqkv), wq_own, theirs, *hbm(x), vecs, *hbm(gh))


def tie(value, *after):
    return lax.optimization_barrier((value, *after))[0]


def swap(v):
    return lax.ppermute(v, "tensor", SWAP)


class Stage:
    def __init__(self, count, bits, distances=None):
        self.count, self.bits = count, bits
        self.size = 1 << len(bits[0])
        each = list(range(1, self.size))
        self.distances = distances or (each, each)
        at = lax.axis_index("dp")
        core = lax.axis_index("tensor")

        def value(t, v):
            return sum((jnp.right_shift(v, b) & 1) << k for k, b in enumerate(bits[t]))

        self.place = jnp.where(core == 0, value(0, at), value(1, at)).astype(jnp.int32)
        met = [jnp.where(core == 0, self.distances[0][k], self.distances[1][k]) ^ self.place for k in range(self.size - 1)]
        self.scalars = jnp.stack([self.place] + met).astype(jnp.int32)

    def exchange(self, values):
        out = []
        for k, v in enumerate(values):
            pairs = []
            for i in range(self.count):
                for t in range(2):
                    d = self.distances[t][k]
                    flip = sum(((d >> j) & 1) << b for j, b in enumerate(self.bits[t]))
                    pairs.append((i * 2 + t, (i ^ flip) * 2 + t))
            out.append(lax.ppermute(v, ("dp", "tensor"), pairs))
        return out


def small_call(kernel, out_shape, name, scalars, *arrays, scratch=(), mib=16):
    return pl.pallas_call(
        kernel,
        in_specs=[pl.BlockSpec(memory_space=pltpu.SMEM)] + [pl.BlockSpec(memory_space=pltpu.VMEM)] * len(arrays),
        out_specs=[pl.BlockSpec(memory_space=pltpu.VMEM)] * len(out_shape),
        out_shape=out_shape,
        scratch_shapes=list(scratch),
        compiler_params=pltpu.CompilerParams(vmem_limit_bytes=mib * MIB),
        name=name,
    )(scalars, *arrays)


def pack_kernel(*refs):
    (*rows, up_bias, wq, wo), (packed, vecs), scratch = refs[:9], refs[9:11], refs[11:]
    *held, whole_sem, sem = scratch
    first = wq.shape[0]
    everything = held[-1]
    last = everything.shape[0] - 16
    big = [
        pltpu.make_async_copy(wq, everything.at[pl.ds(0, first)], sem.at[0]),
        pltpu.make_async_copy(wo, everything.at[pl.ds(first, last - first)], sem.at[1]),
    ]
    small = [pltpu.make_async_copy(r, h, sem.at[2 + k]) for k, (r, h) in enumerate(zip((*rows, up_bias), held))]
    for c in big + small:
        c.start()
    for c in small:
        c.wait()
    parts = [h[...].astype(F32).reshape(1, D) for h in held[:-2]]
    bias = held[-2][...].astype(F32)
    parts += [bias[i:i + D].reshape(1, D) for i in range(0, bias.shape[0], D)]
    everything[last:] = jnp.concatenate(parts + [jnp.zeros((16 - len(parts), D), F32)], 0).astype(BF)
    for c in big:
        c.wait()
    out = [
        pltpu.make_async_copy(everything, packed, whole_sem.at[0]),
        pltpu.make_async_copy(everything.at[pl.ds(last, 16)], vecs, whole_sem.at[1]),
    ]
    for c in out:
        c.start()
    for c in out:
        c.wait()


def pack(rows, up_bias, wq, wo):
    shape = (wq.shape[0] + wo.shape[0] + 16, D)
    return pl.pallas_call(
        pack_kernel,
        in_specs=[pl.BlockSpec(memory_space=pl.ANY)] * 9,
        out_specs=[pl.BlockSpec(memory_space=pl.ANY)] * 2,
        out_shape=[pltpu.HBM(shape, BF), pltpu.HBM((16, D), BF)],
        scratch_shapes=[pltpu.VMEM((D,), BF)] * 6 + [
            pltpu.VMEM(up_bias.shape, BF), pltpu.VMEM(shape, BF), pltpu.SemaphoreType.DMA((2,)),
            pltpu.SemaphoreType.DMA((9,)),
        ],
        compiler_params=pltpu.CompilerParams(vmem_limit_bytes=16 * MIB),
        name="pack",
    )(*hbm(*rows, up_bias, wq, wo))


def chunk(place, m):
    return pl.ds(pl.multiple_of(place * m, 16), m)


def hand_out(total, scalars, keep_out, sends):
    m = keep_out.shape[0]
    keep_out[...] = total[chunk(scalars[0], m)]
    for k, out in enumerate(sends):
        out[...] = total[chunk(scalars[1 + k], m)].astype(BF)


def split_kernel(scalars, *refs, count):
    (keep, *recvs), (keep_out, *sends), total = refs[:count], refs[count:-1], refs[-1]
    v = keep[...]
    for r in recvs:
        v = v + r[...].astype(F32)
    total[...] = v
    hand_out(total, scalars, keep_out, sends)


def pieces(stage, rows):
    m = rows // stage.size
    return [jax.ShapeDtypeStruct((m, 128), F32)] + [jax.ShapeDtypeStruct((m, 128), BF)] * (stage.size - 1)


def split(keep, recvs, stage):
    keep, *sends = small_call(
        functools.partial(split_kernel, count=1 + len(recvs)), pieces(stage, keep.shape[0]), "split", stage.scalars, keep,
        *recvs, scratch=[pltpu.VMEM(keep.shape, F32)],
    )
    return keep, sends


def settle_kernel(scalars, keep, *refs):
    v = keep[...]
    for r in refs[:-1]:
        v = v + r[...].astype(F32)
    refs[-1][...] = v.astype(BF)


def settle(keep, recvs, stage):
    return small_call(settle_kernel, [jax.ShapeDtypeStruct(keep.shape, BF)], "settle", stage.scalars, keep, *recvs)[0]


def fill(full, scalars, own, recvs):
    m = full.shape[0] // (1 + len(recvs))
    full[chunk(scalars[0], m)] = own[:m]
    for k, r in enumerate(recvs):
        full[chunk(scalars[1 + k], m)] = r[:m]


def join_kernel(scalars, own, *refs):
    fill(refs[-1], scalars, own, refs[:-1])


def join(own, recvs, stage):
    return small_call(
        join_kernel, [jax.ShapeDtypeStruct((stage.size * own.shape[0], 128), BF)], "join", stage.scalars, own, *recvs
    )[0]


def split_mlp_kernel(scalars, own, recv, keep_out, *sends):
    m = keep_out.shape[0]
    at = chunk(scalars[0], m)
    keep_out[...] = own[at].astype(F32) + recv[at].astype(F32)
    for k, out in enumerate(sends):
        at = chunk(scalars[1 + k], m)
        out[...] = (own[at].astype(F32) + recv[at].astype(F32)).astype(BF)


def split_mlp(own, recv, stage):
    keep, *sends = small_call(
        split_mlp_kernel, pieces(stage, own.shape[0]), "split_mlp", stage.scalars, *hbm(own), recv, mib=24,
    )
    return keep, sends


def finish_mlp_kernel(scalars, *refs):
    (own, *recvs), (dup, ddown, dwo, dub), full = refs[:-5], refs[-5:-1], refs[-1]
    fill(full, scalars, own, recvs)
    units, half = dup.shape[0], dwo.shape[0]
    for c in range(D // 128):
        at = slice(c * 128, c * 128 + 128)
        dup[:, at] = full[c * units:(c + 1) * units].astype(F32)
        ddown[:, at] = full[(4 + c) * units:(5 + c) * units].astype(F32)
        dwo[:, at] = full[8 * units + c * half:8 * units + (c + 1) * half].astype(F32)
    base = 8 * units + 4 * half
    dub[...] = full[base:base + dub.shape[0]].astype(F32)


def finish_mlp(own, recvs, stage, units, half):
    return small_call(
        finish_mlp_kernel,
        [
            jax.ShapeDtypeStruct((units, D), F32), jax.ShapeDtypeStruct((units, D), F32),
            jax.ShapeDtypeStruct((half, D), F32), jax.ShapeDtypeStruct((units // 128, 128), F32),
        ],
        "finish_mlp", stage.scalars, own, *recvs, scratch=[pltpu.VMEM((stage.size * own.shape[0], 128), BF)],
    )


def parts_of(v):
    high = v.astype(BF)
    return jnp.concatenate([high, (v - high.astype(F32)).astype(BF)], 0)


def whole_of(v):
    m = v.shape[0] // 2
    return v[:m].astype(F32) + v[m:].astype(F32)


def settle_cols_kernel(scalars, keep, *refs):
    *recvs, cols, cols_recv, out = refs
    m = keep.shape[0]
    v = keep[...]
    for r in recvs:
        v = v + r[...].astype(F32)
    out[:m] = v.astype(BF)
    out[m:] = parts_of(cols[...] + cols_recv[...])


def settle_cols(keep, recvs, cols, cols_recv, stage):
    shape = (keep.shape[0] + 2 * cols.shape[0], 128)
    return small_call(
        settle_cols_kernel, [jax.ShapeDtypeStruct(shape, BF)], "settle_cols", stage.scalars, keep, *recvs, cols, cols_recv
    )[0]


def sum_cols(scalars, own, recvs, m, held):
    held[scalars[0]] = whole_of(own[m:])
    for k, r in enumerate(recvs):
        held[scalars[1 + k]] = whole_of(r[m:])
    total = held[0]
    for k in range(1, held.shape[0]):
        total = total + held[k]
    return total


def join_cols_kernel(scalars, *refs):
    (own, *recvs), out, held = refs[:-2], refs[-2], refs[-1]
    size = 1 + len(recvs)
    m = own.shape[0] - 2 * held.shape[1]
    fill(out.at[pl.ds(0, size * m)], scalars, own, recvs)
    out[size * m:] = parts_of(sum_cols(scalars, own, recvs, m, held))


def join_cols(own, recvs, stage, extra):
    m = own.shape[0] - extra
    return small_call(
        join_cols_kernel, [jax.ShapeDtypeStruct((stage.size * m + extra, 128), BF)], "join_cols", stage.scalars, own, *recvs,
        scratch=[pltpu.VMEM((stage.size, extra // 2, 128), F32)],
    )[0]


def finish_qkv_kernel(scalars, *refs):
    (own, *recvs), (out, cols), (full, held) = refs[:-4], refs[-4:-2], refs[-2:]
    m = full.shape[0] // (1 + len(recvs))
    fill(full, scalars, own, recvs)
    cols[...] = sum_cols(scalars, own, recvs, m, held)
    half = out.shape[1]
    for c in range(D // 128):
        for t in range(3):
            row = (c * 3 + t) * half
            out[t, :, c * 128:c * 128 + 128] = full[row:row + half].astype(F32)


def finish_qkv(own, recvs, stage, half, extra):
    m = own.shape[0] - extra
    return small_call(
        finish_qkv_kernel,
        [jax.ShapeDtypeStruct((3, half, D), F32), jax.ShapeDtypeStruct((extra // 2, 128), F32)],
        "finish_qkv", stage.scalars, own, *recvs,
        scratch=[pltpu.VMEM((stage.size * m, 128), BF), pltpu.VMEM((stage.size, extra // 2, 128), F32)],
    )


def advance(steps, token):
    try:
        return steps.send(token), None
    except StopIteration as end:
        return token, end.value


def body(
    latents, scene_len, attn_gain, attn_shift, qkv_weight, out_weight, out_bias, mlp_gain, mlp_shift,
    up_weight, up_bias, down_weight, down_bias, cotangent,
):
    rows = latents.shape[0] // lax.axis_size("tensor")
    units, half = up_weight.shape[0], out_weight.shape[0]
    heads = half // HD
    tens = lax.axis_index("tensor").astype(jnp.int32).reshape(1)
    count = lax.axis_size("dp")
    steps = count.bit_length() - 1
    assert 1 << steps == count and steps > 1
    lower, upper = list(range(steps - 2)), [steps - 2, steps - 1]
    turned = [b ^ 1 if b ^ 1 < steps - 2 else b for b in lower]
    group = Stage(count, (upper, upper), ([1, 2, 3], [2, 1, 3]))
    pairs = [Stage(count, ([a], [b])) for a, b in zip(lower, turned)]
    mlp_stages = pairs + [group]
    if len(lower) % 2:
        qkv_stages = mlp_stages
    else:
        qkv_stages = [
            Stage(count, (lower[i:i + 2],) * 2, ([1, 2, 3], [2, 1, 3])) for i in range(0, len(lower), 2)
        ] + [group]

    packed, vecs = pack(
        (attn_gain, attn_shift, out_bias, mlp_gain, mlp_shift, down_bias), up_bias, qkv_weight.reshape(3 * half, D), out_weight
    )
    theirs = swap(packed)
    up_oth, down_oth = swap(up_weight), swap(down_weight)

    n1, qkv, p, att, rl, h1, n2 = attention_forward(
        tens, scene_len, latents, vecs, qkv_weight.reshape(3 * half, D), theirs, out_weight, rows
    )
    need = 8 * units + 4 * half + 16
    total_rows = -(-need // (16 * count)) * 16 * count
    block_out, gh, doa, grads_own, grads_oth, cols_two = mlp(
        tens, n2, cotangent, up_weight, down_weight, up_oth, down_oth, theirs, vecs, h1, att, rl, out_weight, total_rows
    )
    from_peer = swap(grads_oth)

    def exchanges(stages, keep, sends, settled, joined):
        for s, stage in enumerate(stages):
            recvs = stage.exchange(sends)
            token = yield sends[-1]
            recvs = [tie(r, token) for r in recvs]
            if s + 1 < len(stages):
                keep, sends = split(keep, recvs, stages[s + 1])
            else:
                have = settled(keep, recvs, stage)
        for s in range(len(stages) - 1, -1, -1):
            recvs = stages[s].exchange([have] * (stages[s].size - 1))
            token = yield have
            recvs = [tie(r, token) for r in recvs]
            if s:
                have = joined(have, recvs, stages[s])
        return have, recvs

    scenes = rows // LAT
    qkv_rows = -(-12 * half // (16 * count)) * 16 * count
    dqkv, dw = None, None
    token = grads_oth
    mlp_steps, mlp_result = None, None
    calls = 0
    for side in (1, 0):
        for scene in range(0, scenes, BACK_SCENES):
            dqkv, dw = attention_back(tie(tens, token), p, doa, qkv, n1, dqkv, dw, side, scene, BACK_SCENES, qkv_rows)
            token = dw
            if calls == 0:
                mlp_steps = exchanges(mlp_stages, *split_mlp(grads_own, tie(from_peer, token), mlp_stages[0]), settle, join)
                token = next(mlp_steps)
            elif calls in GO_ON and mlp_result is None:
                token, mlp_result = advance(mlp_steps, token)
            calls += 1
        if side:
            qkv_peer = swap(dw)
    keep, sends = split(dw, [qkv_peer], qkv_stages[0])
    cols = []
    extra = 48
    qkv_steps = exchanges(
        qkv_stages, keep, sends, lambda keep, recvs, stage: settle_cols(keep, recvs, *cols, stage),
        lambda own, recvs, stage: join_cols(own, recvs, stage, extra),
    )
    token = next(qkv_steps)
    grad_latents, cols_one = norm_one_back(tie(tens, token), dqkv, qkv_weight.reshape(3 * half, D), theirs, latents, vecs, gh)
    cols.append(jnp.concatenate([cols_one[:2], cols_two[:4]], 0).reshape(24, 128))
    cols.append(swap(cols[0]))
    token, qkv_result = advance(qkv_steps, cols_one)
    while mlp_result is None:
        token, mlp_result = advance(mlp_steps, token)
    dup, ddown, dwo, dub = finish_mlp(tie(mlp_result[0], token), *mlp_result[1:], mlp_stages[0], units, half)
    token = dub
    while qkv_result is None:
        token, qkv_result = advance(qkv_steps, token)
    dwq, shared = finish_qkv(*qkv_result, qkv_stages[0], half, extra)
    shared = shared.reshape(6, D)
    return (
        block_out, grad_latents, shared[0], shared[1], dwq, dwo, shared[4],
        shared[2], shared[3], dup, dub.reshape(units), ddown, shared[5],
    )


def solution(mesh):
    placed = (
        P("dp", None), P("dp"), P(), P(), P(None, "tensor", None), P("tensor", None), P(), P(), P(),
        P("tensor", None), P("tensor"), P("tensor", None), P(), P("dp", None),
    )
    return jax.shard_map(
        body,
        mesh=mesh,
        in_specs=placed,
        out_specs=(
            P(("dp", "tensor"), None), P(("dp", "tensor"), None), P(), P(), P(None, "tensor", None),
            P("tensor", None), P(), P(), P(), P("tensor", None), P("tensor"), P("tensor", None), P(),
        ),
        check_vma=False,
    )
```

time: 300 us -> 226 us (0.75)
  Pallas kernels: 204 us -> 130 us
  waiting for transfers between devices: 32.7 us -> 49.6 us
  local copies, waits for them, and re-layouts: 19.2 us -> 5.69 us
  other arithmetic: 4.8 us -> 0.31 us
    pallas_call x10 -> x6, Pallas kernels: 113 us -> 81.6 us  [the longest x1 42.7 us: mlp(): pl.pallas_call(mlp_kernel, grid_spec=pltpu.PrefetchScalarGridSpec(num_sca...]
    pallas_call x18 -> x12, Pallas kernels: 43 us -> 15.3 us  [small_call(): pl.pallas_call(kernel, in_specs=[pl.BlockSpec(memory_space=pltpu.SMEM)] +...]
    ppermute x20 -> x22, waiting for transfers between devices: 26.2 us -> 47.6 us  [exchange(): out.append(lax.ppermute(v, ('dp', 'tensor'), pairs))]
    pallas_call x1, Pallas kernels: 37.1 us -> 23.3 us  [attention_forward(): pl.pallas_call(forward_kernel, grid_spec=pltpu.PrefetchScalarGridSpec(num...]
    unnamed x68 -> x20, local copies, waits for them, and re-layouts: 16.4 us -> 4.36 us
    ppermute x6, waiting for transfers between devices: 6.45 us -> 2.02 us  [swap(): return lax.ppermute(v, 'tensor', SWAP)]
    concatenate x3 -> x1, other arithmetic: 4.18 us -> 0.01 us  [body(): jnp.concatenate([cols_one[:2], cols_two[:4]], 0).reshape(24, 128)]
    ppermute x20 -> x22, starting transfers between devices: 36.4 us -> 37.4 us  [exchange(): out.append(lax.ppermute(v, ('dp', 'tensor'), pairs))]
  transfers between devices with their start and end apart: 26 -> 28, of which waited for: 16 -> 11; matrix products, arithmetic and copies ran while one was open for 1% -> 0% of each run, Pallas kernels for 52% -> 34%
where the time goes in v2:
time: 226 us; the launch traced here: 225 us
  Pallas kernels  130 us (58%)
  waiting for transfers between devices  49.6 us (22%)
  starting transfers between devices  39 us (17%)
  local copies, waits for them, and re-layouts  5.69 us (3%)
    ppermute x22, waiting for transfers between devices, exchange(): out.append(lax.ppermute(v, ('dp', 'tensor'), pairs))  47.6 us
    pallas_call x1, Pallas kernels, mlp(): pl.pallas_call(mlp_kernel, grid_spec=pltpu.PrefetchScalarGridSpec(num_sca...  42.7 us
    ppermute x22, starting transfers between devices, exchange(): out.append(lax.ppermute(v, ('dp', 'tensor'), pairs))  37.4 us
    pallas_call x4, Pallas kernels, attention_back(): pl.pallas_call(functools.partial(back_kernel, ends=ends), grid_spec=pltpu...  36.6 us
    pallas_call x1, Pallas kernels, attention_forward(): pl.pallas_call(forward_kernel, grid_spec=pltpu.PrefetchScalarGridSpec(num...  23.3 us
    pallas_call x12, Pallas kernels, small_call(): pl.pallas_call(kernel, in_specs=[pl.BlockSpec(memory_space=pltpu.SMEM)] +...  15.3 us
    pallas_call x1, Pallas kernels, norm_one_back(): pl.pallas_call(norm_one_back_kernel, grid_spec=pltpu.PrefetchScalarGridSp...  9.58 us
  transfers between devices with their start and end apart: 28, of which 11 were waited for; matrix products, arithmetic and copies ran while one was open for 0% of the time, Pallas kernels for 34%

profile of v2, /device:TPU:0, one launch (start us, length us, event | category | flops | bytes accessed | tf_op | source)
XLA Modules:
  0.0 225.3 jit_solution(985684631020804780)
XLA Ops:
  0.6 2.3 %pack.1 = (bf16[1040,512]{1,0:T(8,128)(2,1)}, bf16[16,512]{1,0:T(8,128)(2,1)}) custom-call(bf16[512]{0:T(512)(128)(2,1)} %refs_0_.1, bf16[512]{0:T(512)(128)(2,1)} %refs_1_.1, bf16[512]{0:T(512)(128)(2,1)} %refs_2_.1, bf16[512]{0:T(512)(128)(2,1)} %refs_3_.1, bf16[512]{0:T(512)(128)(2,1)} %refs_4_.1, bf16[512]{0:T(512)(128)(2,1)} %refs_5_.1, ...), custom_call_target="tpu_custom_call" | custom-call | tf_op jit(solution)/shard_map/pack/pallas_call | solution.py:546
  3.9 2.0 collective-permute-done.wq_oth.wo_oth.vecs_oth
  7.6 23.3 %attention_forward.1 = (bf16[2048,512]{1,0:T(8,128)(2,1)}, bf16[4,2,3,256,512]{4,3,2,1,0:T(8,128)(2,1)}, bf16[4,8,512,512]{3,2,1,0:T(8,128)(2,1)}, bf16[4,512,51...) custom-call(s32[1]{0:T(128)} %bitcast.tens, s32[8]{0:T(128)S(1)} %copy-done.6, ...), custom_call_target="tpu_custom_call" | custom-call | tf_op jit(solution)/shard_map/attention_forward/pallas_call | solution.py:135
  32.2 42.7 %mlp.1 = (bf16[2048,512]{1,0:T(8,128)(2,1)}, f32[2048,512]{1,0:T(8,128)}, bf16[4,8,80,512]{3,2,1,0:T(8,128)(2,1)}, bf16[9472,128]{1,0:T(8,128)(2,1)}, bf16[9472,128]{1,0:T(8,128)(2,1)}, /*index=5*/f32[8,512]{1,0:T(8,128)}) custom-call(s32[1]{0:T(128)} %bitcast.tens, bf16[2048,512]{1,0:T(8,128)(2,1)} %get-tuple-element.91.n2_ref, bf16[4096,512]{1,0:T(8,128)(2,1)} %cot_ref.1, ...), custom_call_target="tpu_custom_call" | custom-call | tf_op jit(solution)/shard_map/mlp/pallas_call | solution.py:282
  75.4 9.0 %attention_back.4 = (bf16[4,2,3,256,512]{4,3,2,1,0:T(8,128)(2,1)}, f32[2,3,128,512]{3,2,1,0:T(8,128)}) custom-call(s32[1]{0:T(128)} %bitcast.tens, bf16[4,8,512,512]{3,2,1,0:T(8,128)(2,1)} %get-tuple-element.99.p_ref, bf16[4,8,80,512]{3,2,1,0:T(8,128)(2,1)} %get-tuple-element.100.doa_ref, bf16[4,2,3,256,512]{4,3,2,1,0:T(8,128)(2,1)} %get-tuple-element.101.qkv_ref, ...), custom_call_target="tpu_custom_call" | custom-call | tf_op jit(solution)/shard_map/attention_back/pallas_call | solution.py:404
  84.4 3.2 %split_mlp.1 = (f32[4736,128]{1,0:T(8,128)S(1)}, bf16[4736,128]{1,0:T(8,128)(2,1)}) custom-call(s32[2]{0:T(128)S(1)} %pad_add_fusion.3.scalars, bf16[9472,128]{1,0:T(8,128)(2,1)} %get-tuple-element.96.own, bf16[9472,128]{1,0:T(8,128)(2,1)S(1)} %collective-permute-done.3.recv), custom_call_target="tpu_custom_call" | custom-call | tf_op jit(solution)/shard_map/split_mlp/pallas_call | solution.py:502
  89.0 2.6 %collective-permute-start.4 = (bf16[4736,128]{1,0:T(8,128)(2,1)}, bf16[4736,128]{1,0:T(8,128)(2,1)S(1)}, u32[]{:S(2)}, u32[]{:S(2)}) collective-permute-start(bf16[4736,128]{1,0:T(8,128)(2,1)} %get-tuple-element.106), channel_id=1, source_target_pairs={{0,2},{1,5},{2,0},{3,7},{4,6},{5,1},{6,4},{7,3},{8,10},{9,13},{10,... | collective-permute-start | bytes 3637256 | tf_op jit(solution)/shard_map/ppermute | solution.py:497
  91.7 9.5 %attention_back.5 = (bf16[4,2,3,256,512]{4,3,2,1,0:T(8,128)(2,1)}, bf16[3072,128]{1,0:T(8,128)(2,1)}) custom-call(s32[1]{0:T(128)} %bitcast.tens, bf16[4,8,512,512]{3,2,1,0:T(8,128)(2,1)} %get-tuple-element.99.p_ref, bf16[4,8,80,512]{3,2,1,0:T(8,128)(2,1)} %get-tuple-element.100.doa_ref, ...), custom_call_target="tpu_custom_call", output_to_operand_aliasing={{0}: (6, {})} | custom-call | tf_op jit(solution)/shard_map/attention_back/pallas_call | solution.py:404
  101.4 5.0 %collective-permute-done.4.refs_1_ = bf16[4736,128]{1,0:T(8,128)(2,1)S(1)} collective-permute-done((bf16[4736,128]{1,0:T(8,128)(2,1)}, bf16[4736,128]{1,0:T(8,128)(2,1)S(1)}, u32[]{:S(2)}, u32[]{:S(2)}) %collective-permute-start.4) | collective-permute-done | bytes 1212448 | tf_op jit(solution)/shard_map/ppermute | solution.py:497
  106.4 1.8 split.4
  108.2 2.1 collective-permute-start.5
  110.3 9.0 %attention_back.6 = (bf16[4,2,3,256,512]{4,3,2,1,0:T(8,128)(2,1)}, f32[2,3,128,512]{3,2,1,0:T(8,128)}) custom-call(s32[1]{0:T(128)} %bitcast.tens, bf16[4,8,512,512]{3,2,1,0:T(8,128)(2,1)} %get-tuple-element.99.p_ref, bf16[4,8,80,512]{3,2,1,0:T(8,128)(2,1)} %get-tuple-element.100.doa_ref, ...), custom_call_target="tpu_custom_call", output_to_operand_aliasing={{0}: (5, {})} | custom-call | tf_op jit(solution)/shard_map/attention_back/pallas_call | solution.py:404
  120.1 1.6 collective-permute-start.11
  121.8 9.0 %attention_back.7 = (bf16[4,2,3,256,512]{4,3,2,1,0:T(8,128)(2,1)}, f32[3072,128]{1,0:T(8,128)S(1)}) custom-call(s32[1]{0:T(128)} %bitcast.tens, bf16[4,8,512,512]{3,2,1,0:T(8,128)(2,1)} %get-tuple-element.99.p_ref, bf16[4,8,80,512]{3,2,1,0:T(8,128)(2,1)} %get-tuple-element.100.doa_ref, ...), custom_call_target="tpu_custom_call", output_to_operand_aliasing={{0}: (6, {})} | custom-call | tf_op jit(solution)/shard_map/attention_back/pallas_call | solution.py:404
  131.7 1.5 collective-permute-start.7
  133.3 2.6 %collective-permute-start.12 = (bf16[592,128]{1,0:T(8,128)(2,1)S(1)}, bf16[592,128]{1,0:T(8,128)(2,1)S(1)}, u32[]{:S(2)}, u32[]{:S(2)}) collective-permute-start(bf16[592,128]{1,0:T(8,128)(2,1)S(1)} %get-tuple-element.138), channel_id=1, source_target_pairs={{0,16},{1,9},{2,18},{3,11},{4,20},{5,13},{6,22},{7,15},{8,24},{9,1... | collective-permute-start | bytes 454664 | tf_op jit(solution)/shard_map/ppermute | solution.py:497
  138.1 6.8 %collective-permute-done.12.refs_1_ = bf16[592,128]{1,0:T(8,128)(2,1)S(1)} collective-permute-done((bf16[592,128]{1,0:T(8,128)(2,1)S(1)}, bf16[592,128]{1,0:T(8,128)(2,1)S(1)}, u32[]{:S(2)}, u32[]{:S(2)}) %collective-permute-start.12) | collective-permute-done | bytes 151584 | tf_op jit(solution)/shard_map/ppermute | solution.py:497
  145.5 1.9 collective-permute-start.16
  147.4 3.8 %collective-permute-start.15 = (bf16[592,128]{1,0:T(8,128)(2,1)S(1)}, bf16[592,128]{1,0:T(8,128)(2,1)S(1)}, u32[]{:S(2)}, u32[]{:S(2)}) collective-permute-start(bf16[592,128]{1,0:T(8,128)(2,1)S(1)} %settle.1.own), channel_id=1, source_target_pairs={{0,16},{1,9},{2,18},{3,11},{4,20},{5,13},{6,22},{7,15},{8,24},{9,1... | collective-permute-start | bytes 454664 | tf_op jit(solution)/shard_map/ppermute | solution.py:497
  151.3 9.6 %norm_one_back.1 = (f32[2048,512]{1,0:T(8,128)}, f32[8,512]{1,0:T(8,128)}) custom-call(s32[1]{0:T(128)} %bitcast.tens, bf16[4,2,3,256,512]{4,3,2,1,0:T(8,128)(2,1)} %get-tuple-element.123.dqkv, bf16[768,512]{1,0:T(8,128)(2,1)S(1)} %bitcast.29, bf16[1040,512]{1,0:T(8,128)(2,1)S(1)} %copy-done.1, bf16[4096,512]{1,0:T(8,128)(2,1)} %x_ref.3, ...), custom_call_target="tpu_custom_call" | custom-call | tf_op jit(solution)/shard_map/norm_one_back/pallas_call | solution.py:444
  162.2 6.4 %collective-permute-start.17 = (bf16[2368,128]{1,0:T(8,128)(2,1)S(1)}, bf16[2368,128]{1,0:T(8,128)(2,1)S(1)}, u32[]{:S(2)}, u32[]{:S(2)}) collective-permute-start(bf16[2368,128]{1,0:T(8,128)(2,1)S(1)} %join.2.own), channel_id=1, source_target_pairs={{0,4},{1,3},{2,6},{3,1},{4,0},{5,7},{6,2},{7,5},{8,12},{9,11},{10,... | collective-permute-start | bytes 1818632 | tf_op jit(solution)/shard_map/ppermute | solution.py:497
  168.6 14.5 %collective-permute-done.17.refs_0_ = bf16[2368,128]{1,0:T(8,128)(2,1)S(1)} collective-permute-done((bf16[2368,128]{1,0:T(8,128)(2,1)S(1)}, bf16[2368,128]{1,0:T(8,128)(2,1)S(1)}, u32[]{:S(2)}, u32[]{:S(2)}) %collective-permute-start.17) | collective-permute-done | bytes 606240 | tf_op jit(solution)/shard_map/ppermute | solution.py:497
  186.6 2.3 %collective-permute-start.19 = (bf16[192,128]{1,0:T(8,128)(2,1)S(1)}, bf16[192,128]{1,0:T(8,128)(2,1)S(1)}, u32[]{:S(2)}, u32[]{:S(2)}) collective-permute-start(bf16[192,128]{1,0:T(8,128)(2,1)S(1)} %get-tuple-element.150), channel_id=1, source_target_pairs={{0,16},{1,9},{2,18},{3,11},{4,20},{5,13},{6,22},{7,15},{8,24},{9,1... | collective-permute-start | bytes 147464 | tf_op jit(solution)/shard_map/ppermute | solution.py:497
  189.1 11.3 %collective-permute-done.18.refs_1_ = bf16[4736,128]{1,0:T(8,128)(2,1)S(1)} collective-permute-done((bf16[4736,128]{1,0:T(8,128)(2,1)S(1)}, bf16[4736,128]{1,0:T(8,128)(2,1)S(1)}, u32[]{:S(2)}, u32[]{:S(2)}) %collective-permute-start.18) | collective-permute-done | bytes 1212448 | tf_op jit(solution)/shard_map/ppermute | solution.py:497
  200.4 3.2 %finish_mlp.1 = (f32[1024,512]{1,0:T(8,128)}, f32[1024,512]{1,0:T(8,128)}, f32[256,512]{1,0:T(8,128)}, f32[8,128]{1,0:T(8,128)}) custom-call(s32[2]{0:T(128)S(1)} %pad_add_fusion.3.scalars, bf16[4736,128]{1,0:T(8,128)(2,1)S(1)} %join.3.refs_0_, bf16[4736,128]{1,0:T(8,128)(2,1)S(1)} %collective-permute-done.18.refs_1_), custom_call_target="tpu_custom_call" | custom-call | tf_op jit(solution)/shard_map/finish_mlp/pallas_call | solution.py:502
  205.1 2.6 %collective-permute-start.23 = (bf16[240,128]{1,0:T(8,128)(2,1)S(1)}, bf16[240,128]{1,0:T(8,128)(2,1)S(1)}, u32[]{:S(2)}, u32[]{:S(2)}) collective-permute-start(bf16[240,128]{1,0:T(8,128)(2,1)S(1)} %settle_cols.1.refs_0_), channel_id=1, source_target_pairs={{0,16},{1,9},{2,18},{3,11},{4,20},{5,13},{6,22},{7,15},{8,24},{9,1... | collective-permute-start | bytes 184328 | tf_op jit(solution)/shard_map/ppermute | solution.py:497
  208.6 1.7 collective-permute-done.24.refs_3_
  210.3 1.6 collective-permute-done.23.refs_2_
  213.1 1.6 collective-permute-start.27
  216.7 3.3 %collective-permute-done.27.refs_3_ = bf16[816,128]{1,0:T(8,128)(2,1)S(1)} collective-permute-done((bf16[816,128]{1,0:T(8,128)(2,1)S(1)}, bf16[816,128]{1,0:T(8,128)(2,1)S(1)}, u32[]{:S(2)}, u32[]{:S(2)}) %collective-permute-start.27) | collective-permute-done | bytes 208928 | tf_op jit(solution)/shard_map/ppermute | solution.py:497
  220.0 2.1 collective-permute-done.26.refs_2_
  222.8 2.0 finish_qkv.1
  (73 shorter events, 22.4 us)
Async XLA Ops:
  2.9 3.0 %collective-permute-start = (bf16[1040,512]{1,0:T(8,128)(2,1)}, bf16[1040,512]{1,0:T(8,128)(2,1)S(1)}, u32[]{:S(2)}, u32[]{:S(2)}) collective-permute-start(bf16[1040,512]{1,0:T(8,128)(2,1)} %get-tuple-element.90), channel_id=1, source_target_pairs={{0,1},{1,0},{2,3},{3,2},{4,5},{5,4},{6,7},{7,6},{8,9},{9,8},{10,11... | collective-permute-start | bytes 3194888 | tf_op jit(solution)/shard_map/ppermute | solution.py:469
  3.4 27.5 %collective-permute-start.1 = (bf16[1024,512]{1,0:T(8,128)(2,1)}, bf16[1024,512]{1,0:T(8,128)(2,1)S(1)}, u32[]{:S(2)}, u32[]{:S(2)}) collective-permute-start(bf16[1024,512]{1,0:T(8,128)(2,1)} %up_own.1), channel_id=1, source_target_pairs={{0,1},{1,0},{2,3},{3,2},{4,5},{5,4},{6,7},{7,6},{8,9},{9,8},{10,11... | collective-permute-start | bytes 3145736 | tf_op jit(solution)/shard_map/ppermute | solution.py:469
  3.5 27.4 %collective-permute-start.2 = (bf16[1024,512]{1,0:T(8,128)(2,1)}, bf16[1024,512]{1,0:T(8,128)(2,1)S(1)}, u32[]{:S(2)}, u32[]{:S(2)}) collective-permute-start(bf16[1024,512]{1,0:T(8,128)(2,1)} %down_own.1), channel_id=1, source_target_pairs={{0,1},{1,0},{2,3},{3,2},{4,5},{5,4},{6,7},{7,6},{8,9},{9,8},{10,11... | collective-permute-start | bytes 3145736 | tf_op jit(solution)/shard_map/ppermute | solution.py:469
  74.9 9.5 %collective-permute-start.3 = (bf16[9472,128]{1,0:T(8,128)(2,1)}, bf16[9472,128]{1,0:T(8,128)(2,1)S(1)}, u32[]{:S(2)}, u32[]{:S(2)}) collective-permute-start(bf16[9472,128]{1,0:T(8,128)(2,1)} %get-tuple-element.97), channel_id=1, source_target_pairs={{0,1},{1,0},{2,3},{3,2},{4,5},{5,4},{6,7},{7,6},{8,9},{9,8},{10,11... | collective-permute-start | bytes 7274504 | tf_op jit(solution)/shard_map/ppermute | solution.py:469
  89.0 17.4 %collective-permute-start.4 = (bf16[4736,128]{1,0:T(8,128)(2,1)}, bf16[4736,128]{1,0:T(8,128)(2,1)S(1)}, u32[]{:S(2)}, u32[]{:S(2)}) collective-permute-start(bf16[4736,128]{1,0:T(8,128)(2,1)} %get-tuple-element.106), channel_id=1, source_target_pairs={{0,2},{1,5},{2,0},{3,7},{4,6},{5,1},{6,4},{7,3},{8,10},{9,13},{10,... | collective-permute-start | bytes 3637256 | tf_op jit(solution)/shard_map/ppermute | solution.py:497
  101.2 29.7 %collective-permute-start.6 = (bf16[3072,128]{1,0:T(8,128)(2,1)}, bf16[3072,128]{1,0:T(8,128)(2,1)S(1)}, u32[]{:S(2)}, u32[]{:S(2)}) collective-permute-start(bf16[3072,128]{1,0:T(8,128)(2,1)} %get-tuple-element.109), channel_id=1, source_target_pairs={{0,1},{1,0},{2,3},{3,2},{4,5},{5,4},{6,7},{7,6},{8,9},{9,8},{10,11... | collective-permute-start | bytes 2359304 | tf_op jit(solution)/shard_map/ppermute | solution.py:469
  108.2 11.2 %collective-permute-start.5 = (bf16[2368,128]{1,0:T(8,128)(2,1)}, bf16[2368,128]{1,0:T(8,128)(2,1)S(1)}, u32[]{:S(2)}, u32[]{:S(2)}) collective-permute-start(bf16[2368,128]{1,0:T(8,128)(2,1)} %get-tuple-element.112), channel_id=1, source_target_pairs={{0,4},{1,3},{2,6},{3,1},{4,0},{5,7},{6,2},{7,5},{8,12},{9,11},{10,... | collective-permute-start | bytes 1818632 | tf_op jit(solution)/shard_map/ppermute | solution.py:497
  120.1 17.1 %collective-permute-start.11 = (bf16[592,128]{1,0:T(8,128)(2,1)S(1)}, bf16[592,128]{1,0:T(8,128)(2,1)S(1)}, u32[]{:S(2)}, u32[]{:S(2)}) collective-permute-start(bf16[592,128]{1,0:T(8,128)(2,1)S(1)} %get-tuple-element.136), channel_id=1, source_target_pairs={{0,8},{1,17},{2,10},{3,19},{4,12},{5,21},{6,14},{7,23},{8,0},{9,25... | collective-permute-start | bytes 454664 | tf_op jit(solution)/shard_map/ppermute | solution.py:497
  130.9 20.4 %copy-start.1 = (bf16[1040,512]{1,0:T(8,128)(2,1)S(1)}, bf16[1040,512]{1,0:T(8,128)(2,1)}, u32[]{:S(2)}) copy-start(bf16[1040,512]{1,0:T(8,128)(2,1)} %copy-done) | copy-start | bytes 3194884
  130.9 20.4 %copy-start.2 = (bf16[3,256,512]{2,1,0:T(8,128)(2,1)S(1)}, bf16[3,256,512]{2,1,0:T(8,128)(2,1)}, u32[]{:S(2)}) copy-start(bf16[3,256,512]{2,1,0:T(8,128)(2,1)} %param.18) | copy-start | bytes 2359300
  130.9 20.4 %copy-start.5 = (bf16[16,512]{1,0:T(8,128)(2,1)S(1)}, bf16[16,512]{1,0:T(8,128)(2,1)}, u32[]{:S(2)}) copy-start(bf16[16,512]{1,0:T(8,128)(2,1)} %get-tuple-element.89.vecs) | copy-start | bytes 49156
  131.7 19.5 %collective-permute-start.7 = (bf16[768,128]{1,0:T(8,128)(2,1)S(1)}, bf16[768,128]{1,0:T(8,128)(2,1)S(1)}, u32[]{:S(2)}, u32[]{:S(2)}) collective-permute-start(bf16[768,128]{1,0:T(8,128)(2,1)S(1)} %get-tuple-element.127), channel_id=1, source_target_pairs={{0,2},{1,5},{2,0},{3,7},{4,6},{5,1},{6,4},{7,3},{8,10},{9,13},{10,... | collective-permute-start | bytes 589832 | tf_op jit(solution)/shard_map/ppermute | solution.py:497
  133.3 11.6 %collective-permute-start.12 = (bf16[592,128]{1,0:T(8,128)(2,1)S(1)}, bf16[592,128]{1,0:T(8,128)(2,1)S(1)}, u32[]{:S(2)}, u32[]{:S(2)}) collective-permute-start(bf16[592,128]{1,0:T(8,128)(2,1)S(1)} %get-tuple-element.138), channel_id=1, source_target_pairs={{0,16},{1,9},{2,18},{3,11},{4,20},{5,13},{6,22},{7,15},{8,24},{9,1... | collective-permute-start | bytes 454664 | tf_op jit(solution)/shard_map/ppermute | solution.py:497
  135.9 9.0 %collective-permute-start.13 = (bf16[592,128]{1,0:T(8,128)(2,1)S(1)}, bf16[592,128]{1,0:T(8,128)(2,1)S(1)}, u32[]{:S(2)}, u32[]{:S(2)}) collective-permute-start(bf16[592,128]{1,0:T(8,128)(2,1)S(1)} %get-tuple-element.117), channel_id=1, source_target_pairs={{0,24},{1,25},{2,26},{3,27},{4,28},{5,29},{6,30},{7,31},{8,16},{9,... | collective-permute-start | bytes 454664 | tf_op jit(solution)/shard_map/ppermute | solution.py:497
  136.1 24.8 %collective-permute-start.8 = (bf16[768,128]{1,0:T(8,128)(2,1)S(1)}, bf16[768,128]{1,0:T(8,128)(2,1)S(1)}, u32[]{:S(2)}, u32[]{:S(2)}) collective-permute-start(bf16[768,128]{1,0:T(8,128)(2,1)S(1)} %get-tuple-element.130), channel_id=1, source_target_pairs={{0,4},{1,3},{2,6},{3,1},{4,0},{5,7},{6,2},{7,5},{8,12},{9,11},{10,... | collective-permute-start | bytes 589832 | tf_op jit(solution)/shard_map/ppermute | solution.py:497
  137.3 23.6 %collective-permute-start.9 = (bf16[768,128]{1,0:T(8,128)(2,1)S(1)}, bf16[768,128]{1,0:T(8,128)(2,1)S(1)}, u32[]{:S(2)}, u32[]{:S(2)}) collective-permute-start(bf16[768,128]{1,0:T(8,128)(2,1)S(1)} %get-tuple-element.121), channel_id=1, source_target_pairs={{0,6},{1,7},{2,4},{3,5},{4,2},{5,3},{6,0},{7,1},{8,14},{9,15},{10,... | collective-permute-start | bytes 589832 | tf_op jit(solution)/shard_map/ppermute | solution.py:497
  145.5 16.1 %collective-permute-start.16 = (bf16[592,128]{1,0:T(8,128)(2,1)S(1)}, bf16[592,128]{1,0:T(8,128)(2,1)S(1)}, u32[]{:S(2)}, u32[]{:S(2)}) collective-permute-start(bf16[592,128]{1,0:T(8,128)(2,1)S(1)} %settle.1.own), channel_id=1, source_target_pairs={{0,24},{1,25},{2,26},{3,27},{4,28},{5,29},{6,30},{7,31},{8,16},{9,... | collective-permute-start | bytes 454664 | tf_op jit(solution)/shard_map/ppermute | solution.py:497
  147.4 14.2 %collective-permute-start.15 = (bf16[592,128]{1,0:T(8,128)(2,1)S(1)}, bf16[592,128]{1,0:T(8,128)(2,1)S(1)}, u32[]{:S(2)}, u32[]{:S(2)}) collective-permute-start(bf16[592,128]{1,0:T(8,128)(2,1)S(1)} %settle.1.own), channel_id=1, source_target_pairs={{0,16},{1,9},{2,18},{3,11},{4,20},{5,13},{6,22},{7,15},{8,24},{9,1... | collective-permute-start | bytes 454664 | tf_op jit(solution)/shard_map/ppermute | solution.py:497
  151.3 10.3 %collective-permute-start.14 = (bf16[592,128]{1,0:T(8,128)(2,1)S(1)}, bf16[592,128]{1,0:T(8,128)(2,1)S(1)}, u32[]{:S(2)}, u32[]{:S(2)}) collective-permute-start(bf16[592,128]{1,0:T(8,128)(2,1)S(1)} %settle.1.own), channel_id=1, source_target_pairs={{0,8},{1,17},{2,10},{3,19},{4,12},{5,21},{6,14},{7,23},{8,0},{9,25... | collective-permute-start | bytes 454664 | tf_op jit(solution)/shard_map/ppermute | solution.py:497
  160.9 23.0 %copy-start.9 = (f32[8,512]{1,0:T(8,128)S(1)}, f32[8,512]{1,0:T(8,128)}, u32[]{:S(2)}) copy-start(f32[8,512]{1,0:T(8,128)} %get-tuple-element.153) | copy-start | bytes 49156
  162.2 20.9 %collective-permute-start.17 = (bf16[2368,128]{1,0:T(8,128)(2,1)S(1)}, bf16[2368,128]{1,0:T(8,128)(2,1)S(1)}, u32[]{:S(2)}, u32[]{:S(2)}) collective-permute-start(bf16[2368,128]{1,0:T(8,128)(2,1)S(1)} %join.2.own), channel_id=1, source_target_pairs={{0,4},{1,3},{2,6},{3,1},{4,0},{5,7},{6,2},{7,5},{8,12},{9,11},{10,... | collective-permute-start | bytes 1818632 | tf_op jit(solution)/shard_map/ppermute | solution.py:497
  183.8 16.6 %collective-permute-start.18 = (bf16[4736,128]{1,0:T(8,128)(2,1)S(1)}, bf16[4736,128]{1,0:T(8,128)(2,1)S(1)}, u32[]{:S(2)}, u32[]{:S(2)}) collective-permute-start(bf16[4736,128]{1,0:T(8,128)(2,1)S(1)} %join.3.refs_0_), channel_id=1, source_target_pairs={{0,2},{1,5},{2,0},{3,7},{4,6},{5,1},{6,4},{7,3},{8,10},{9,13},{10,... | collective-permute-start | bytes 3637256 | tf_op jit(solution)/shard_map/ppermute | solution.py:497
  184.6 19.0 %collective-permute-start.20 = (bf16[192,128]{1,0:T(8,128)(2,1)S(1)}, bf16[192,128]{1,0:T(8,128)(2,1)S(1)}, u32[]{:S(2)}, u32[]{:S(2)}) collective-permute-start(bf16[192,128]{1,0:T(8,128)(2,1)S(1)} %get-tuple-element.141), channel_id=1, source_target_pairs={{0,24},{1,25},{2,26},{3,27},{4,28},{5,29},{6,30},{7,31},{8,16},{9,... | collective-permute-start | bytes 147464 | tf_op jit(solution)/shard_map/ppermute | solution.py:497
  185.5 18.1 %collective-permute-start.10 = (bf16[192,128]{1,0:T(8,128)(2,1)S(1)}, bf16[192,128]{1,0:T(8,128)(2,1)S(1)}, u32[]{:S(2)}, u32[]{:S(2)}) collective-permute-start(bf16[192,128]{1,0:T(8,128)(2,1)S(1)} %get-tuple-element.134), channel_id=1, source_target_pairs={{0,8},{1,17},{2,10},{3,19},{4,12},{5,21},{6,14},{7,23},{8,0},{9,25... | collective-permute-start | bytes 147464 | tf_op jit(solution)/shard_map/ppermute | solution.py:497
  186.6 16.9 %collective-permute-start.19 = (bf16[192,128]{1,0:T(8,128)(2,1)S(1)}, bf16[192,128]{1,0:T(8,128)(2,1)S(1)}, u32[]{:S(2)}, u32[]{:S(2)}) collective-permute-start(bf16[192,128]{1,0:T(8,128)(2,1)S(1)} %get-tuple-element.150), channel_id=1, source_target_pairs={{0,16},{1,9},{2,18},{3,11},{4,20},{5,13},{6,22},{7,15},{8,24},{9,1... | collective-permute-start | bytes 147464 | tf_op jit(solution)/shard_map/ppermute | solution.py:497
  189.0 14.6 %collective-permute-start.21 = (f32[24,128]{1,0:T(8,128)S(1)}, f32[24,128]{1,0:T(8,128)S(1)}, u32[]{:S(2)}, u32[]{:S(2)}) collective-permute-start(f32[24,128]{1,0:T(8,128)S(1)} %reshape.55.refs_3_), channel_id=1, source_target_pairs={{0,1},{1,0},{2,3},{3,2},{4,5},{5,4},{6,7},{7,6},{8,9},{9,8},{10,11... | collective-permute-start | bytes 36872 | tf_op jit(solution)/shard_map/ppermute | solution.py:469
  204.2 6.2 %collective-permute-start.24 = (bf16[240,128]{1,0:T(8,128)(2,1)S(1)}, bf16[240,128]{1,0:T(8,128)(2,1)S(1)}, u32[]{:S(2)}, u32[]{:S(2)}) collective-permute-start(bf16[240,128]{1,0:T(8,128)(2,1)S(1)} %settle_cols.1.refs_0_), channel_id=1, source_target_pairs={{0,24},{1,25},{2,26},{3,27},{4,28},{5,29},{6,30},{7,31},{8,16},{9,... | collective-permute-start | bytes 184328 | tf_op jit(solution)/shard_map/ppermute | solution.py:497
  205.1 6.8 %collective-permute-start.23 = (bf16[240,128]{1,0:T(8,128)(2,1)S(1)}, bf16[240,128]{1,0:T(8,128)(2,1)S(1)}, u32[]{:S(2)}, u32[]{:S(2)}) collective-permute-start(bf16[240,128]{1,0:T(8,128)(2,1)S(1)} %settle_cols.1.refs_0_), channel_id=1, source_target_pairs={{0,16},{1,9},{2,18},{3,11},{4,20},{5,13},{6,22},{7,15},{8,24},{9,1... | collective-permute-start | bytes 184328 | tf_op jit(solution)/shard_map/ppermute | solution.py:497
  207.7 4.8 %collective-permute-start.22 = (bf16[240,128]{1,0:T(8,128)(2,1)S(1)}, bf16[240,128]{1,0:T(8,128)(2,1)S(1)}, u32[]{:S(2)}, u32[]{:S(2)}) collective-permute-start(bf16[240,128]{1,0:T(8,128)(2,1)S(1)} %settle_cols.1.refs_0_), channel_id=1, source_target_pairs={{0,8},{1,17},{2,10},{3,19},{4,12},{5,21},{6,14},{7,23},{8,0},{9,25... | collective-permute-start | bytes 184328 | tf_op jit(solution)/shard_map/ppermute | solution.py:497
  213.1 6.9 %collective-permute-start.27 = (bf16[816,128]{1,0:T(8,128)(2,1)S(1)}, bf16[816,128]{1,0:T(8,128)(2,1)S(1)}, u32[]{:S(2)}, u32[]{:S(2)}) collective-permute-start(bf16[816,128]{1,0:T(8,128)(2,1)S(1)} %join_cols.1.refs_0_), channel_id=1, source_target_pairs={{0,6},{1,7},{2,4},{3,5},{4,2},{5,3},{6,0},{7,1},{8,14},{9,15},{10,... | collective-permute-start | bytes 626696 | tf_op jit(solution)/shard_map/ppermute | solution.py:497
  214.7 7.4 %collective-permute-start.26 = (bf16[816,128]{1,0:T(8,128)(2,1)S(1)}, bf16[816,128]{1,0:T(8,128)(2,1)S(1)}, u32[]{:S(2)}, u32[]{:S(2)}) collective-permute-start(bf16[816,128]{1,0:T(8,128)(2,1)S(1)} %join_cols.1.refs_0_), channel_id=1, source_target_pairs={{0,4},{1,3},{2,6},{3,1},{4,0},{5,7},{6,2},{7,5},{8,12},{9,11},{10,... | collective-permute-start | bytes 626696 | tf_op jit(solution)/shard_map/ppermute | solution.py:497
  215.3 7.4 %collective-permute-start.25 = (bf16[816,128]{1,0:T(8,128)(2,1)S(1)}, bf16[816,128]{1,0:T(8,128)(2,1)S(1)}, u32[]{:S(2)}, u32[]{:S(2)}) collective-permute-start(bf16[816,128]{1,0:T(8,128)(2,1)S(1)} %join_cols.1.refs_0_), channel_id=1, source_target_pairs={{0,2},{1,5},{2,0},{3,7},{4,6},{5,1},{6,4},{7,3},{8,10},{9,13},{10,... | collective-permute-start | bytes 626696 | tf_op jit(solution)/shard_map/ppermute | solution.py:497
  (6 other events, 20.1 us)

commit v3 on v2

--- a/solution.py
+++ b/solution.py
@@ -17,8 +17,9 @@
 F32 = jnp.float32
 MIB = 2**20
 SWAP = [(0, 1), (1, 0)]
-GO_ON = (1, 2, 3)
-BACK_SCENES = 2
+PLAN = (
+("back", 1, 0, 1), ("mlp",), ("back", 1, 1, 3), ("mlp+",), ("back", 0, 0, 1), ("mlp+",), ("back", 0, 1, 3), ("mlp+",), ("qkv",), ("norm",), ("qkv+",), ("mlp+",), ("qkv+",), ("mlp+",), ("qkv+",), ("out",), ("end",), ("qkv+",),
+)
 
 
 def _dot(a, b, ca, cb):
@@ -114,6 +115,10 @@
 def whole(shape, row=0):
     at = (row,) + (0,) * (len(shape) - 1)
     return pl.BlockSpec(shape, lambda i, *_: at, pipeline_mode=pl.Buffered(1))
+
+
+def takes(microseconds):
+    return pl.CostEstimate(flops=int(microseconds * 1e9), bytes_accessed=0, transcendentals=0)
 
 
 def params(mib):
@@ -161,8 +166,9 @@
             pltpu.HBM((rows, D), BF),
         ],
         compiler_params=params(40),
+        cost_estimate=takes(23),
         name="attention_forward",
-    )(tens, lens, *hbm(x, vecs, wq_own, theirs, wo_own, theirs))
+    )(tens, *hbm(lens, x, vecs, wq_own), theirs, *hbm(wo_own), theirs)
 
 
 LOG2E = 1.4426950408889634
@@ -188,7 +194,7 @@
 
 def mlp_kernel(
     tens, n2_ref, cot_ref, up_own, down_own, up_oth, down_oth, vecs_oth, vecs, h1_ref, att_ref, rl_ref, wo_own, wo_oth,
-    block_ref, gh_ref, doa_ref, own_ref, oth_ref, cols_ref, acc_up, acc_down, acc_ub, acc_wo,
+    act_ref, gh_ref, doa_ref, own_ref, oth_ref, cols_ref, acc_up, acc_down, acc_ub, acc_wo,
 ):
     @pl.when(pl.program_id(0) == 0)
     def _():
@@ -218,26 +224,24 @@
         return act.astype(BF), (grad_act * slope).astype(BF)
 
     def after(j, act, dpre):
-        u, d, _ = place(j)
+        u, _, _ = place(j)
         at = slice(j * SUB, j * SUB + SUB)
+        act_ref[:, at] = act
         acc_down[at] += tn(act, cot)
         acc_up[at] += tn(dpre, n2)
         acc_ub[:, at] += jnp.sum(dpre.astype(F32), 0, keepdims=True)
-        return nn(act, d), nn(dpre, u)
-
-    out, back = 0.0, 0.0
+        return nn(dpre, u)
+
+    back = 0.0
     first, second = [], []
     for j in range(2 * per + 2):
         if j < 2 * per:
             first.append(before(j))
         if j >= 2:
-            o, b = after(j - 2, *second.pop(0))
-            out, back = out + o, back + b
+            back += after(j - 2, *second.pop(0))
         if 1 <= j <= 2 * per:
             second.append(between(*first.pop(0)))
-    h1 = h1_ref[...]
-    block_ref[...] = (h1 + out + vec(vecs, 5)).astype(BF)
-    xh, r = normalised(h1)
+    xh, r = normalised(h1_ref[...])
     cot32 = cot.astype(F32)
     gh = cot32 + norm_back(back * vec(vecs, 3), xh, r)
     gh_ref[...] = gh
@@ -293,7 +297,7 @@
                 whole((half, D)), whole((half, D), 3),
             ],
             out_specs=[
-                rowblock, rowblock,
+                pl.BlockSpec((LAT, 2 * units), lambda i, *_: (i, 0)), rowblock,
                 pl.BlockSpec((1, heads, HD + AUG, LAT), lambda i, *_: (i, 0, 0, 0)),
                 whole((total_rows, 128)), whole((total_rows, 128)), whole((8, D)),
             ],
@@ -303,7 +307,7 @@
             ],
         ),
         out_shape=[
-            pltpu.HBM((rows, D), BF),
+            pltpu.HBM((rows, 2 * units), BF),
             pltpu.HBM((rows, D), F32),
             pltpu.HBM((scenes, heads, HD + AUG, LAT), BF),
             pltpu.HBM((total_rows, 128), BF),
@@ -311,8 +315,36 @@
             pltpu.HBM((8, D), F32),
         ],
         compiler_params=params(56),
+        cost_estimate=takes(39),
         name="mlp",
     )(tens, *hbm(n2, cot, up, down, up_oth, down_oth, theirs, vecs, h1, att, rl, wo, theirs))
+
+
+def block_out_kernel(tens, act_ref, down_own, down_oth, vecs, h1_ref, out_ref):
+    units = down_own.shape[0]
+    term = nn(act_ref[:, :units], down_own[...]) + nn(act_ref[:, units:], down_oth[...])
+    out_ref[...] = (h1_ref[...] + term + vec(vecs, 5)).astype(BF)
+
+
+def block_out(tens, act, down, down_oth, vecs, h1):
+    rows = h1.shape[0]
+    units = down.shape[0]
+    rowblock = pl.BlockSpec((LAT, D), lambda i, *_: (i, 0))
+    return pl.pallas_call(
+        block_out_kernel,
+        grid_spec=pltpu.PrefetchScalarGridSpec(
+            num_scalar_prefetch=1,
+            grid=(rows // LAT,),
+            in_specs=[
+                pl.BlockSpec((LAT, 2 * units), lambda i, *_: (i, 0)), whole((units, D)), whole((units, D)), vecs_spec(), rowblock,
+            ],
+            out_specs=[rowblock],
+        ),
+        out_shape=[pltpu.HBM((rows, D), BF)],
+        compiler_params=params(24),
+        cost_estimate=takes(7),
+        name="block_out",
+    )(tens, *hbm(act, down, down_oth, vecs, h1))[0]
 
 
 def back_kernel(tens, p_ref, doa_ref, qkv_ref, n1_ref, *refs, ends):
@@ -418,27 +450,34 @@
         out_shape=[pltpu.HBM(qkv.shape, BF), dw],
         input_output_aliases=aliases,
         compiler_params=pltpu.CompilerParams(vmem_limit_bytes=24 * MIB, dimension_semantics=("arbitrary", "arbitrary")),
+        cost_estimate=takes(4.5 * count),
         name="attention_back",
     )(tens, *hbm(p, doa, qkv, n1, *carried))
 
 
-def norm_one_back_kernel(tens, dqkv, wq_own, wq_oth, x_ref, vecs, gh_ref, gl_ref, cols_ref):
+def norm_one_back_kernel(tens, dqkv, wq_own, wq_oth, x_ref, vecs, gh_ref, cols_two, gl_ref, cols_ref, acc):
     feats = wq_own.shape[0]
     g = tn(dqkv[0, 0].reshape(feats, LAT), wq_own[...]) + tn(dqkv[0, 1].reshape(feats, LAT), wq_oth[...])
     xh, r = normalised(x_ref[...].astype(F32))
     gl_ref[...] = gh_ref[...] + norm_back(g * vec(vecs, 0), xh, r)
-    sums = jnp.concatenate([jnp.sum(v, 0, keepdims=True) for v in (g * xh, g)] + [jnp.zeros((6, D), F32)], 0)
+    sums = jnp.concatenate([jnp.sum(v, 0, keepdims=True) for v in (g * xh, g)] + [cols_two[:4], cols_two[6:]], 0)
 
     @pl.when(pl.program_id(0) == 0)
     def _():
-        cols_ref[...] = sums
+        acc[...] = sums
 
     @pl.when(pl.program_id(0) > 0)
     def _():
-        cols_ref[...] += sums
-
-
-def norm_one_back(tens, dqkv, wq_own, theirs, x, vecs, gh):
+        acc[:2] += sums[:2]
+
+    @pl.when(pl.program_id(0) == pl.num_programs(0) - 1)
+    def _():
+        total = acc[...]
+        for c in range(D // 128):
+            cols_ref[c * 8:c * 8 + 8] = total[:, c * 128:c * 128 + 128]
+
+
+def norm_one_back(tens, dqkv, wq_own, theirs, x, vecs, gh, cols_two):
     scenes, half = dqkv.shape[0], dqkv.shape[3]
     rowblock = pl.BlockSpec((LAT, D), lambda i, *_: (i, 0))
     return pl.pallas_call(
@@ -452,13 +491,16 @@
                 pl.BlockSpec((LAT, D), lambda i, tens: (tens[0] * scenes + i, 0)),
                 vecs_spec(),
                 rowblock,
+                whole((8, D)),
             ],
-            out_specs=[rowblock, whole((8, D))],
+            out_specs=[rowblock, whole((32, 128))],
+            scratch_shapes=[pltpu.VMEM((8, D), F32)],
         ),
-        out_shape=[pltpu.HBM((scenes * LAT, D), F32), pltpu.HBM((8, D), F32)],
+        out_shape=[pltpu.HBM((scenes * LAT, D), F32), jax.ShapeDtypeStruct((32, 128), F32)],
         compiler_params=params(28),
+        cost_estimate=takes(10),
         name="norm_one_back",
-    )(tens, *hbm(dqkv), wq_own, theirs, *hbm(x), vecs, *hbm(gh))
+    )(tens, *hbm(dqkv, wq_own, theirs, x, vecs, gh, cols_two))
 
 
 def tie(value, *after):
@@ -774,7 +816,7 @@
     )
     need = 8 * units + 4 * half + 16
     total_rows = -(-need // (16 * count)) * 16 * count
-    block_out, gh, doa, grads_own, grads_oth, cols_two = mlp(
+    act, gh, doa, grads_own, grads_oth, cols_two = mlp(
         tens, n2, cotangent, up_weight, down_weight, up_oth, down_oth, theirs, vecs, h1, att, rl, out_weight, total_rows
     )
     from_peer = swap(grads_oth)
@@ -796,46 +838,63 @@
                 have = joined(have, recvs, stages[s])
         return have, recvs
 
-    scenes = rows // LAT
     qkv_rows = -(-12 * half // (16 * count)) * 16 * count
-    dqkv, dw = None, None
+    extra = 64
+    dqkv, dw, qkv_peer = None, None, None
     token = grads_oth
-    mlp_steps, mlp_result = None, None
-    calls = 0
-    for side in (1, 0):
-        for scene in range(0, scenes, BACK_SCENES):
-            dqkv, dw = attention_back(tie(tens, token), p, doa, qkv, n1, dqkv, dw, side, scene, BACK_SCENES, qkv_rows)
+    chains, results = {}, {}
+    cols = []
+
+    def step(name):
+        if name not in results:
+            after, result = advance(chains[name], token)
+            if result is not None:
+                results[name] = result
+            return after
+        return token
+
+    for action, *rest in PLAN:
+        if action == "back":
+            side, first, number = rest
+            dqkv, dw = attention_back(tie(tens, token), p, doa, qkv, n1, dqkv, dw, side, first, number, qkv_rows)
             token = dw
-            if calls == 0:
-                mlp_steps = exchanges(mlp_stages, *split_mlp(grads_own, tie(from_peer, token), mlp_stages[0]), settle, join)
-                token = next(mlp_steps)
-            elif calls in GO_ON and mlp_result is None:
-                token, mlp_result = advance(mlp_steps, token)
-            calls += 1
-        if side:
-            qkv_peer = swap(dw)
-    keep, sends = split(dw, [qkv_peer], qkv_stages[0])
-    cols = []
-    extra = 48
-    qkv_steps = exchanges(
-        qkv_stages, keep, sends, lambda keep, recvs, stage: settle_cols(keep, recvs, *cols, stage),
-        lambda own, recvs, stage: join_cols(own, recvs, stage, extra),
-    )
-    token = next(qkv_steps)
-    grad_latents, cols_one = norm_one_back(tie(tens, token), dqkv, qkv_weight.reshape(3 * half, D), theirs, latents, vecs, gh)
-    cols.append(jnp.concatenate([cols_one[:2], cols_two[:4]], 0).reshape(24, 128))
-    cols.append(swap(cols[0]))
-    token, qkv_result = advance(qkv_steps, cols_one)
-    while mlp_result is None:
-        token, mlp_result = advance(mlp_steps, token)
-    dup, ddown, dwo, dub = finish_mlp(tie(mlp_result[0], token), *mlp_result[1:], mlp_stages[0], units, half)
-    token = dub
-    while qkv_result is None:
-        token, qkv_result = advance(qkv_steps, token)
-    dwq, shared = finish_qkv(*qkv_result, qkv_stages[0], half, extra)
-    shared = shared.reshape(6, D)
+            if side and first + number == rows // LAT:
+                qkv_peer = swap(dw)
+        elif action == "mlp":
+            chains["mlp"] = exchanges(
+                mlp_stages, *split_mlp(grads_own, tie(from_peer, token), mlp_stages[0]), settle, join
+            )
+            token = next(chains["mlp"])
+        elif action == "qkv":
+            chains["qkv"] = exchanges(
+                qkv_stages, *split(tie(dw, token), [qkv_peer], qkv_stages[0]),
+                lambda keep, recvs, stage: settle_cols(keep, recvs, *cols, stage),
+                lambda own, recvs, stage: join_cols(own, recvs, stage, extra),
+            )
+            token = next(chains["qkv"])
+        elif action == "norm":
+            grad_latents, cols_one = norm_one_back(
+                tie(tens, token), dqkv, qkv_weight.reshape(3 * half, D), theirs, latents, vecs, gh, cols_two
+            )
+            cols.extend((cols_one, swap(cols_one)))
+            token = cols_one
+        elif action == "out":
+            out = block_out(tie(tens, token), act, down_weight, down_oth, vecs, h1)
+            token = out
+        elif action == "end":
+            while "mlp" not in results:
+                token = step("mlp")
+            have, recvs = results["mlp"]
+            dup, ddown, dwo, dub = finish_mlp(tie(have, token), recvs, mlp_stages[0], units, half)
+            token = dub
+        else:
+            token = step(action[:3])
+    while "qkv" not in results:
+        token = step("qkv")
+    dwq, shared = finish_qkv(*results["qkv"], qkv_stages[0], half, extra)
+    shared = shared.reshape(D // 128, 8, 128).transpose(1, 0, 2).reshape(8, D)
     return (
-        block_out, grad_latents, shared[0], shared[1], dwq, dwo, shared[4],
+        out, grad_latents, shared[0], shared[1], dwq, dwo, shared[4],
         shared[2], shared[3], dup, dub.reshape(units), ddown, shared[5],
     )
 

time: 226 us -> 187 us (0.83)
  waiting for transfers between devices: 49.6 us -> 15 us
  starting transfers between devices: 39 us -> 34.6 us
  Pallas kernels: 130 us -> 134 us
  local copies, waits for them, and re-layouts: 5.69 us -> 1.92 us
    ppermute x22, waiting for transfers between devices: 47.6 us -> 13 us  [exchange(): out.append(lax.ppermute(v, ('dp', 'tensor'), pairs))]
    pallas_call x0 -> x1, Pallas kernels: none -> 9.32 us  [block_out(): pl.pallas_call(block_out_kernel, grid_spec=pltpu.PrefetchScalarGridSpec(n...]
    ppermute x22, starting transfers between devices: 37.4 us -> 33.2 us  [exchange(): out.append(lax.ppermute(v, ('dp', 'tensor'), pairs))]
    pallas_call x1, Pallas kernels: 42.7 us -> 39 us  [mlp(): pl.pallas_call(mlp_kernel, grid_spec=pltpu.PrefetchScalarGridSpec(num_sca...]
    unnamed x20 -> x6, local copies, waits for them, and re-layouts: 4.36 us -> 1.31 us
  transfers between devices with their start and end apart: 28 -> 28, of which waited for: 11 -> 9; matrix products, arithmetic and copies ran while one was open for 0% -> 0% of each run, Pallas kernels for 34% -> 46%
where the time goes in v3:
time: 187 us
  Pallas kernels  134 us (72%)
  starting transfers between devices  34.6 us (19%)
  waiting for transfers between devices  15 us (8%)
  local copies, waits for them, and re-layouts  1.92 us (1%)
    pallas_call x1, Pallas kernels, mlp(): pl.pallas_call(mlp_kernel, grid_spec=pltpu.PrefetchScalarGridSpec(num_sca...  39 us
    pallas_call x4, Pallas kernels, attention_back(): pl.pallas_call(functools.partial(back_kernel, ends=ends), grid_spec=pltpu...  36.4 us
    ppermute x22, starting transfers between devices, exchange(): out.append(lax.ppermute(v, ('dp', 'tensor'), pairs))  33.2 us
    pallas_call x1, Pallas kernels, attention_forward(): pl.pallas_call(forward_kernel, grid_spec=pltpu.PrefetchScalarGridSpec(num...  23.1 us
    pallas_call x12, Pallas kernels, small_call(): pl.pallas_call(kernel, in_specs=[pl.BlockSpec(memory_space=pltpu.SMEM)] +...  13.5 us
    ppermute x22, waiting for transfers between devices, exchange(): out.append(lax.ppermute(v, ('dp', 'tensor'), pairs))  13 us
    pallas_call x1, Pallas kernels, norm_one_back(): pl.pallas_call(norm_one_back_kernel, grid_spec=pltpu.PrefetchScalarGridSp...  10.2 us
    pallas_call x1, Pallas kernels, block_out(): pl.pallas_call(block_out_kernel, grid_spec=pltpu.PrefetchScalarGridSpec(n...  9.32 us
  transfers between devices with their start and end apart: 28, of which 9 were waited for; matrix products, arithmetic and copies ran while one was open for 0% of the time, Pallas kernels for 46%

profile of v3, /device:TPU:0, one launch (start us, length us, event | category | flops | bytes accessed | tf_op | source)
XLA Modules:
  0.0 186.5 jit_solution(1983112194999904679)
XLA Ops:
  0.6 2.3 %pack.1 = (bf16[1040,512]{1,0:T(8,128)(2,1)}, bf16[16,512]{1,0:T(8,128)(2,1)}) custom-call(bf16[512]{0:T(512)(128)(2,1)} %refs_0_.1, bf16[512]{0:T(512)(128)(2,1)} %refs_1_.1, bf16[512]{0:T(512)(128)(2,1)} %refs_2_.1, bf16[512]{0:T(512)(128)(2,1)} %refs_3_.1, bf16[512]{0:T(512)(128)(2,1)} %refs_4_.1, bf16[512]{0:T(512)(128)(2,1)} %refs_5_.1, ...), custom_call_target="tpu_custom_call" | custom-call | tf_op jit(solution)/shard_map/pack/pallas_call | solution.py:588
  3.9 2.0 %collective-permute-done.wq_oth.wo_oth.vecs_oth = bf16[1040,512]{1,0:T(8,128)(2,1)S(1)} collective-permute-done((bf16[1040,512]{1,0:T(8,128)(2,1)}, bf16[1040,512]{1,0:T(8,128)(2,1)S(1)}, u32[]{:S(2)}, u32[]{:S(2)}) %collective-permute-start) | collective-permute-done | bytes 1064992 | tf_op jit(solution)/shard_map/ppermute | solution.py:511
  6.0 23.1 %attention_forward.1 = (bf16[2048,512]{1,0:T(8,128)(2,1)}, bf16[4,2,3,256,512]{4,3,2,1,0:T(8,128)(2,1)}, bf16[4,8,512,512]{3,2,1,0:T(8,128)(2,1)}, bf16[4,512,51...) custom-call(s32[1]{0:T(128)} %bitcast.tens, s32[8]{0:T(128)} %lens.1, ...), custom_call_target="tpu_custom_call" | custom-call | flops 23000000512 | tf_op jit(solution)/shard_map/attention_forward/pallas_call | solution.py:140
  30.4 39.0 %mlp.1 = (bf16[2048,2048]{1,0:T(8,128)(2,1)}, f32[2048,512]{1,0:T(8,128)}, bf16[4,8,80,512]{3,2,1,0:T(8,128)(2,1)}, bf16[9472,128]{1,0:T(8,128)(2,1)}, bf16[9472,128]{1,0:T(8,128)(2,1)}, /*index=5*/f32[8,512]{1,0:T(8,128)}) custom-call(s32[1]{0:T(128)} %bitcast.tens, bf16[2048,512]{1,0:T(8,128)(2,1)} %get-tuple-element.93.n2_ref, bf16[4096,512]{1,0:T(8,128)(2,1)} %cot_ref.1, ...), custom_call_target="tpu_custom_call" | custom-call | flops 38999998464 | tf_op jit(solution)/shard_map/mlp/pallas_call | solution.py:286
  70.1 5.9 %attention_back.4 = (bf16[4,2,3,256,512]{4,3,2,1,0:T(8,128)(2,1)}, f32[2,3,128,512]{3,2,1,0:T(8,128)}) custom-call(s32[1]{0:T(128)} %bitcast.tens, bf16[4,8,512,512]{3,2,1,0:T(8,128)(2,1)} %get-tuple-element.100.p_ref, bf16[4,8,80,512]{3,2,1,0:T(8,128)(2,1)} %get-tuple-element.101.doa_ref, bf16[4,2,3,256,512]{4,3,2,1,0:T(8,128)(2,1)} %get-tuple-element.102.qkv_ref, ...), custom_call_target="tpu_custom_call" | custom-call | flops 4499999744 | tf_op jit(solution)/shard_map/attention_back/pallas_call | solution.py:436
  75.9 2.2 %split_mlp.1 = (f32[4736,128]{1,0:T(8,128)S(1)}, bf16[4736,128]{1,0:T(8,128)(2,1)S(1)}) custom-call(s32[2]{0:T(128)S(1)} %pad_add_fusion.3.scalars, bf16[9472,128]{1,0:T(8,128)(2,1)} %get-tuple-element.97.own, bf16[9472,128]{1,0:T(8,128)(2,1)S(1)} %collective-permute-done.3.recv), custom_call_target="tpu_custom_call" | custom-call | tf_op jit(solution)/shard_map/split_mlp/pallas_call | solution.py:544
  78.2 2.7 %collective-permute-start.4 = (bf16[4736,128]{1,0:T(8,128)(2,1)S(1)}, bf16[4736,128]{1,0:T(8,128)(2,1)S(1)}, u32[]{:S(2)}, u32[]{:S(2)}) collective-permute-start(bf16[4736,128]{1,0:T(8,128)(2,1)S(1)} %get-tuple-element.107), channel_id=1, source_target_pairs={{0,2},{1,5},{2,0},{3,7},{4,6},{5,1},{6,4},{7,3},{8,10},{9,13},{10,... | collective-permute-start | bytes 3637256 | tf_op jit(solution)/shard_map/ppermute | solution.py:539
  80.8 12.2 %attention_back.5 = (bf16[4,2,3,256,512]{4,3,2,1,0:T(8,128)(2,1)}, bf16[3072,128]{1,0:T(8,128)(2,1)S(1)}) custom-call(s32[1]{0:T(128)} %bitcast.tens, bf16[4,8,512,512]{3,2,1,0:T(8,128)(2,1)} %get-tuple-element.100.p_ref, bf16[4,8,80,512]{3,2,1,0:T(8,128)(2,1)} %get-tuple-element.101.doa_ref, ...), custom_call_target="tpu_custom_call", output_to_operand_aliasing={{0}: (6, {})} | custom-call | flops 13500000256 | tf_op jit(solution)/shard_map/attention_back/pallas_call | solution.py:436
  93.1 2.3 %collective-permute-done.4.refs_1_ = bf16[4736,128]{1,0:T(8,128)(2,1)S(1)} collective-permute-done((bf16[4736,128]{1,0:T(8,128)(2,1)S(1)}, bf16[4736,128]{1,0:T(8,128)(2,1)S(1)}, u32[]{:S(2)}, u32[]{:S(2)}) %collective-permute-start.4) | collective-permute-done | bytes 1212448 | tf_op jit(solution)/shard_map/ppermute | solution.py:539
  96.4 2.1 %collective-permute-start.5 = (bf16[2368,128]{1,0:T(8,128)(2,1)S(1)}, bf16[2368,128]{1,0:T(8,128)(2,1)S(1)}, u32[]{:S(2)}, u32[]{:S(2)}) collective-permute-start(bf16[2368,128]{1,0:T(8,128)(2,1)S(1)} %get-tuple-element.113), channel_id=1, source_target_pairs={{0,4},{1,3},{2,6},{3,1},{4,0},{5,7},{6,2},{7,5},{8,12},{9,11},{10,... | collective-permute-start | bytes 1818632 | tf_op jit(solution)/shard_map/ppermute | solution.py:539
  98.7 6.1 %attention_back.6 = (bf16[4,2,3,256,512]{4,3,2,1,0:T(8,128)(2,1)}, f32[2,3,128,512]{3,2,1,0:T(8,128)}) custom-call(s32[1]{0:T(128)} %bitcast.tens, bf16[4,8,512,512]{3,2,1,0:T(8,128)(2,1)} %get-tuple-element.100.p_ref, bf16[4,8,80,512]{3,2,1,0:T(8,128)(2,1)} %get-tuple-element.101.doa_ref, ...), custom_call_target="tpu_custom_call", output_to_operand_aliasing={{0}: (5, {})} | custom-call | flops 4499999744 | tf_op jit(solution)/shard_map/attention_back/pallas_call | solution.py:436
  104.8 1.7 collective-permute-done.5.refs_1_
  107.3 4.2 %collective-permute-start.8 = (bf16[592,128]{1,0:T(8,128)(2,1)S(1)}, bf16[592,128]{1,0:T(8,128)(2,1)S(1)}, u32[]{:S(2)}, u32[]{:S(2)}) collective-permute-start(bf16[592,128]{1,0:T(8,128)(2,1)S(1)} %get-tuple-element.118), channel_id=1, source_target_pairs={{0,24},{1,25},{2,26},{3,27},{4,28},{5,29},{6,30},{7,31},{8,16},{9,... | collective-permute-start | bytes 454664 | tf_op jit(solution)/shard_map/ppermute | solution.py:539
  112.1 12.1 %attention_back.7 = (bf16[4,2,3,256,512]{4,3,2,1,0:T(8,128)(2,1)}, f32[3072,128]{1,0:T(8,128)S(1)}) custom-call(s32[1]{0:T(128)} %bitcast.tens, bf16[4,8,512,512]{3,2,1,0:T(8,128)(2,1)} %get-tuple-element.100.p_ref, bf16[4,8,80,512]{3,2,1,0:T(8,128)(2,1)} %get-tuple-element.101.doa_ref, ...), custom_call_target="tpu_custom_call", output_to_operand_aliasing={{0}: (6, {})} | custom-call | flops 13500000256 | tf_op jit(solution)/shard_map/attention_back/pallas_call | solution.py:436
  125.7 1.7 collective-permute-start.10
  127.4 3.6 %collective-permute-start.16 = (bf16[592,128]{1,0:T(8,128)(2,1)S(1)}, bf16[592,128]{1,0:T(8,128)(2,1)S(1)}, u32[]{:S(2)}, u32[]{:S(2)}) collective-permute-start(bf16[592,128]{1,0:T(8,128)(2,1)S(1)} %settle.1.own), channel_id=1, source_target_pairs={{0,24},{1,25},{2,26},{3,27},{4,28},{5,29},{6,30},{7,31},{8,16},{9,... | collective-permute-start | bytes 454664 | tf_op jit(solution)/shard_map/ppermute | solution.py:539
  131.8 1.5 collective-permute-start.12
  133.7 10.2 %norm_one_back.1 = (f32[2048,512]{1,0:T(8,128)}, f32[32,128]{1,0:T(8,128)S(1)}) custom-call(s32[1]{0:T(128)} %bitcast.tens, bf16[4,2,3,256,512]{4,3,2,1,0:T(8,128)(2,1)} %get-tuple-element.133.dqkv, bf16[768,512]{1,0:T(8,128)(2,1)} %bitcast.27, bf16[1040,512]{1,0:T(8,128)(2,1)} %copy-done, bf16[4096,512]{1,0:T(8,128)(2,1)} %x_ref.3, ...), custom_call_target="tpu_custom_call" | custom-call | flops 10000000000 | tf_op jit(solution)/shard_map/norm_one_back/pallas_call | solution.py:483
  145.2 1.7 collective-permute-start.21
  148.2 2.9 %collective-permute-start.17 = (bf16[192,128]{1,0:T(8,128)(2,1)S(1)}, bf16[192,128]{1,0:T(8,128)(2,1)S(1)}, u32[]{:S(2)}, u32[]{:S(2)}) collective-permute-start(bf16[192,128]{1,0:T(8,128)(2,1)S(1)} %get-tuple-element.148), channel_id=1, source_target_pairs={{0,16},{1,9},{2,18},{3,11},{4,20},{5,13},{6,22},{7,15},{8,24},{9,1... | collective-permute-start | bytes 147464 | tf_op jit(solution)/shard_map/ppermute | solution.py:539
  151.5 2.1 %collective-permute-done.17.refs_1_ = bf16[192,128]{1,0:T(8,128)(2,1)S(1)} collective-permute-done((bf16[192,128]{1,0:T(8,128)(2,1)S(1)}, bf16[192,128]{1,0:T(8,128)(2,1)S(1)}, u32[]{:S(2)}, u32[]{:S(2)}) %collective-permute-start.17) | collective-permute-done | bytes 49184 | tf_op jit(solution)/shard_map/ppermute | solution.py:539
  153.7 3.3 %collective-permute-done.18.refs_2_ = bf16[192,128]{1,0:T(8,128)(2,1)S(1)} collective-permute-done((bf16[192,128]{1,0:T(8,128)(2,1)S(1)}, bf16[192,128]{1,0:T(8,128)(2,1)S(1)}, u32[]{:S(2)}, u32[]{:S(2)}) %collective-permute-start.18) | collective-permute-done | bytes 49184 | tf_op jit(solution)/shard_map/ppermute | solution.py:539
  158.2 1.5 collective-permute-start.25
  159.8 1.5 collective-permute-start.23
  161.2 2.9 %collective-permute-start.20 = (bf16[256,128]{1,0:T(8,128)(2,1)S(1)}, bf16[256,128]{1,0:T(8,128)(2,1)S(1)}, u32[]{:S(2)}, u32[]{:S(2)}) collective-permute-start(bf16[256,128]{1,0:T(8,128)(2,1)S(1)} %settle_cols.1.refs_0_), channel_id=1, source_target_pairs={{0,8},{1,17},{2,10},{3,19},{4,12},{5,21},{6,14},{7,23},{8,0},{9,25... | collective-permute-start | bytes 196616 | tf_op jit(solution)/shard_map/ppermute | solution.py:539
  164.2 1.7 collective-permute-done.23.refs_3_
  165.9 1.4 collective-permute-done.22.refs_2_
  168.5 1.4 collective-permute-start.26
  169.9 1.5 collective-permute-start.24
  171.4 9.3 %block_out.1 = bf16[2048,512]{1,0:T(8,128)(2,1)} custom-call(s32[1]{0:T(128)} %bitcast.tens, bf16[2048,2048]{1,0:T(8,128)(2,1)} %get-tuple-element.156.act_ref, bf16[1024,512]{1,0:T(8,128)(2,1)} %down_own.3, bf16[1024,512]{1,0:T(8,128)(2,1)} %copy-done.1, bf16[16,512]{1,0:T(8,128)(2,1)} %get-tuple-element.91.vecs, f32[2048,512]{1,0:T(8,128)} %get-tuple-element.94.h1_ref), custom_call_target="tpu_custom_call" | custom-call | flops 7000000000 | tf_op jit(solution)/shard_map/block_out/pallas_call | solution.py:333
  180.7 3.2 %finish_mlp.1 = (f32[1024,512]{1,0:T(8,128)}, f32[1024,512]{1,0:T(8,128)}, f32[256,512]{1,0:T(8,128)}, f32[8,128]{1,0:T(8,128)}) custom-call(s32[2]{0:T(128)S(1)} %pad_add_fusion.3.scalars, bf16[4736,128]{1,0:T(8,128)(2,1)S(1)} %join.3.refs_0_, bf16[4736,128]{1,0:T(8,128)(2,1)S(1)} %collective-permute-done.25.refs_1_), custom_call_target="tpu_custom_call" | custom-call | tf_op jit(solution)/shard_map/finish_mlp/pallas_call | solution.py:544
  184.0 2.0 %finish_qkv.1 = (f32[3,256,512]{2,1,0:T(8,128)}, f32[32,128]{1,0:T(8,128)S(1)}) custom-call(s32[4]{0:T(128)S(1)} %pad_add_fusion.1.scalars, bf16[832,128]{1,0:T(8,128)(2,1)S(1)} %join_cols.1.refs_0_, bf16[832,128]{1,0:T(8,128)(2,1)S(1)} %collective-permute-done.24.refs_1_, bf16[832,128]{1,0:T(8,128)(2,1)S(1)} %collective-permute-done.26.refs_2_, ...), custom_call_target="tpu_custom_call" | custom-call | tf_op jit(solution)/shard_map/finish_qkv/pallas_call | solution.py:544
  (56 shorter events, 14.2 us)
Async XLA Ops:
  2.9 3.0 %collective-permute-start = (bf16[1040,512]{1,0:T(8,128)(2,1)}, bf16[1040,512]{1,0:T(8,128)(2,1)S(1)}, u32[]{:S(2)}, u32[]{:S(2)}) collective-permute-start(bf16[1040,512]{1,0:T(8,128)(2,1)} %get-tuple-element.92), channel_id=1, source_target_pairs={{0,1},{1,0},{2,3},{3,2},{4,5},{5,4},{6,7},{7,6},{8,9},{9,8},{10,11... | collective-permute-start | bytes 3194888 | tf_op jit(solution)/shard_map/ppermute | solution.py:511
  3.4 25.6 %collective-permute-start.1 = (bf16[1024,512]{1,0:T(8,128)(2,1)}, bf16[1024,512]{1,0:T(8,128)(2,1)S(1)}, u32[]{:S(2)}, u32[]{:S(2)}) collective-permute-start(bf16[1024,512]{1,0:T(8,128)(2,1)} %up_own.1), channel_id=1, source_target_pairs={{0,1},{1,0},{2,3},{3,2},{4,5},{5,4},{6,7},{7,6},{8,9},{9,8},{10,11... | collective-permute-start | bytes 3145736 | tf_op jit(solution)/shard_map/ppermute | solution.py:511
  3.5 25.6 %collective-permute-start.2 = (bf16[1024,512]{1,0:T(8,128)(2,1)}, bf16[1024,512]{1,0:T(8,128)(2,1)S(1)}, u32[]{:S(2)}, u32[]{:S(2)}) collective-permute-start(bf16[1024,512]{1,0:T(8,128)(2,1)} %down_own.3), channel_id=1, source_target_pairs={{0,1},{1,0},{2,3},{3,2},{4,5},{5,4},{6,7},{7,6},{8,9},{9,8},{10,11... | collective-permute-start | bytes 3145736 | tf_op jit(solution)/shard_map/ppermute | solution.py:511
  6.0 23.1 %copy-start = (bf16[1040,512]{1,0:T(8,128)(2,1)}, bf16[1040,512]{1,0:T(8,128)(2,1)S(1)}, u32[]{:S(2)}) copy-start(bf16[1040,512]{1,0:T(8,128)(2,1)S(1)} %collective-permute-done.wq_oth.wo_oth.vecs_oth) | copy-start | bytes 3194884
  29.1 1.0 copy-start.2
  29.1 1.3 copy-start.1
  69.5 6.5 %collective-permute-start.3 = (bf16[9472,128]{1,0:T(8,128)(2,1)}, bf16[9472,128]{1,0:T(8,128)(2,1)S(1)}, u32[]{:S(2)}, u32[]{:S(2)}) collective-permute-start(bf16[9472,128]{1,0:T(8,128)(2,1)} %get-tuple-element.98), channel_id=1, source_target_pairs={{0,1},{1,0},{2,3},{3,2},{4,5},{5,4},{6,7},{7,6},{8,9},{9,8},{10,11... | collective-permute-start | bytes 7274504 | tf_op jit(solution)/shard_map/ppermute | solution.py:511
  78.2 17.2 %collective-permute-start.4 = (bf16[4736,128]{1,0:T(8,128)(2,1)S(1)}, bf16[4736,128]{1,0:T(8,128)(2,1)S(1)}, u32[]{:S(2)}, u32[]{:S(2)}) collective-permute-start(bf16[4736,128]{1,0:T(8,128)(2,1)S(1)} %get-tuple-element.107), channel_id=1, source_target_pairs={{0,2},{1,5},{2,0},{3,7},{4,6},{5,1},{6,4},{7,3},{8,10},{9,13},{10,... | collective-permute-start | bytes 3637256 | tf_op jit(solution)/shard_map/ppermute | solution.py:539
  96.4 10.2 %collective-permute-start.5 = (bf16[2368,128]{1,0:T(8,128)(2,1)S(1)}, bf16[2368,128]{1,0:T(8,128)(2,1)S(1)}, u32[]{:S(2)}, u32[]{:S(2)}) collective-permute-start(bf16[2368,128]{1,0:T(8,128)(2,1)S(1)} %get-tuple-element.113), channel_id=1, source_target_pairs={{0,4},{1,3},{2,6},{3,1},{4,0},{5,7},{6,2},{7,5},{8,12},{9,11},{10,... | collective-permute-start | bytes 1818632 | tf_op jit(solution)/shard_map/ppermute | solution.py:539
  98.6 26.2 %collective-permute-start.9 = (bf16[3072,128]{1,0:T(8,128)(2,1)S(1)}, bf16[3072,128]{1,0:T(8,128)(2,1)S(1)}, u32[]{:S(2)}, u32[]{:S(2)}) collective-permute-start(bf16[3072,128]{1,0:T(8,128)(2,1)S(1)} %get-tuple-element.110), channel_id=1, source_target_pairs={{0,1},{1,0},{2,3},{3,2},{4,5},{5,4},{6,7},{7,6},{8,9},{9,8},{10,11... | collective-permute-start | bytes 2359304 | tf_op jit(solution)/shard_map/ppermute | solution.py:511
  107.3 17.0 %collective-permute-start.8 = (bf16[592,128]{1,0:T(8,128)(2,1)S(1)}, bf16[592,128]{1,0:T(8,128)(2,1)S(1)}, u32[]{:S(2)}, u32[]{:S(2)}) collective-permute-start(bf16[592,128]{1,0:T(8,128)(2,1)S(1)} %get-tuple-element.118), channel_id=1, source_target_pairs={{0,24},{1,25},{2,26},{3,27},{4,28},{5,29},{6,30},{7,31},{8,16},{9,... | collective-permute-start | bytes 454664 | tf_op jit(solution)/shard_map/ppermute | solution.py:539
  111.5 12.8 %collective-permute-start.6 = (bf16[592,128]{1,0:T(8,128)(2,1)S(1)}, bf16[592,128]{1,0:T(8,128)(2,1)S(1)}, u32[]{:S(2)}, u32[]{:S(2)}) collective-permute-start(bf16[592,128]{1,0:T(8,128)(2,1)S(1)} %get-tuple-element.123), channel_id=1, source_target_pairs={{0,8},{1,17},{2,10},{3,19},{4,12},{5,21},{6,14},{7,23},{8,0},{9,25... | collective-permute-start | bytes 454664 | tf_op jit(solution)/shard_map/ppermute | solution.py:539
  111.5 12.8 %collective-permute-start.7 = (bf16[592,128]{1,0:T(8,128)(2,1)S(1)}, bf16[592,128]{1,0:T(8,128)(2,1)S(1)}, u32[]{:S(2)}, u32[]{:S(2)}) collective-permute-start(bf16[592,128]{1,0:T(8,128)(2,1)S(1)} %get-tuple-element.125), channel_id=1, source_target_pairs={{0,16},{1,9},{2,18},{3,11},{4,20},{5,13},{6,22},{7,15},{8,24},{9,1... | collective-permute-start | bytes 454664 | tf_op jit(solution)/shard_map/ppermute | solution.py:539
  125.7 7.6 %collective-permute-start.10 = (bf16[768,128]{1,0:T(8,128)(2,1)S(1)}, bf16[768,128]{1,0:T(8,128)(2,1)S(1)}, u32[]{:S(2)}, u32[]{:S(2)}) collective-permute-start(bf16[768,128]{1,0:T(8,128)(2,1)S(1)} %get-tuple-element.130), channel_id=1, source_target_pairs={{0,2},{1,5},{2,0},{3,7},{4,6},{5,1},{6,4},{7,3},{8,10},{9,13},{10,... | collective-permute-start | bytes 589832 | tf_op jit(solution)/shard_map/ppermute | solution.py:539
  127.4 17.1 %collective-permute-start.16 = (bf16[592,128]{1,0:T(8,128)(2,1)S(1)}, bf16[592,128]{1,0:T(8,128)(2,1)S(1)}, u32[]{:S(2)}, u32[]{:S(2)}) collective-permute-start(bf16[592,128]{1,0:T(8,128)(2,1)S(1)} %settle.1.own), channel_id=1, source_target_pairs={{0,24},{1,25},{2,26},{3,27},{4,28},{5,29},{6,30},{7,31},{8,16},{9,... | collective-permute-start | bytes 454664 | tf_op jit(solution)/shard_map/ppermute | solution.py:539
  131.0 13.5 %collective-permute-start.15 = (bf16[592,128]{1,0:T(8,128)(2,1)S(1)}, bf16[592,128]{1,0:T(8,128)(2,1)S(1)}, u32[]{:S(2)}, u32[]{:S(2)}) collective-permute-start(bf16[592,128]{1,0:T(8,128)(2,1)S(1)} %settle.1.own), channel_id=1, source_target_pairs={{0,16},{1,9},{2,18},{3,11},{4,20},{5,13},{6,22},{7,15},{8,24},{9,1... | collective-permute-start | bytes 454664 | tf_op jit(solution)/shard_map/ppermute | solution.py:539
  131.0 13.5 %collective-permute-start.14 = (bf16[592,128]{1,0:T(8,128)(2,1)S(1)}, bf16[592,128]{1,0:T(8,128)(2,1)S(1)}, u32[]{:S(2)}, u32[]{:S(2)}) collective-permute-start(bf16[592,128]{1,0:T(8,128)(2,1)S(1)} %settle.1.own), channel_id=1, source_target_pairs={{0,8},{1,17},{2,10},{3,19},{4,12},{5,21},{6,14},{7,23},{8,0},{9,25... | collective-permute-start | bytes 454664 | tf_op jit(solution)/shard_map/ppermute | solution.py:539
  131.8 12.0 %collective-permute-start.12 = (bf16[768,128]{1,0:T(8,128)(2,1)S(1)}, bf16[768,128]{1,0:T(8,128)(2,1)S(1)}, u32[]{:S(2)}, u32[]{:S(2)}) collective-permute-start(bf16[768,128]{1,0:T(8,128)(2,1)S(1)} %get-tuple-element.131), channel_id=1, source_target_pairs={{0,6},{1,7},{2,4},{3,5},{4,2},{5,3},{6,0},{7,1},{8,14},{9,15},{10,... | collective-permute-start | bytes 589832 | tf_op jit(solution)/shard_map/ppermute | solution.py:539
  133.3 10.5 %collective-permute-start.11 = (bf16[768,128]{1,0:T(8,128)(2,1)S(1)}, bf16[768,128]{1,0:T(8,128)(2,1)S(1)}, u32[]{:S(2)}, u32[]{:S(2)}) collective-permute-start(bf16[768,128]{1,0:T(8,128)(2,1)S(1)} %get-tuple-element.138), channel_id=1, source_target_pairs={{0,4},{1,3},{2,6},{3,1},{4,0},{5,7},{6,2},{7,5},{8,12},{9,11},{10,... | collective-permute-start | bytes 589832 | tf_op jit(solution)/shard_map/ppermute | solution.py:539
  145.2 12.4 %collective-permute-start.21 = (bf16[2368,128]{1,0:T(8,128)(2,1)S(1)}, bf16[2368,128]{1,0:T(8,128)(2,1)S(1)}, u32[]{:S(2)}, u32[]{:S(2)}) collective-permute-start(bf16[2368,128]{1,0:T(8,128)(2,1)S(1)} %join.2.own), channel_id=1, source_target_pairs={{0,4},{1,3},{2,6},{3,1},{4,0},{5,7},{6,2},{7,5},{8,12},{9,11},{10,... | collective-permute-start | bytes 1818632 | tf_op jit(solution)/shard_map/ppermute | solution.py:539
  146.9 4.6 %collective-permute-start.13 = (bf16[192,128]{1,0:T(8,128)(2,1)S(1)}, bf16[192,128]{1,0:T(8,128)(2,1)S(1)}, u32[]{:S(2)}, u32[]{:S(2)}) collective-permute-start(bf16[192,128]{1,0:T(8,128)(2,1)S(1)} %get-tuple-element.142), channel_id=1, source_target_pairs={{0,8},{1,17},{2,10},{3,19},{4,12},{5,21},{6,14},{7,23},{8,0},{9,25... | collective-permute-start | bytes 147464 | tf_op jit(solution)/shard_map/ppermute | solution.py:539
  148.2 5.5 %collective-permute-start.17 = (bf16[192,128]{1,0:T(8,128)(2,1)S(1)}, bf16[192,128]{1,0:T(8,128)(2,1)S(1)}, u32[]{:S(2)}, u32[]{:S(2)}) collective-permute-start(bf16[192,128]{1,0:T(8,128)(2,1)S(1)} %get-tuple-element.148), channel_id=1, source_target_pairs={{0,16},{1,9},{2,18},{3,11},{4,20},{5,13},{6,22},{7,15},{8,24},{9,1... | collective-permute-start | bytes 147464 | tf_op jit(solution)/shard_map/ppermute | solution.py:539
  151.1 5.9 %collective-permute-start.18 = (bf16[192,128]{1,0:T(8,128)(2,1)S(1)}, bf16[192,128]{1,0:T(8,128)(2,1)S(1)}, u32[]{:S(2)}, u32[]{:S(2)}) collective-permute-start(bf16[192,128]{1,0:T(8,128)(2,1)S(1)} %get-tuple-element.143), channel_id=1, source_target_pairs={{0,24},{1,25},{2,26},{3,27},{4,28},{5,29},{6,30},{7,31},{8,16},{9,... | collective-permute-start | bytes 147464 | tf_op jit(solution)/shard_map/ppermute | solution.py:539
  151.3 5.7 %collective-permute-start.19 = (f32[32,128]{1,0:T(8,128)S(1)}, f32[32,128]{1,0:T(8,128)S(1)}, u32[]{:S(2)}, u32[]{:S(2)}) collective-permute-start(f32[32,128]{1,0:T(8,128)S(1)} %get-tuple-element.136.refs_3_), channel_id=1, source_target_pairs={{0,1},{1,0},{2,3},{3,2},{4,5},{5,4},{6,7},{7,6},{8,9},{9,8},{10,11... | collective-permute-start | bytes 49160 | tf_op jit(solution)/shard_map/ppermute | solution.py:511
  158.2 22.5 %collective-permute-start.25 = (bf16[4736,128]{1,0:T(8,128)(2,1)S(1)}, bf16[4736,128]{1,0:T(8,128)(2,1)S(1)}, u32[]{:S(2)}, u32[]{:S(2)}) collective-permute-start(bf16[4736,128]{1,0:T(8,128)(2,1)S(1)} %join.3.refs_0_), channel_id=1, source_target_pairs={{0,2},{1,5},{2,0},{3,7},{4,6},{5,1},{6,4},{7,3},{8,10},{9,13},{10,... | collective-permute-start | bytes 3637256 | tf_op jit(solution)/shard_map/ppermute | solution.py:539
  159.8 6.1 %collective-permute-start.23 = (bf16[256,128]{1,0:T(8,128)(2,1)S(1)}, bf16[256,128]{1,0:T(8,128)(2,1)S(1)}, u32[]{:S(2)}, u32[]{:S(2)}) collective-permute-start(bf16[256,128]{1,0:T(8,128)(2,1)S(1)} %settle_cols.1.refs_0_), channel_id=1, source_target_pairs={{0,24},{1,25},{2,26},{3,27},{4,28},{5,29},{6,30},{7,31},{8,16},{9,... | collective-permute-start | bytes 196616 | tf_op jit(solution)/shard_map/ppermute | solution.py:539
  161.2 6.0 %collective-permute-start.22 = (bf16[256,128]{1,0:T(8,128)(2,1)S(1)}, bf16[256,128]{1,0:T(8,128)(2,1)S(1)}, u32[]{:S(2)}, u32[]{:S(2)}) collective-permute-start(bf16[256,128]{1,0:T(8,128)(2,1)S(1)} %settle_cols.1.refs_0_), channel_id=1, source_target_pairs={{0,16},{1,9},{2,18},{3,11},{4,20},{5,13},{6,22},{7,15},{8,24},{9,1... | collective-permute-start | bytes 196616 | tf_op jit(solution)/shard_map/ppermute | solution.py:539
  161.2 6.0 %collective-permute-start.20 = (bf16[256,128]{1,0:T(8,128)(2,1)S(1)}, bf16[256,128]{1,0:T(8,128)(2,1)S(1)}, u32[]{:S(2)}, u32[]{:S(2)}) collective-permute-start(bf16[256,128]{1,0:T(8,128)(2,1)S(1)} %settle_cols.1.refs_0_), channel_id=1, source_target_pairs={{0,8},{1,17},{2,10},{3,19},{4,12},{5,21},{6,14},{7,23},{8,0},{9,25... | collective-permute-start | bytes 196616 | tf_op jit(solution)/shard_map/ppermute | solution.py:539
  167.8 16.0 %collective-permute-start.27 = (bf16[832,128]{1,0:T(8,128)(2,1)S(1)}, bf16[832,128]{1,0:T(8,128)(2,1)S(1)}, u32[]{:S(2)}, u32[]{:S(2)}) collective-permute-start(bf16[832,128]{1,0:T(8,128)(2,1)S(1)} %join_cols.1.refs_0_), channel_id=1, source_target_pairs={{0,6},{1,7},{2,4},{3,5},{4,2},{5,3},{6,0},{7,1},{8,14},{9,15},{10,... | collective-permute-start | bytes 638984 | tf_op jit(solution)/shard_map/ppermute | solution.py:539
  168.5 15.3 %collective-permute-start.26 = (bf16[832,128]{1,0:T(8,128)(2,1)S(1)}, bf16[832,128]{1,0:T(8,128)(2,1)S(1)}, u32[]{:S(2)}, u32[]{:S(2)}) collective-permute-start(bf16[832,128]{1,0:T(8,128)(2,1)S(1)} %join_cols.1.refs_0_), channel_id=1, source_target_pairs={{0,4},{1,3},{2,6},{3,1},{4,0},{5,7},{6,2},{7,5},{8,12},{9,11},{10,... | collective-permute-start | bytes 638984 | tf_op jit(solution)/shard_map/ppermute | solution.py:539
  169.9 14.1 %collective-permute-start.24 = (bf16[832,128]{1,0:T(8,128)(2,1)S(1)}, bf16[832,128]{1,0:T(8,128)(2,1)S(1)}, u32[]{:S(2)}, u32[]{:S(2)}) collective-permute-start(bf16[832,128]{1,0:T(8,128)(2,1)S(1)} %join_cols.1.refs_0_), channel_id=1, source_target_pairs={{0,2},{1,5},{2,0},{3,7},{4,6},{5,1},{6,4},{7,3},{8,10},{9,13},{10,... | collective-permute-start | bytes 638984 | tf_op jit(solution)/shard_map/ppermute | solution.py:539

commit v4 on v3

--- a/solution.py
+++ b/solution.py
@@ -18,7 +18,7 @@
 MIB = 2**20
 SWAP = [(0, 1), (1, 0)]
 PLAN = (
-("back", 1, 0, 1), ("mlp",), ("back", 1, 1, 3), ("mlp+",), ("back", 0, 0, 1), ("mlp+",), ("back", 0, 1, 3), ("mlp+",), ("qkv",), ("norm",), ("qkv+",), ("mlp+",), ("qkv+",), ("mlp+",), ("qkv+",), ("out",), ("end",), ("qkv+",),
+("back", 1, 0, 1), ("mlp",), ("back", 1, 1, 3), ("mlp+",), ("back", 0, 0, 2), ("mlp+",), ("back", 0, 2, 2), ("mlp+",), ("qkv",), ("norm",), ("qkv+",), ("mlp+",), ("qkv+",), ("mlp+",), ("qkv+",), ("out",), ("end",), ("qkv+",),
 )
 
 
@@ -28,6 +28,10 @@
 
 def hbm(*values):
     return tuple(pltpu.with_memory_space_constraint(v, pltpu.HBM) for v in values)
+
+
+def vmem(*values):
+    return tuple(pltpu.with_memory_space_constraint(v, pltpu.VMEM) for v in values)
 
 
 def nn(a, b):
@@ -112,8 +116,8 @@
     n2_ref[...] = (normalised(h1)[0] * vec(vecs, 3) + vec(vecs, 4)).astype(BF)
 
 
-def whole(shape, row=0):
-    at = (row,) + (0,) * (len(shape) - 1)
+def whole(shape):
+    at = (0,) * len(shape)
     return pl.BlockSpec(shape, lambda i, *_: at, pipeline_mode=pl.Buffered(1))
 
 
@@ -126,14 +130,14 @@
 
 
 def vec(vecs, i):
-    return vecs[i:i + 1].astype(F32)
-
-
-def vecs_spec(row=0):
-    return whole((16, D), row)
-
-
-def attention_forward(tens, lens, x, vecs, wq_own, theirs, wo_own, rows):
+    return vecs[i:i + 1]
+
+
+def vecs_spec():
+    return whole((8, D))
+
+
+def attention_forward(tens, lens, x, vecs, wq_own, wq_oth, wo_own, wo_oth, rows):
     scenes = rows // LAT
     rowblock = pl.BlockSpec((LAT, D), lambda i, *_: (i, 0))
     half = wo_own.shape[0]
@@ -144,7 +148,7 @@
             grid=(scenes,),
             in_specs=[
                 pl.BlockSpec((LAT, D), lambda i, tens, lens: (tens[0] * scenes + i, 0)),
-                vecs_spec(), whole((3 * half, D)), whole((3 * half, D)), whole((half, D)), whole((half, D), 3),
+                vecs_spec(), whole((3 * half, D)), whole((3 * half, D)), whole((half, D)), whole((half, D)),
             ],
             out_specs=[
                 rowblock,
@@ -168,7 +172,7 @@
         compiler_params=params(40),
         cost_estimate=takes(23),
         name="attention_forward",
-    )(tens, *hbm(lens, x, vecs, wq_own), theirs, *hbm(wo_own), theirs)
+    )(tens, *hbm(lens, x), vecs, *hbm(wq_own), wq_oth, *hbm(wo_own), wo_oth)
 
 
 LOG2E = 1.4426950408889634
@@ -276,7 +280,7 @@
                 ref[base + 16:] = jnp.zeros((ref.shape[0] - base - 16, 128), ref.dtype)
 
 
-def mlp(tens, n2, cot, up, down, up_oth, down_oth, theirs, vecs, h1, att, rl, wo, total_rows):
+def mlp(tens, n2, cot, up, down, up_oth, down_oth, vecs_oth, vecs, h1, att, rl, wo, wo_oth, total_rows):
     rows = n2.shape[0]
     scenes = rows // LAT
     units, half = up.shape[0], wo.shape[0]
@@ -291,10 +295,10 @@
             in_specs=[
                 rowblock,
                 pl.BlockSpec((LAT, D), lambda i, tens: (tens[0] * scenes + i, 0)),
-                weights, weights, weights, weights, vecs_spec(theirs.shape[0] // 16 - 1), vecs_spec(), rowblock,
+                weights, weights, weights, weights, vecs_spec(), vecs_spec(), rowblock,
                 pl.BlockSpec((1, D, LAT), lambda i, *_: (i, 0, 0)),
                 pl.BlockSpec((1, heads, LAT), lambda i, *_: (i, 0, 0)),
-                whole((half, D)), whole((half, D), 3),
+                whole((half, D)), whole((half, D)),
             ],
             out_specs=[
                 pl.BlockSpec((LAT, 2 * units), lambda i, *_: (i, 0)), rowblock,
@@ -314,10 +318,10 @@
             pltpu.HBM((total_rows, 128), BF),
             pltpu.HBM((8, D), F32),
         ],
-        compiler_params=params(56),
+        compiler_params=params(40),
         cost_estimate=takes(39),
         name="mlp",
-    )(tens, *hbm(n2, cot, up, down, up_oth, down_oth, theirs, vecs, h1, att, rl, wo, theirs))
+    )(tens, *hbm(n2, cot, up, down), up_oth, down_oth, vecs_oth, vecs, *hbm(h1, att, rl, wo), wo_oth)
 
 
 def block_out_kernel(tens, act_ref, down_own, down_oth, vecs, h1_ref, out_ref):
@@ -344,7 +348,7 @@
         compiler_params=params(24),
         cost_estimate=takes(7),
         name="block_out",
-    )(tens, *hbm(act, down, down_oth, vecs, h1))[0]
+    )(tens, *vmem(act), down, down_oth, vecs, *hbm(h1))[0]
 
 
 def back_kernel(tens, p_ref, doa_ref, qkv_ref, n1_ref, *refs, ends):
@@ -407,7 +411,7 @@
             dw_ref[used:] = jnp.zeros((dw_ref.shape[0] - used, 128), dw_ref.dtype)
 
 
-BACK_HEADS = 2
+BACK_HEADS = 4
 
 
 def attention_back(tens, p, doa, qkv, n1, dqkv, partial, side, first, count, total_rows):
@@ -421,11 +425,11 @@
     zeros = lambda i, j, *_: (0, 0, 0, 0)
     carried, specs, aliases = [], [], {}
     if not ends[0]:
-        carried.append(partial)
+        carried.extend(hbm(partial))
         specs.append(pl.BlockSpec(sums, zeros, pipeline_mode=pl.Buffered(1)))
     if dqkv is not None:
         aliases = {5 + len(carried): 0}
-        carried.append(dqkv)
+        carried.extend(vmem(dqkv))
         specs.append(pl.BlockSpec(memory_space=pl.ANY))
     if ends[1]:
         dw = jax.ShapeDtypeStruct((total_rows, 128), BF if side else F32)
@@ -447,12 +451,12 @@
             out_specs=[pl.BlockSpec((1, 1, 3, feats, LAT), block), dw_spec],
             scratch_shapes=[pltpu.VMEM(sums, F32)],
         ),
-        out_shape=[pltpu.HBM(qkv.shape, BF), dw],
+        out_shape=[pltpu.VMEM(qkv.shape, BF), dw],
         input_output_aliases=aliases,
         compiler_params=pltpu.CompilerParams(vmem_limit_bytes=24 * MIB, dimension_semantics=("arbitrary", "arbitrary")),
         cost_estimate=takes(4.5 * count),
         name="attention_back",
-    )(tens, *hbm(p, doa, qkv, n1, *carried))
+    )(tens, *hbm(p, doa, qkv, n1), *carried)
 
 
 def norm_one_back_kernel(tens, dqkv, wq_own, wq_oth, x_ref, vecs, gh_ref, cols_two, gl_ref, cols_ref, acc):
@@ -477,7 +481,7 @@
             cols_ref[c * 8:c * 8 + 8] = total[:, c * 128:c * 128 + 128]
 
 
-def norm_one_back(tens, dqkv, wq_own, theirs, x, vecs, gh, cols_two):
+def norm_one_back(tens, dqkv, wq_own, wq_oth, x, vecs, gh, cols_two):
     scenes, half = dqkv.shape[0], dqkv.shape[3]
     rowblock = pl.BlockSpec((LAT, D), lambda i, *_: (i, 0))
     return pl.pallas_call(
@@ -500,7 +504,7 @@
         compiler_params=params(28),
         cost_estimate=takes(10),
         name="norm_one_back",
-    )(tens, *hbm(dqkv, wq_own, theirs, x, vecs, gh, cols_two))
+    )(tens, *vmem(dqkv), wq_own, wq_oth, *hbm(x), vecs, *vmem(gh), cols_two)
 
 
 def tie(value, *after):
@@ -552,51 +556,31 @@
     )(scalars, *arrays)
 
 
-def pack_kernel(*refs):
-    (*rows, up_bias, wq, wo), (packed, vecs), scratch = refs[:9], refs[9:11], refs[11:]
-    *held, whole_sem, sem = scratch
-    first = wq.shape[0]
-    everything = held[-1]
-    last = everything.shape[0] - 16
-    big = [
-        pltpu.make_async_copy(wq, everything.at[pl.ds(0, first)], sem.at[0]),
-        pltpu.make_async_copy(wo, everything.at[pl.ds(first, last - first)], sem.at[1]),
-    ]
-    small = [pltpu.make_async_copy(r, h, sem.at[2 + k]) for k, (r, h) in enumerate(zip((*rows, up_bias), held))]
-    for c in big + small:
+def rows_kernel(*refs):
+    count = (len(refs) - 2) // 2
+    ins, out, held, sem = refs[:count], refs[count], refs[count + 1:-1], refs[-1]
+    copies = [pltpu.make_async_copy(r, h, sem.at[k]) for k, (r, h) in enumerate(zip(ins, held))]
+    for c in copies:
         c.start()
-    for c in small:
+    for c in copies:
         c.wait()
-    parts = [h[...].astype(F32).reshape(1, D) for h in held[:-2]]
-    bias = held[-2][...].astype(F32)
-    parts += [bias[i:i + D].reshape(1, D) for i in range(0, bias.shape[0], D)]
-    everything[last:] = jnp.concatenate(parts + [jnp.zeros((16 - len(parts), D), F32)], 0).astype(BF)
-    for c in big:
-        c.wait()
-    out = [
-        pltpu.make_async_copy(everything, packed, whole_sem.at[0]),
-        pltpu.make_async_copy(everything.at[pl.ds(last, 16)], vecs, whole_sem.at[1]),
-    ]
-    for c in out:
-        c.start()
-    for c in out:
-        c.wait()
-
-
-def pack(rows, up_bias, wq, wo):
-    shape = (wq.shape[0] + wo.shape[0] + 16, D)
+    parts = []
+    for h in held:
+        v = h[...].astype(F32)
+        parts += [v[i:i + D].reshape(1, D) for i in range(0, v.shape[0], D)]
+    out[...] = jnp.concatenate(parts + [jnp.zeros((1, D), F32)] * (out.shape[0] - len(parts)), 0)
+
+
+def rows_of(*vectors):
+    count = -(-sum(v.shape[0] for v in vectors) // (8 * D)) * 8
     return pl.pallas_call(
-        pack_kernel,
-        in_specs=[pl.BlockSpec(memory_space=pl.ANY)] * 9,
-        out_specs=[pl.BlockSpec(memory_space=pl.ANY)] * 2,
-        out_shape=[pltpu.HBM(shape, BF), pltpu.HBM((16, D), BF)],
-        scratch_shapes=[pltpu.VMEM((D,), BF)] * 6 + [
-            pltpu.VMEM(up_bias.shape, BF), pltpu.VMEM(shape, BF), pltpu.SemaphoreType.DMA((2,)),
-            pltpu.SemaphoreType.DMA((9,)),
-        ],
+        rows_kernel,
+        in_specs=[pl.BlockSpec(memory_space=pl.ANY)] * len(vectors),
+        out_shape=jax.ShapeDtypeStruct((count, D), F32),
+        scratch_shapes=[pltpu.VMEM(v.shape, BF) for v in vectors] + [pltpu.SemaphoreType.DMA((len(vectors),))],
         compiler_params=pltpu.CompilerParams(vmem_limit_bytes=16 * MIB),
-        name="pack",
-    )(*hbm(*rows, up_bias, wq, wo))
+        name="rows_of",
+    )(*hbm(*vectors))
 
 
 def chunk(place, m):
@@ -805,19 +789,19 @@
             Stage(count, (lower[i:i + 2],) * 2, ([1, 2, 3], [2, 1, 3])) for i in range(0, len(lower), 2)
         ] + [group]
 
-    packed, vecs = pack(
-        (attn_gain, attn_shift, out_bias, mlp_gain, mlp_shift, down_bias), up_bias, qkv_weight.reshape(3 * half, D), out_weight
-    )
-    theirs = swap(packed)
+    wq = qkv_weight.reshape(3 * half, D)
+    wq_oth, wo_oth = swap(wq), swap(out_weight)
+    vecs = rows_of(attn_gain, attn_shift, out_bias, mlp_gain, mlp_shift, down_bias, up_bias)
+    vecs_oth = swap(vecs)
     up_oth, down_oth = swap(up_weight), swap(down_weight)
 
     n1, qkv, p, att, rl, h1, n2 = attention_forward(
-        tens, scene_len, latents, vecs, qkv_weight.reshape(3 * half, D), theirs, out_weight, rows
+        tens, scene_len, latents, vecs, wq, wq_oth, out_weight, wo_oth, rows
     )
     need = 8 * units + 4 * half + 16
     total_rows = -(-need // (16 * count)) * 16 * count
     act, gh, doa, grads_own, grads_oth, cols_two = mlp(
-        tens, n2, cotangent, up_weight, down_weight, up_oth, down_oth, theirs, vecs, h1, att, rl, out_weight, total_rows
+        tens, n2, cotangent, up_weight, down_weight, up_oth, down_oth, vecs_oth, vecs, h1, att, rl, out_weight, wo_oth, total_rows
     )
     from_peer = swap(grads_oth)
 
@@ -874,7 +858,7 @@
             token = next(chains["qkv"])
         elif action == "norm":
             grad_latents, cols_one = norm_one_back(
-                tie(tens, token), dqkv, qkv_weight.reshape(3 * half, D), theirs, latents, vecs, gh, cols_two
+                tie(tens, token), dqkv, wq, wq_oth, latents, vecs, gh, cols_two
             )
             cols.extend((cols_one, swap(cols_one)))
             token = cols_one

time: 187 us -> 179 us (0.957)
  Pallas kernels: 134 us -> 124 us
  waiting for transfers between devices: 15 us -> 17.7 us
    ppermute x22, waiting for transfers between devices: 13 us -> 17.2 us  [exchange(): out.append(lax.ppermute(v, ('dp', 'tensor'), pairs))]
    pallas_call x4, Pallas kernels: 36.4 us -> 33.2 us  [attention_back(): pl.pallas_call(functools.partial(back_kernel, ends=ends), grid_spec=pltpu...]
    pallas_call x1, Pallas kernels: 10.2 us -> 8.03 us  [norm_one_back(): pl.pallas_call(norm_one_back_kernel, grid_spec=pltpu.PrefetchScalarGridSp...]
    pallas_call x1, Pallas kernels: 9.32 us -> 7.26 us  [block_out(): pl.pallas_call(block_out_kernel, grid_spec=pltpu.PrefetchScalarGridSpec(n...]
  transfers between devices with their start and end apart: 28 -> 30, of which waited for: 9 -> 9; matrix products, arithmetic and copies ran while one was open for 0% -> 0% of each run, Pallas kernels for 46% -> 45%
where the time goes in v4:
time: 179 us; the launch traced here: 178 us
  Pallas kernels  124 us (69%)
  starting transfers between devices  34.3 us (19%)
  waiting for transfers between devices  17.7 us (10%)
    pallas_call x1, Pallas kernels, mlp(): pl.pallas_call(mlp_kernel, grid_spec=pltpu.PrefetchScalarGridSpec(num_sca...  38.4 us
    pallas_call x4, Pallas kernels, attention_back(): pl.pallas_call(functools.partial(back_kernel, ends=ends), grid_spec=pltpu...  33.2 us
    ppermute x22, starting transfers between devices, exchange(): out.append(lax.ppermute(v, ('dp', 'tensor'), pairs))  32.1 us
    pallas_call x1, Pallas kernels, attention_forward(): pl.pallas_call(forward_kernel, grid_spec=pltpu.PrefetchScalarGridSpec(num...  23.1 us
    ppermute x22, waiting for transfers between devices, exchange(): out.append(lax.ppermute(v, ('dp', 'tensor'), pairs))  17.2 us
    pallas_call x12, Pallas kernels, small_call(): pl.pallas_call(kernel, in_specs=[pl.BlockSpec(memory_space=pltpu.SMEM)] +...  13.5 us
    pallas_call x1, Pallas kernels, norm_one_back(): pl.pallas_call(norm_one_back_kernel, grid_spec=pltpu.PrefetchScalarGridSp...  8.03 us
    pallas_call x1, Pallas kernels, block_out(): pl.pallas_call(block_out_kernel, grid_spec=pltpu.PrefetchScalarGridSpec(n...  7.26 us
  transfers between devices with their start and end apart: 30, of which 9 were waited for; matrix products, arithmetic and copies ran while one was open for 0% of the time, Pallas kernels for 45%

profile of v4, /device:TPU:0, one launch (start us, length us, event | category | flops | bytes accessed | tf_op | source)
XLA Modules:
  0.0 178.2 jit_solution(15704233556861186012)
XLA Ops:
  3.7 23.1 %attention_forward.1 = (bf16[2048,512]{1,0:T(8,128)(2,1)}, bf16[4,2,3,256,512]{4,3,2,1,0:T(8,128)(2,1)}, bf16[4,8,512,512]{3,2,1,0:T(8,128)(2,1)}, bf16[4,512,51...) custom-call(s32[1]{0:T(128)} %bitcast.tens, s32[8]{0:T(128)} %lens.1, ...), custom_call_target="tpu_custom_call" | custom-call | flops 23000000512 | tf_op jit(solution)/shard_map/attention_forward/pallas_call | solution.py:144
  26.8 38.4 %mlp.1 = (bf16[2048,2048]{1,0:T(8,128)(2,1)}, f32[2048,512]{1,0:T(8,128)}, bf16[4,8,80,512]{3,2,1,0:T(8,128)(2,1)}, bf16[9472,128]{1,0:T(8,128)(2,1)}, bf16[9472,128]{1,0:T(8,128)(2,1)}, /*index=5*/f32[8,512]{1,0:T(8,128)}) custom-call(s32[1]{0:T(128)} %bitcast.tens, bf16[2048,512]{1,0:T(8,128)(2,1)} %get-tuple-element.89.n2_ref, bf16[4096,512]{1,0:T(8,128)(2,1)} %cot_ref.1, ...), custom_call_target="tpu_custom_call" | custom-call | flops 38999998464 | tf_op jit(solution)/shard_map/mlp/pallas_call | solution.py:290
  65.9 5.7 %attention_back.4 = (bf16[4,2,3,256,512]{4,3,2,1,0:T(8,128)(2,1)S(1)}, f32[1,3,256,512]{3,2,1,0:T(8,128)}) custom-call(s32[1]{0:T(128)} %bitcast.tens, bf16[4,8,512,512]{3,2,1,0:T(8,128)(2,1)} %get-tuple-element.96.p_ref, bf16[4,8,80,512]{3,2,1,0:T(8,128)(2,1)} %get-tuple-element.97.doa_ref, bf16[4,2,3,256,512]{4,3,2,1,0:T(8,128)(2,1)} %get-tuple-element.98.qkv_ref, ...), custom_call_target="tpu_custom_call" | custom-call | flops 4499999744 | tf_op jit(solution)/shard_map/attention_back/pallas_call | solution.py:440
  71.6 2.2 %split_mlp.1 = (f32[4736,128]{1,0:T(8,128)S(1)}, bf16[4736,128]{1,0:T(8,128)(2,1)S(1)}) custom-call(s32[2]{0:T(128)S(1)} %pad_add_fusion.3.scalars, bf16[9472,128]{1,0:T(8,128)(2,1)} %get-tuple-element.93.own, bf16[9472,128]{1,0:T(8,128)(2,1)S(1)} %collective-permute-done.5.recv), custom_call_target="tpu_custom_call" | custom-call | tf_op jit(solution)/shard_map/split_mlp/pallas_call | solution.py:548
  73.8 2.7 %collective-permute-start.6 = (bf16[4736,128]{1,0:T(8,128)(2,1)S(1)}, bf16[4736,128]{1,0:T(8,128)(2,1)S(1)}, u32[]{:S(2)}, u32[]{:S(2)}) collective-permute-start(bf16[4736,128]{1,0:T(8,128)(2,1)S(1)} %get-tuple-element.103), channel_id=1, source_target_pairs={{0,2},{1,5},{2,0},{3,7},{4,6},{5,1},{6,4},{7,3},{8,10},{9,13},{10,... | collective-permute-start | bytes 3637256 | tf_op jit(solution)/shard_map/ppermute | solution.py:543
  76.6 10.7 %attention_back.5 = (bf16[4,2,3,256,512]{4,3,2,1,0:T(8,128)(2,1)S(1)}, bf16[3072,128]{1,0:T(8,128)(2,1)S(1)}) custom-call(s32[1]{0:T(128)} %bitcast.tens, bf16[4,8,512,512]{3,2,1,0:T(8,128)(2,1)} %get-tuple-element.96.p_ref, bf16[4,8,80,512]{3,2,1,0:T(8,128)(2,1)} %get-tuple-element.97.doa_ref, ...), custom_call_target="tpu_custom_call", output_to_operand_aliasing={{0}: (6, {})} | custom-call | flops 13500000256 | tf_op jit(solution)/shard_map/attention_back/pallas_call | solution.py:440
  87.4 3.7 %collective-permute-done.6.refs_1_ = bf16[4736,128]{1,0:T(8,128)(2,1)S(1)} collective-permute-done((bf16[4736,128]{1,0:T(8,128)(2,1)S(1)}, bf16[4736,128]{1,0:T(8,128)(2,1)S(1)}, u32[]{:S(2)}, u32[]{:S(2)}) %collective-permute-start.6) | collective-permute-done | bytes 1212448 | tf_op jit(solution)/shard_map/ppermute | solution.py:543
  91.1 1.0 split.4
  92.1 2.1 %collective-permute-start.7 = (bf16[2368,128]{1,0:T(8,128)(2,1)S(1)}, bf16[2368,128]{1,0:T(8,128)(2,1)S(1)}, u32[]{:S(2)}, u32[]{:S(2)}) collective-permute-start(bf16[2368,128]{1,0:T(8,128)(2,1)S(1)} %get-tuple-element.109), channel_id=1, source_target_pairs={{0,4},{1,3},{2,6},{3,1},{4,0},{5,7},{6,2},{7,5},{8,12},{9,11},{10,... | collective-permute-start | bytes 1818632 | tf_op jit(solution)/shard_map/ppermute | solution.py:543
  94.2 8.6 %attention_back.6 = (bf16[4,2,3,256,512]{4,3,2,1,0:T(8,128)(2,1)S(1)}, f32[1,3,256,512]{3,2,1,0:T(8,128)}) custom-call(s32[1]{0:T(128)} %bitcast.tens, bf16[4,8,512,512]{3,2,1,0:T(8,128)(2,1)} %get-tuple-element.96.p_ref, bf16[4,8,80,512]{3,2,1,0:T(8,128)(2,1)} %get-tuple-element.97.doa_ref, ...), custom_call_target="tpu_custom_call", output_to_operand_aliasing={{0}: (5, {})} | custom-call | flops 8999999488 | tf_op jit(solution)/shard_map/attention_back/pallas_call | solution.py:440
  103.5 3.6 %collective-permute-start.10 = (bf16[592,128]{1,0:T(8,128)(2,1)S(1)}, bf16[592,128]{1,0:T(8,128)(2,1)S(1)}, u32[]{:S(2)}, u32[]{:S(2)}) collective-permute-start(bf16[592,128]{1,0:T(8,128)(2,1)S(1)} %get-tuple-element.114), channel_id=1, source_target_pairs={{0,24},{1,25},{2,26},{3,27},{4,28},{5,29},{6,30},{7,31},{8,16},{9,... | collective-permute-start | bytes 454664 | tf_op jit(solution)/shard_map/ppermute | solution.py:543
  108.0 8.2 %attention_back.7 = (bf16[4,2,3,256,512]{4,3,2,1,0:T(8,128)(2,1)S(1)}, f32[3072,128]{1,0:T(8,128)S(1)}) custom-call(s32[1]{0:T(128)} %bitcast.tens, bf16[4,8,512,512]{3,2,1,0:T(8,128)(2,1)} %get-tuple-element.96.p_ref, bf16[4,8,80,512]{3,2,1,0:T(8,128)(2,1)} %get-tuple-element.97.doa_ref, ...), custom_call_target="tpu_custom_call", output_to_operand_aliasing={{0}: (6, {})} | custom-call | flops 8999999488 | tf_op jit(solution)/shard_map/attention_back/pallas_call | solution.py:440
  116.2 3.1 %collective-permute-done.9.refs_1_ = bf16[592,128]{1,0:T(8,128)(2,1)S(1)} collective-permute-done((bf16[592,128]{1,0:T(8,128)(2,1)S(1)}, bf16[592,128]{1,0:T(8,128)(2,1)S(1)}, u32[]{:S(2)}, u32[]{:S(2)}) %collective-permute-start.9) | collective-permute-done | bytes 151584 | tf_op jit(solution)/shard_map/ppermute | solution.py:543
  121.8 2.5 %collective-permute-start.18 = (bf16[592,128]{1,0:T(8,128)(2,1)S(1)}, bf16[592,128]{1,0:T(8,128)(2,1)S(1)}, u32[]{:S(2)}, u32[]{:S(2)}) collective-permute-start(bf16[592,128]{1,0:T(8,128)(2,1)S(1)} %settle.1.own), channel_id=1, source_target_pairs={{0,24},{1,25},{2,26},{3,27},{4,28},{5,29},{6,30},{7,31},{8,16},{9,... | collective-permute-start | bytes 454664 | tf_op jit(solution)/shard_map/ppermute | solution.py:543
  124.3 1.9 %collective-permute-start.16 = (bf16[592,128]{1,0:T(8,128)(2,1)S(1)}, bf16[592,128]{1,0:T(8,128)(2,1)S(1)}, u32[]{:S(2)}, u32[]{:S(2)}) collective-permute-start(bf16[592,128]{1,0:T(8,128)(2,1)S(1)} %settle.1.own), channel_id=1, source_target_pairs={{0,8},{1,17},{2,10},{3,19},{4,12},{5,21},{6,14},{7,23},{8,0},{9,25... | collective-permute-start | bytes 454664 | tf_op jit(solution)/shard_map/ppermute | solution.py:543
  126.2 2.1 %collective-permute-start.14 = (bf16[768,128]{1,0:T(8,128)(2,1)S(1)}, bf16[768,128]{1,0:T(8,128)(2,1)S(1)}, u32[]{:S(2)}, u32[]{:S(2)}) collective-permute-start(bf16[768,128]{1,0:T(8,128)(2,1)S(1)} %get-tuple-element.127), channel_id=1, source_target_pairs={{0,6},{1,7},{2,4},{3,5},{4,2},{5,3},{6,0},{7,1},{8,14},{9,15},{10,... | collective-permute-start | bytes 589832 | tf_op jit(solution)/shard_map/ppermute | solution.py:543
  128.8 8.0 %norm_one_back.1 = (f32[2048,512]{1,0:T(8,128)}, f32[32,128]{1,0:T(8,128)S(1)}) custom-call(s32[1]{0:T(128)} %bitcast.tens, bf16[4,2,3,256,512]{4,3,2,1,0:T(8,128)(2,1)S(1)} %get-tuple-element.129.dqkv, bf16[768,512]{1,0:T(8,128)(2,1)S(1)} %bitcast.27, bf16[768,512]{1,0:T(8,128)(2,1)S(1)} %copy-done.3, bf16[4096,512]{1,0:T(8,128)(2,1)} %x_ref.3, ...), custom_call_target="tpu_custom_call" | custom-call | flops 10000000000 | tf_op jit(solution)/shard_map/norm_one_back/pallas_call | solution.py:487
  138.2 1.6 collective-permute-start.23
  139.9 2.9 %collective-permute-start.19 = (bf16[192,128]{1,0:T(8,128)(2,1)S(1)}, bf16[192,128]{1,0:T(8,128)(2,1)S(1)}, u32[]{:S(2)}, u32[]{:S(2)}) collective-permute-start(bf16[192,128]{1,0:T(8,128)(2,1)S(1)} %get-tuple-element.144), channel_id=1, source_target_pairs={{0,16},{1,9},{2,18},{3,11},{4,20},{5,13},{6,22},{7,15},{8,24},{9,1... | collective-permute-start | bytes 147464 | tf_op jit(solution)/shard_map/ppermute | solution.py:543
  142.8 1.3 collective-permute-start.20
  144.9 3.8 %collective-permute-done.20.refs_2_ = bf16[192,128]{1,0:T(8,128)(2,1)S(1)} collective-permute-done((bf16[192,128]{1,0:T(8,128)(2,1)S(1)}, bf16[192,128]{1,0:T(8,128)(2,1)S(1)}, u32[]{:S(2)}, u32[]{:S(2)}) %collective-permute-start.20) | collective-permute-done | bytes 49184 | tf_op jit(solution)/shard_map/ppermute | solution.py:543
  150.9 2.3 %collective-permute-start.25 = (bf16[256,128]{1,0:T(8,128)(2,1)S(1)}, bf16[256,128]{1,0:T(8,128)(2,1)S(1)}, u32[]{:S(2)}, u32[]{:S(2)}) collective-permute-start(bf16[256,128]{1,0:T(8,128)(2,1)S(1)} %settle_cols.1.refs_0_), channel_id=1, source_target_pairs={{0,24},{1,25},{2,26},{3,27},{4,28},{5,29},{6,30},{7,31},{8,16},{9,... | collective-permute-start | bytes 196616 | tf_op jit(solution)/shard_map/ppermute | solution.py:543
  153.2 2.1 %collective-permute-start.22 = (bf16[256,128]{1,0:T(8,128)(2,1)S(1)}, bf16[256,128]{1,0:T(8,128)(2,1)S(1)}, u32[]{:S(2)}, u32[]{:S(2)}) collective-permute-start(bf16[256,128]{1,0:T(8,128)(2,1)S(1)} %settle_cols.1.refs_0_), channel_id=1, source_target_pairs={{0,8},{1,17},{2,10},{3,19},{4,12},{5,21},{6,14},{7,23},{8,0},{9,25... | collective-permute-start | bytes 196616 | tf_op jit(solution)/shard_map/ppermute | solution.py:543
  155.3 1.7 collective-permute-done.25.refs_3_
  157.0 1.4 collective-permute-done.24.refs_2_
  158.9 1.4 collective-permute-start.29
  160.3 1.3 collective-permute-start.28
  162.5 7.3 %block_out.1 = bf16[2048,512]{1,0:T(8,128)(2,1)} custom-call(s32[1]{0:T(128)} %bitcast.tens, bf16[2048,2048]{1,0:T(8,128)(2,1)S(1)} %bitcast.29, bf16[1024,512]{1,0:T(8,128)(2,1)S(1)} %copy-done, bf16[1024,512]{1,0:T(8,128)(2,1)S(1)} %collective-permute-done.3.down_oth, f32[8,512]{1,0:T(8,128)S(1)} %rows_of.1.vecs, f32[2048,512]{1,0:T(8,128)} %get-tuple-element.90.h1_ref), custom_call_target="tpu_custom_call" | custom-call | flops 7000000000 | tf_op jit(solution)/shard_map/block_out/pallas_call | solution.py:337
  169.8 1.3 collective-permute-done.27.refs_1_
  171.1 3.2 %finish_mlp.1 = (f32[1024,512]{1,0:T(8,128)}, f32[1024,512]{1,0:T(8,128)}, f32[256,512]{1,0:T(8,128)}, f32[8,128]{1,0:T(8,128)}) custom-call(s32[2]{0:T(128)S(1)} %pad_add_fusion.3.scalars, bf16[4736,128]{1,0:T(8,128)(2,1)S(1)} %join.3.refs_0_, bf16[4736,128]{1,0:T(8,128)(2,1)S(1)} %collective-permute-done.27.refs_1_), custom_call_target="tpu_custom_call" | custom-call | tf_op jit(solution)/shard_map/finish_mlp/pallas_call | solution.py:548
  174.3 1.4 collective-permute-done.26.refs_1_
  175.7 2.0 %finish_qkv.1 = (f32[3,256,512]{2,1,0:T(8,128)}, f32[32,128]{1,0:T(8,128)S(1)}) custom-call(s32[4]{0:T(128)S(1)} %pad_add_fusion.1.scalars, bf16[832,128]{1,0:T(8,128)(2,1)S(1)} %join_cols.1.refs_0_, bf16[832,128]{1,0:T(8,128)(2,1)S(1)} %collective-permute-done.26.refs_1_, bf16[832,128]{1,0:T(8,128)(2,1)S(1)} %collective-permute-done.28.refs_2_, ...), custom_call_target="tpu_custom_call" | custom-call | tf_op jit(solution)/shard_map/finish_qkv/pallas_call | solution.py:548
  (71 shorter events, 14.8 us)
Async XLA Ops:
  0.6 3.0 %collective-permute-start = (bf16[768,512]{1,0:T(8,128)(2,1)}, bf16[768,512]{1,0:T(8,128)(2,1)S(1)}, u32[]{:S(2)}, u32[]{:S(2)}) collective-permute-start(bf16[768,512]{1,0:T(8,128)(2,1)} %bitcast.25), channel_id=1, source_target_pairs={{0,1},{1,0},{2,3},{3,2},{4,5},{5,4},{6,7},{7,6},{8,9},{9,8},{10,11... | collective-permute-start | bytes 2359304 | tf_op jit(solution)/shard_map/ppermute | solution.py:515
  1.2 2.5 %collective-permute-start.1 = (bf16[256,512]{1,0:T(8,128)(2,1)}, bf16[256,512]{1,0:T(8,128)(2,1)S(1)}, u32[]{:S(2)}, u32[]{:S(2)}) collective-permute-start(bf16[256,512]{1,0:T(8,128)(2,1)} %wo_own.3), channel_id=1, source_target_pairs={{0,1},{1,0},{2,3},{3,2},{4,5},{5,4},{6,7},{7,6},{8,9},{9,8},{10,11... | collective-permute-start | bytes 786440 | tf_op jit(solution)/shard_map/ppermute | solution.py:515
  2.1 24.6 %collective-permute-start.4 = (f32[8,512]{1,0:T(8,128)S(1)}, f32[8,512]{1,0:T(8,128)S(1)}, u32[]{:S(2)}, u32[]{:S(2)}) collective-permute-start(f32[8,512]{1,0:T(8,128)S(1)} %rows_of.1.vecs), channel_id=1, source_target_pairs={{0,1},{1,0},{2,3},{3,2},{4,5},{5,4},{6,7},{7,6},{8,9},{9,8},{10,11... | collective-permute-start | bytes 49160 | tf_op jit(solution)/shard_map/ppermute | solution.py:515
  2.6 24.2 %collective-permute-start.2 = (bf16[1024,512]{1,0:T(8,128)(2,1)}, bf16[1024,512]{1,0:T(8,128)(2,1)S(1)}, u32[]{:S(2)}, u32[]{:S(2)}) collective-permute-start(bf16[1024,512]{1,0:T(8,128)(2,1)} %up_own.1), channel_id=1, source_target_pairs={{0,1},{1,0},{2,3},{3,2},{4,5},{5,4},{6,7},{7,6},{8,9},{9,8},{10,11... | collective-permute-start | bytes 3145736 | tf_op jit(solution)/shard_map/ppermute | solution.py:515
  2.7 24.1 %collective-permute-start.3 = (bf16[1024,512]{1,0:T(8,128)(2,1)}, bf16[1024,512]{1,0:T(8,128)(2,1)S(1)}, u32[]{:S(2)}, u32[]{:S(2)}) collective-permute-start(bf16[1024,512]{1,0:T(8,128)(2,1)} %down_own.3), channel_id=1, source_target_pairs={{0,1},{1,0},{2,3},{3,2},{4,5},{5,4},{6,7},{7,6},{8,9},{9,8},{10,11... | collective-permute-start | bytes 3145736 | tf_op jit(solution)/shard_map/ppermute | solution.py:515
  65.2 6.4 %collective-permute-start.5 = (bf16[9472,128]{1,0:T(8,128)(2,1)}, bf16[9472,128]{1,0:T(8,128)(2,1)S(1)}, u32[]{:S(2)}, u32[]{:S(2)}) collective-permute-start(bf16[9472,128]{1,0:T(8,128)(2,1)} %get-tuple-element.94), channel_id=1, source_target_pairs={{0,1},{1,0},{2,3},{3,2},{4,5},{5,4},{6,7},{7,6},{8,9},{9,8},{10,11... | collective-permute-start | bytes 7274504 | tf_op jit(solution)/shard_map/ppermute | solution.py:515
  73.8 17.3 %collective-permute-start.6 = (bf16[4736,128]{1,0:T(8,128)(2,1)S(1)}, bf16[4736,128]{1,0:T(8,128)(2,1)S(1)}, u32[]{:S(2)}, u32[]{:S(2)}) collective-permute-start(bf16[4736,128]{1,0:T(8,128)(2,1)S(1)} %get-tuple-element.103), channel_id=1, source_target_pairs={{0,2},{1,5},{2,0},{3,7},{4,6},{5,1},{6,4},{7,3},{8,10},{9,13},{10,... | collective-permute-start | bytes 3637256 | tf_op jit(solution)/shard_map/ppermute | solution.py:543
  87.3 32.7 %collective-permute-start.11 = (bf16[3072,128]{1,0:T(8,128)(2,1)S(1)}, bf16[3072,128]{1,0:T(8,128)(2,1)S(1)}, u32[]{:S(2)}, u32[]{:S(2)}) collective-permute-start(bf16[3072,128]{1,0:T(8,128)(2,1)S(1)} %get-tuple-element.106), channel_id=1, source_target_pairs={{0,1},{1,0},{2,3},{3,2},{4,5},{5,4},{6,7},{7,6},{8,9},{9,8},{10,11... | collective-permute-start | bytes 2359304 | tf_op jit(solution)/shard_map/ppermute | solution.py:515
  92.1 10.7 %collective-permute-start.7 = (bf16[2368,128]{1,0:T(8,128)(2,1)S(1)}, bf16[2368,128]{1,0:T(8,128)(2,1)S(1)}, u32[]{:S(2)}, u32[]{:S(2)}) collective-permute-start(bf16[2368,128]{1,0:T(8,128)(2,1)S(1)} %get-tuple-element.109), channel_id=1, source_target_pairs={{0,4},{1,3},{2,6},{3,1},{4,0},{5,7},{6,2},{7,5},{8,12},{9,11},{10,... | collective-permute-start | bytes 1818632 | tf_op jit(solution)/shard_map/ppermute | solution.py:543
  103.5 15.9 %collective-permute-start.10 = (bf16[592,128]{1,0:T(8,128)(2,1)S(1)}, bf16[592,128]{1,0:T(8,128)(2,1)S(1)}, u32[]{:S(2)}, u32[]{:S(2)}) collective-permute-start(bf16[592,128]{1,0:T(8,128)(2,1)S(1)} %get-tuple-element.114), channel_id=1, source_target_pairs={{0,24},{1,25},{2,26},{3,27},{4,28},{5,29},{6,30},{7,31},{8,16},{9,... | collective-permute-start | bytes 454664 | tf_op jit(solution)/shard_map/ppermute | solution.py:543
  107.1 9.1 %collective-permute-start.8 = (bf16[592,128]{1,0:T(8,128)(2,1)S(1)}, bf16[592,128]{1,0:T(8,128)(2,1)S(1)}, u32[]{:S(2)}, u32[]{:S(2)}) collective-permute-start(bf16[592,128]{1,0:T(8,128)(2,1)S(1)} %get-tuple-element.119), channel_id=1, source_target_pairs={{0,8},{1,17},{2,10},{3,19},{4,12},{5,21},{6,14},{7,23},{8,0},{9,25... | collective-permute-start | bytes 454664 | tf_op jit(solution)/shard_map/ppermute | solution.py:543
  107.1 12.2 %collective-permute-start.9 = (bf16[592,128]{1,0:T(8,128)(2,1)S(1)}, bf16[592,128]{1,0:T(8,128)(2,1)S(1)}, u32[]{:S(2)}, u32[]{:S(2)}) collective-permute-start(bf16[592,128]{1,0:T(8,128)(2,1)S(1)} %get-tuple-element.121), channel_id=1, source_target_pairs={{0,16},{1,9},{2,18},{3,11},{4,20},{5,13},{6,22},{7,15},{8,24},{9,1... | collective-permute-start | bytes 454664 | tf_op jit(solution)/shard_map/ppermute | solution.py:543
  120.8 7.4 %collective-permute-start.12 = (bf16[768,128]{1,0:T(8,128)(2,1)S(1)}, bf16[768,128]{1,0:T(8,128)(2,1)S(1)}, u32[]{:S(2)}, u32[]{:S(2)}) collective-permute-start(bf16[768,128]{1,0:T(8,128)(2,1)S(1)} %get-tuple-element.126), channel_id=1, source_target_pairs={{0,2},{1,5},{2,0},{3,7},{4,6},{5,1},{6,4},{7,3},{8,10},{9,13},{10,... | collective-permute-start | bytes 589832 | tf_op jit(solution)/shard_map/ppermute | solution.py:543
  121.8 15.7 %collective-permute-start.18 = (bf16[592,128]{1,0:T(8,128)(2,1)S(1)}, bf16[592,128]{1,0:T(8,128)(2,1)S(1)}, u32[]{:S(2)}, u32[]{:S(2)}) collective-permute-start(bf16[592,128]{1,0:T(8,128)(2,1)S(1)} %settle.1.own), channel_id=1, source_target_pairs={{0,24},{1,25},{2,26},{3,27},{4,28},{5,29},{6,30},{7,31},{8,16},{9,... | collective-permute-start | bytes 454664 | tf_op jit(solution)/shard_map/ppermute | solution.py:543
  124.3 13.3 %collective-permute-start.17 = (bf16[592,128]{1,0:T(8,128)(2,1)S(1)}, bf16[592,128]{1,0:T(8,128)(2,1)S(1)}, u32[]{:S(2)}, u32[]{:S(2)}) collective-permute-start(bf16[592,128]{1,0:T(8,128)(2,1)S(1)} %settle.1.own), channel_id=1, source_target_pairs={{0,16},{1,9},{2,18},{3,11},{4,20},{5,13},{6,22},{7,15},{8,24},{9,1... | collective-permute-start | bytes 454664 | tf_op jit(solution)/shard_map/ppermute | solution.py:543
  124.3 13.3 %collective-permute-start.16 = (bf16[592,128]{1,0:T(8,128)(2,1)S(1)}, bf16[592,128]{1,0:T(8,128)(2,1)S(1)}, u32[]{:S(2)}, u32[]{:S(2)}) collective-permute-start(bf16[592,128]{1,0:T(8,128)(2,1)S(1)} %settle.1.own), channel_id=1, source_target_pairs={{0,8},{1,17},{2,10},{3,19},{4,12},{5,21},{6,14},{7,23},{8,0},{9,25... | collective-permute-start | bytes 454664 | tf_op jit(solution)/shard_map/ppermute | solution.py:543
  126.2 10.7 %collective-permute-start.14 = (bf16[768,128]{1,0:T(8,128)(2,1)S(1)}, bf16[768,128]{1,0:T(8,128)(2,1)S(1)}, u32[]{:S(2)}, u32[]{:S(2)}) collective-permute-start(bf16[768,128]{1,0:T(8,128)(2,1)S(1)} %get-tuple-element.127), channel_id=1, source_target_pairs={{0,6},{1,7},{2,4},{3,5},{4,2},{5,3},{6,0},{7,1},{8,14},{9,15},{10,... | collective-permute-start | bytes 589832 | tf_op jit(solution)/shard_map/ppermute | solution.py:543
  128.3 8.6 %collective-permute-start.13 = (bf16[768,128]{1,0:T(8,128)(2,1)S(1)}, bf16[768,128]{1,0:T(8,128)(2,1)S(1)}, u32[]{:S(2)}, u32[]{:S(2)}) collective-permute-start(bf16[768,128]{1,0:T(8,128)(2,1)S(1)} %get-tuple-element.134), channel_id=1, source_target_pairs={{0,4},{1,3},{2,6},{3,1},{4,0},{5,7},{6,2},{7,5},{8,12},{9,11},{10,... | collective-permute-start | bytes 589832 | tf_op jit(solution)/shard_map/ppermute | solution.py:543
  128.8 33.7 %slice-start = ((s8[8388608]{0:T(1024)(128)(4,1)}), s8[4194304]{0:T(1024)(128)(4,1)S(1)}, s32[]{:S(2)}) async-start(s8[8388608]{0:T(1024)(128)(4,1)} %bitcast.28), calls=%async_computation | async-start | bytes 8388608
  128.8 33.7 %slice-start.1 = ((s8[8388608]{0:T(1024)(128)(4,1)}), s8[4194304]{0:T(1024)(128)(4,1)S(1)}, s32[]{:S(2)}) async-start(s8[8388608]{0:T(1024)(128)(4,1)} %bitcast.28), calls=%async_computation.1 | async-start | bytes 8388608
  138.2 11.1 %collective-permute-start.23 = (bf16[2368,128]{1,0:T(8,128)(2,1)S(1)}, bf16[2368,128]{1,0:T(8,128)(2,1)S(1)}, u32[]{:S(2)}, u32[]{:S(2)}) collective-permute-start(bf16[2368,128]{1,0:T(8,128)(2,1)S(1)} %join.2.own), channel_id=1, source_target_pairs={{0,4},{1,3},{2,6},{3,1},{4,0},{5,7},{6,2},{7,5},{8,12},{9,11},{10,... | collective-permute-start | bytes 1818632 | tf_op jit(solution)/shard_map/ppermute | solution.py:543
  139.8 4.4 %collective-permute-start.15 = (bf16[192,128]{1,0:T(8,128)(2,1)S(1)}, bf16[192,128]{1,0:T(8,128)(2,1)S(1)}, u32[]{:S(2)}, u32[]{:S(2)}) collective-permute-start(bf16[192,128]{1,0:T(8,128)(2,1)S(1)} %get-tuple-element.138), channel_id=1, source_target_pairs={{0,8},{1,17},{2,10},{3,19},{4,12},{5,21},{6,14},{7,23},{8,0},{9,25... | collective-permute-start | bytes 147464 | tf_op jit(solution)/shard_map/ppermute | solution.py:543
  139.9 5.0 %collective-permute-start.19 = (bf16[192,128]{1,0:T(8,128)(2,1)S(1)}, bf16[192,128]{1,0:T(8,128)(2,1)S(1)}, u32[]{:S(2)}, u32[]{:S(2)}) collective-permute-start(bf16[192,128]{1,0:T(8,128)(2,1)S(1)} %get-tuple-element.144), channel_id=1, source_target_pairs={{0,16},{1,9},{2,18},{3,11},{4,20},{5,13},{6,22},{7,15},{8,24},{9,1... | collective-permute-start | bytes 147464 | tf_op jit(solution)/shard_map/ppermute | solution.py:543
  142.8 5.9 %collective-permute-start.20 = (bf16[192,128]{1,0:T(8,128)(2,1)S(1)}, bf16[192,128]{1,0:T(8,128)(2,1)S(1)}, u32[]{:S(2)}, u32[]{:S(2)}) collective-permute-start(bf16[192,128]{1,0:T(8,128)(2,1)S(1)} %get-tuple-element.139), channel_id=1, source_target_pairs={{0,24},{1,25},{2,26},{3,27},{4,28},{5,29},{6,30},{7,31},{8,16},{9,... | collective-permute-start | bytes 147464 | tf_op jit(solution)/shard_map/ppermute | solution.py:543
  144.1 4.5 %collective-permute-start.21 = (f32[32,128]{1,0:T(8,128)S(1)}, f32[32,128]{1,0:T(8,128)S(1)}, u32[]{:S(2)}, u32[]{:S(2)}) collective-permute-start(f32[32,128]{1,0:T(8,128)S(1)} %get-tuple-element.132.refs_3_), channel_id=1, source_target_pairs={{0,1},{1,0},{2,3},{3,2},{4,5},{5,4},{6,7},{7,6},{8,9},{9,8},{10,11... | collective-permute-start | bytes 49160 | tf_op jit(solution)/shard_map/ppermute | solution.py:515
  149.9 21.2 %collective-permute-start.27 = (bf16[4736,128]{1,0:T(8,128)(2,1)S(1)}, bf16[4736,128]{1,0:T(8,128)(2,1)S(1)}, u32[]{:S(2)}, u32[]{:S(2)}) collective-permute-start(bf16[4736,128]{1,0:T(8,128)(2,1)S(1)} %join.3.refs_0_), channel_id=1, source_target_pairs={{0,2},{1,5},{2,0},{3,7},{4,6},{5,1},{6,4},{7,3},{8,10},{9,13},{10,... | collective-permute-start | bytes 3637256 | tf_op jit(solution)/shard_map/ppermute | solution.py:543
  150.9 6.1 %collective-permute-start.25 = (bf16[256,128]{1,0:T(8,128)(2,1)S(1)}, bf16[256,128]{1,0:T(8,128)(2,1)S(1)}, u32[]{:S(2)}, u32[]{:S(2)}) collective-permute-start(bf16[256,128]{1,0:T(8,128)(2,1)S(1)} %settle_cols.1.refs_0_), channel_id=1, source_target_pairs={{0,24},{1,25},{2,26},{3,27},{4,28},{5,29},{6,30},{7,31},{8,16},{9,... | collective-permute-start | bytes 196616 | tf_op jit(solution)/shard_map/ppermute | solution.py:543
  153.2 5.2 %collective-permute-start.24 = (bf16[256,128]{1,0:T(8,128)(2,1)S(1)}, bf16[256,128]{1,0:T(8,128)(2,1)S(1)}, u32[]{:S(2)}, u32[]{:S(2)}) collective-permute-start(bf16[256,128]{1,0:T(8,128)(2,1)S(1)} %settle_cols.1.refs_0_), channel_id=1, source_target_pairs={{0,16},{1,9},{2,18},{3,11},{4,20},{5,13},{6,22},{7,15},{8,24},{9,1... | collective-permute-start | bytes 196616 | tf_op jit(solution)/shard_map/ppermute | solution.py:543
  153.2 5.2 %collective-permute-start.22 = (bf16[256,128]{1,0:T(8,128)(2,1)S(1)}, bf16[256,128]{1,0:T(8,128)(2,1)S(1)}, u32[]{:S(2)}, u32[]{:S(2)}) collective-permute-start(bf16[256,128]{1,0:T(8,128)(2,1)S(1)} %settle_cols.1.refs_0_), channel_id=1, source_target_pairs={{0,8},{1,17},{2,10},{3,19},{4,12},{5,21},{6,14},{7,23},{8,0},{9,25... | collective-permute-start | bytes 196616 | tf_op jit(solution)/shard_map/ppermute | solution.py:543
  158.9 15.3 %collective-permute-start.29 = (bf16[832,128]{1,0:T(8,128)(2,1)S(1)}, bf16[832,128]{1,0:T(8,128)(2,1)S(1)}, u32[]{:S(2)}, u32[]{:S(2)}) collective-permute-start(bf16[832,128]{1,0:T(8,128)(2,1)S(1)} %join_cols.1.refs_0_), channel_id=1, source_target_pairs={{0,6},{1,7},{2,4},{3,5},{4,2},{5,3},{6,0},{7,1},{8,14},{9,15},{10,... | collective-permute-start | bytes 638984 | tf_op jit(solution)/shard_map/ppermute | solution.py:543
  160.3 14.0 %collective-permute-start.28 = (bf16[832,128]{1,0:T(8,128)(2,1)S(1)}, bf16[832,128]{1,0:T(8,128)(2,1)S(1)}, u32[]{:S(2)}, u32[]{:S(2)}) collective-permute-start(bf16[832,128]{1,0:T(8,128)(2,1)S(1)} %join_cols.1.refs_0_), channel_id=1, source_target_pairs={{0,4},{1,3},{2,6},{3,1},{4,0},{5,7},{6,2},{7,5},{8,12},{9,11},{10,... | collective-permute-start | bytes 638984 | tf_op jit(solution)/shard_map/ppermute | solution.py:543
  161.6 14.1 %collective-permute-start.26 = (bf16[832,128]{1,0:T(8,128)(2,1)S(1)}, bf16[832,128]{1,0:T(8,128)(2,1)S(1)}, u32[]{:S(2)}, u32[]{:S(2)}) collective-permute-start(bf16[832,128]{1,0:T(8,128)(2,1)S(1)} %join_cols.1.refs_0_), channel_id=1, source_target_pairs={{0,2},{1,5},{2,0},{3,7},{4,6},{5,1},{6,4},{7,3},{8,10},{9,13},{10,... | collective-permute-start | bytes 638984 | tf_op jit(solution)/shard_map/ppermute | solution.py:543
  (6 other events, 106.6 us)

commit v5 on v4

--- a/solution.py
+++ b/solution.py
@@ -12,6 +12,7 @@
 LAT = 512
 AUG = 16
 EPS = 1e-05
+LOG2E = 1.4426950408889634
 NEG = -1e30
 BF = jnp.bfloat16
 F32 = jnp.float32
@@ -58,7 +59,7 @@
 
 def forward_kernel(
     tens, lens, x_ref, vecs, wq_own, wq_oth, wo_own, wo_oth,
-    n1_ref, qkv_ref, p_ref, att_ref, rl_ref, h1_ref, n2_ref,
+    n1_ref, qkv_ref, p_ref, att_ref, rl_ref, h1_ref, n2_ref, asked,
 ):
     scenes = pl.num_programs(0)
     length = lens[tens[0] * scenes + pl.program_id(0)]
@@ -70,7 +71,13 @@
 
     def project(side, t):
         part = nt((wq_own, wq_oth)[side][t * half:(t + 1) * half], n1)
+        part = part.astype(BF)
         if t == 0:
+            scaled = part.astype(F32) * (HD**-0.5 * LOG2E)
+            high = scaled.astype(BF)
+            at = slice(side * half, (side + 1) * half)
+            asked[0, at] = high
+            asked[1, at] = (scaled - high.astype(F32)).astype(BF)
             part = part * HD**-0.5
         qkv_ref[0, side, t] = part.astype(BF)
 
@@ -83,10 +90,12 @@
         return qkv_ref[0, h // heads, t, h % heads * HD:h % heads * HD + HD]
 
     def scores(h):
-        return tn(jnp.concatenate([part_of(1, h), bias], 0), jnp.concatenate([part_of(0, h), ones], 0))
+        k = part_of(1, h)
+        at = slice(h * HD, h * HD + HD)
+        return tn(jnp.concatenate([k, k, bias], 0), jnp.concatenate([asked[0, at], asked[1, at], ones], 0))
 
     def weights(h, s):
-        p = jnp.exp(s - jnp.max(s, 0, keepdims=True)).astype(BF)
+        p = jnp.exp2(s - jnp.max(s, 0, keepdims=True)).astype(BF)
         p_ref[0, h] = p
         return p
 
@@ -159,6 +168,7 @@
                 rowblock,
                 rowblock,
             ],
+            scratch_shapes=[pltpu.VMEM((2, 2 * half, LAT), BF)],
         ),
         out_shape=[
             pltpu.HBM((rows, D), BF),
@@ -175,7 +185,6 @@
     )(tens, *hbm(lens, x), vecs, *hbm(wq_own), wq_oth, *hbm(wo_own), wo_oth)
 
 
-LOG2E = 1.4426950408889634
 SUB = 256
 
 
@@ -198,7 +207,7 @@
 
 def mlp_kernel(
     tens, n2_ref, cot_ref, up_own, down_own, up_oth, down_oth, vecs_oth, vecs, h1_ref, att_ref, rl_ref, wo_own, wo_oth,
-    act_ref, gh_ref, doa_ref, own_ref, oth_ref, cols_ref, acc_up, acc_down, acc_ub, acc_wo,
+    act_ref, gh_ref, doa_ref, own_ref, oth_ref, cols_ref, dub_ref, acc_up, acc_down, acc_ub, acc_wo,
 ):
     @pl.when(pl.program_id(0) == 0)
     def _():
@@ -275,9 +284,9 @@
             put_slabs(ref, 0, acc_up.at[side * units:(side + 1) * units])
             put_slabs(ref, 4 * units, acc_down.at[side * units:(side + 1) * units])
             put_slabs(ref, 8 * units, acc_wo.at[side * half:(side + 1) * half])
-            put_row(ref, base, acc_ub[:, side * units:(side + 1) * units], 16)
-            if ref.shape[0] > base + 16:
-                ref[base + 16:] = jnp.zeros((ref.shape[0] - base - 16, 128), ref.dtype)
+            if ref.shape[0] > base:
+                ref[base:] = jnp.zeros((ref.shape[0] - base, 128), ref.dtype)
+        put_row(dub_ref, 0, acc_ub, dub_ref.shape[0])
 
 
 def mlp(tens, n2, cot, up, down, up_oth, down_oth, vecs_oth, vecs, h1, att, rl, wo, wo_oth, total_rows):
@@ -303,7 +312,7 @@
             out_specs=[
                 pl.BlockSpec((LAT, 2 * units), lambda i, *_: (i, 0)), rowblock,
                 pl.BlockSpec((1, heads, HD + AUG, LAT), lambda i, *_: (i, 0, 0, 0)),
-                whole((total_rows, 128)), whole((total_rows, 128)), whole((8, D)),
+                whole((total_rows, 128)), whole((total_rows, 128)), whole((8, D)), whole((2 * units // 128, 128)),
             ],
             scratch_shapes=[
                 pltpu.VMEM((2 * units, D), F32), pltpu.VMEM((2 * units, D), F32), pltpu.VMEM((1, 2 * units), F32),
@@ -317,6 +326,7 @@
             pltpu.HBM((total_rows, 128), BF),
             pltpu.HBM((total_rows, 128), BF),
             pltpu.HBM((8, D), F32),
+            pltpu.HBM((2 * units // 128, 128), F32),
         ],
         compiler_params=params(40),
         cost_estimate=takes(39),
@@ -459,7 +469,7 @@
     )(tens, *hbm(p, doa, qkv, n1), *carried)
 
 
-def norm_one_back_kernel(tens, dqkv, wq_own, wq_oth, x_ref, vecs, gh_ref, cols_two, gl_ref, cols_ref, acc):
+def norm_one_back_kernel(tens, dqkv, wq_own, wq_oth, x_ref, vecs, gh_ref, cols_two, dub, gl_ref, cols_ref, give_ref, acc):
     feats = wq_own.shape[0]
     g = tn(dqkv[0, 0].reshape(feats, LAT), wq_own[...]) + tn(dqkv[0, 1].reshape(feats, LAT), wq_oth[...])
     xh, r = normalised(x_ref[...].astype(F32))
@@ -477,11 +487,15 @@
     @pl.when(pl.program_id(0) == pl.num_programs(0) - 1)
     def _():
         total = acc[...]
-        for c in range(D // 128):
-            cols_ref[c * 8:c * 8 + 8] = total[:, c * 128:c * 128 + 128]
-
-
-def norm_one_back(tens, dqkv, wq_own, wq_oth, x, vecs, gh, cols_two):
+        units = dub.shape[0] // 2
+        for ref, at in ((cols_ref, 0), (give_ref, units)):
+            for c in range(D // 128):
+                ref[c * 8:c * 8 + 8] = total[:, c * 128:c * 128 + 128]
+            ref[32:] = dub[at:at + units]
+
+
+def norm_one_back(tens, dqkv, wq_own, wq_oth, x, vecs, gh, cols_two, dub):
+    cols = (4 * 8 + dub.shape[0] // 2, 128)
     scenes, half = dqkv.shape[0], dqkv.shape[3]
     rowblock = pl.BlockSpec((LAT, D), lambda i, *_: (i, 0))
     return pl.pallas_call(
@@ -495,16 +509,16 @@
                 pl.BlockSpec((LAT, D), lambda i, tens: (tens[0] * scenes + i, 0)),
                 vecs_spec(),
                 rowblock,
-                whole((8, D)),
+                whole((8, D)), whole(dub.shape),
             ],
-            out_specs=[rowblock, whole((32, 128))],
+            out_specs=[rowblock, whole(cols), whole(cols)],
             scratch_shapes=[pltpu.VMEM((8, D), F32)],
         ),
-        out_shape=[pltpu.HBM((scenes * LAT, D), F32), jax.ShapeDtypeStruct((32, 128), F32)],
+        out_shape=[pltpu.HBM((scenes * LAT, D), F32), jax.ShapeDtypeStruct(cols, F32), jax.ShapeDtypeStruct(cols, F32)],
         compiler_params=params(28),
         cost_estimate=takes(10),
         name="norm_one_back",
-    )(tens, *vmem(dqkv), wq_own, wq_oth, *hbm(x), vecs, *vmem(gh), cols_two)
+    )(tens, *vmem(dqkv), wq_own, wq_oth, *hbm(x), vecs, *vmem(gh), cols_two, dub)
 
 
 def tie(value, *after):
@@ -552,6 +566,7 @@
         out_shape=out_shape,
         scratch_shapes=list(scratch),
         compiler_params=pltpu.CompilerParams(vmem_limit_bytes=mib * MIB),
+        cost_estimate=takes(0.5),
         name=name,
     )(scalars, *arrays)
 
@@ -661,7 +676,7 @@
 
 
 def finish_mlp_kernel(scalars, *refs):
-    (own, *recvs), (dup, ddown, dwo, dub), full = refs[:-5], refs[-5:-1], refs[-1]
+    (own, *recvs), (dup, ddown, dwo), full = refs[:-4], refs[-4:-1], refs[-1]
     fill(full, scalars, own, recvs)
     units, half = dup.shape[0], dwo.shape[0]
     for c in range(D // 128):
@@ -669,8 +684,6 @@
         dup[:, at] = full[c * units:(c + 1) * units].astype(F32)
         ddown[:, at] = full[(4 + c) * units:(5 + c) * units].astype(F32)
         dwo[:, at] = full[8 * units + c * half:8 * units + (c + 1) * half].astype(F32)
-    base = 8 * units + 4 * half
-    dub[...] = full[base:base + dub.shape[0]].astype(F32)
 
 
 def finish_mlp(own, recvs, stage, units, half):
@@ -678,7 +691,7 @@
         finish_mlp_kernel,
         [
             jax.ShapeDtypeStruct((units, D), F32), jax.ShapeDtypeStruct((units, D), F32),
-            jax.ShapeDtypeStruct((half, D), F32), jax.ShapeDtypeStruct((units // 128, 128), F32),
+            jax.ShapeDtypeStruct((half, D), F32),
         ],
         "finish_mlp", stage.scalars, own, *recvs, scratch=[pltpu.VMEM((stage.size * own.shape[0], 128), BF)],
     )
@@ -798,9 +811,9 @@
     n1, qkv, p, att, rl, h1, n2 = attention_forward(
         tens, scene_len, latents, vecs, wq, wq_oth, out_weight, wo_oth, rows
     )
-    need = 8 * units + 4 * half + 16
+    need = 8 * units + 4 * half
     total_rows = -(-need // (16 * count)) * 16 * count
-    act, gh, doa, grads_own, grads_oth, cols_two = mlp(
+    act, gh, doa, grads_own, grads_oth, cols_two, grad_ub = mlp(
         tens, n2, cotangent, up_weight, down_weight, up_oth, down_oth, vecs_oth, vecs, h1, att, rl, out_weight, wo_oth, total_rows
     )
     from_peer = swap(grads_oth)
@@ -823,7 +836,7 @@
         return have, recvs
 
     qkv_rows = -(-12 * half // (16 * count)) * 16 * count
-    extra = 64
+    extra = 2 * (4 * 8 + units // 128)
     dqkv, dw, qkv_peer = None, None, None
     token = grads_oth
     chains, results = {}, {}
@@ -857,10 +870,10 @@
             )
             token = next(chains["qkv"])
         elif action == "norm":
-            grad_latents, cols_one = norm_one_back(
-                tie(tens, token), dqkv, wq, wq_oth, latents, vecs, gh, cols_two
+            grad_latents, cols_one, cols_give = norm_one_back(
+                tie(tens, token), dqkv, wq, wq_oth, latents, vecs, gh, cols_two, grad_ub
             )
-            cols.extend((cols_one, swap(cols_one)))
+            cols.extend((cols_one, swap(cols_give)))
             token = cols_one
         elif action == "out":
             out = block_out(tie(tens, token), act, down_weight, down_oth, vecs, h1)
@@ -869,14 +882,15 @@
             while "mlp" not in results:
                 token = step("mlp")
             have, recvs = results["mlp"]
-            dup, ddown, dwo, dub = finish_mlp(tie(have, token), recvs, mlp_stages[0], units, half)
-            token = dub
+            dup, ddown, dwo = finish_mlp(tie(have, token), recvs, mlp_stages[0], units, half)
+            token = dwo
         else:
             token = step(action[:3])
     while "qkv" not in results:
         token = step("qkv")
     dwq, shared = finish_qkv(*results["qkv"], qkv_stages[0], half, extra)
-    shared = shared.reshape(D // 128, 8, 128).transpose(1, 0, 2).reshape(8, D)
+    dub = shared[32:]
+    shared = shared[:32].reshape(D // 128, 8, 128).transpose(1, 0, 2).reshape(8, D)
     return (
         out, grad_latents, shared[0], shared[1], dwq, dwo, shared[4],
         shared[2], shared[3], dup, dub.reshape(units), ddown, shared[5],

time: 179 us -> 177 us (0.989)
  transfers between devices with their start and end apart: 30 -> 30, of which waited for: 9 -> 9; matrix products, arithmetic and copies ran while one was open for 0% -> 0% of each run, Pallas kernels for 45% -> 44%
where the time goes in v5:
time: 177 us; the launch traced here: 176 us
  Pallas kernels  123 us (69%)
  starting transfers between devices  34.1 us (19%)
  waiting for transfers between devices  17 us (10%)
    pallas_call x1, Pallas kernels, mlp(): pl.pallas_call(mlp_kernel, grid_spec=pltpu.PrefetchScalarGridSpec(num_sca...  38.2 us
    pallas_call x4, Pallas kernels, attention_back(): pl.pallas_call(functools.partial(back_kernel, ends=ends), grid_spec=pltpu...  33.2 us
    ppermute x22, starting transfers between devices, exchange(): out.append(lax.ppermute(v, ('dp', 'tensor'), pairs))  31.9 us
    pallas_call x1, Pallas kernels, attention_forward(): pl.pallas_call(forward_kernel, grid_spec=pltpu.PrefetchScalarGridSpec(num...  21.7 us
    ppermute x22, waiting for transfers between devices, exchange(): out.append(lax.ppermute(v, ('dp', 'tensor'), pairs))  16.4 us
    pallas_call x12, Pallas kernels, small_call(): pl.pallas_call(kernel, in_specs=[pl.BlockSpec(memory_space=pltpu.SMEM)] +...  13.5 us
    pallas_call x1, Pallas kernels, norm_one_back(): pl.pallas_call(norm_one_back_kernel, grid_spec=pltpu.PrefetchScalarGridSp...  8.03 us
    pallas_call x1, Pallas kernels, block_out(): pl.pallas_call(block_out_kernel, grid_spec=pltpu.PrefetchScalarGridSpec(n...  7.26 us
  transfers between devices with their start and end apart: 30, of which 9 were waited for; matrix products, arithmetic and copies ran while one was open for 0% of the time, Pallas kernels for 44%

profile of v5, /device:TPU:0, one launch (start us, length us, event | category | flops | bytes accessed | tf_op | source)
XLA Modules:
  0.0 176.4 jit_solution(18006143311827172261)
XLA Ops:
  3.7 21.7 %attention_forward.1 = (bf16[2048,512]{1,0:T(8,128)(2,1)}, bf16[4,2,3,256,512]{4,3,2,1,0:T(8,128)(2,1)}, bf16[4,8,512,512]{3,2,1,0:T(8,128)(2,1)}, bf16[4,512,51...) custom-call(s32[1]{0:T(128)} %bitcast.tens, s32[8]{0:T(128)} %lens.1, ...), custom_call_target="tpu_custom_call" | custom-call | flops 23000000512 | tf_op jit(solution)/shard_map/attention_forward/pallas_call | solution.py:153
  25.4 38.2 %mlp.1 = (bf16[2048,2048]{1,0:T(8,128)(2,1)}, f32[2048,512]{1,0:T(8,128)}, bf16[4,8,80,512]{3,2,1,0:T(8,128)(2,1)}, bf16[9216,128]{1,0:T(8,128)(2,1)}, bf16[9216...) custom-call(s32[1]{0:T(128)} %bitcast.tens, bf16[2048,512]{1,0:T(8,128)(2,1)} %get-tuple-element.90.n2_ref, ...), custom_call_target="tpu_custom_call" | custom-call | flops 38999998464 | tf_op jit(solution)/shard_map/mlp/pallas_call | solution.py:299
  64.4 5.7 %attention_back.4 = (bf16[4,2,3,256,512]{4,3,2,1,0:T(8,128)(2,1)S(1)}, f32[1,3,256,512]{3,2,1,0:T(8,128)}) custom-call(s32[1]{0:T(128)} %bitcast.tens, bf16[4,8,512,512]{3,2,1,0:T(8,128)(2,1)} %get-tuple-element.97.p_ref, bf16[4,8,80,512]{3,2,1,0:T(8,128)(2,1)} %get-tuple-element.98.doa_ref, bf16[4,2,3,256,512]{4,3,2,1,0:T(8,128)(2,1)} %get-tuple-element.99.qkv_ref, ...), custom_call_target="tpu_custom_call" | custom-call | flops 4499999744 | tf_op jit(solution)/shard_map/attention_back/pallas_call | solution.py:450
  70.2 2.2 %split_mlp.1 = (f32[4608,128]{1,0:T(8,128)S(1)}, bf16[4608,128]{1,0:T(8,128)(2,1)S(1)}) custom-call(s32[2]{0:T(128)S(1)} %pad_add_fusion.3.scalars, bf16[9216,128]{1,0:T(8,128)(2,1)} %get-tuple-element.94.own, bf16[9216,128]{1,0:T(8,128)(2,1)S(1)} %collective-permute-done.5.recv), custom_call_target="tpu_custom_call" | custom-call | flops 500000000 | tf_op jit(solution)/shard_map/split_mlp/pallas_call | solution.py:562
  72.3 2.7 %collective-permute-start.6 = (bf16[4608,128]{1,0:T(8,128)(2,1)S(1)}, bf16[4608,128]{1,0:T(8,128)(2,1)S(1)}, u32[]{:S(2)}, u32[]{:S(2)}) collective-permute-start(bf16[4608,128]{1,0:T(8,128)(2,1)S(1)} %get-tuple-element.104), channel_id=1, source_target_pairs={{0,2},{1,5},{2,0},{3,7},{4,6},{5,1},{6,4},{7,3},{8,10},{9,13},{10,... | collective-permute-start | bytes 3538952 | tf_op jit(solution)/shard_map/ppermute | solution.py:557
  75.0 10.7 %attention_back.5 = (bf16[4,2,3,256,512]{4,3,2,1,0:T(8,128)(2,1)S(1)}, bf16[3072,128]{1,0:T(8,128)(2,1)S(1)}) custom-call(s32[1]{0:T(128)} %bitcast.tens, bf16[4,8,512,512]{3,2,1,0:T(8,128)(2,1)} %get-tuple-element.97.p_ref, bf16[4,8,80,512]{3,2,1,0:T(8,128)(2,1)} %get-tuple-element.98.doa_ref, ...), custom_call_target="tpu_custom_call", output_to_operand_aliasing={{0}: (6, {})} | custom-call | flops 13500000256 | tf_op jit(solution)/shard_map/attention_back/pallas_call | solution.py:450
  85.9 3.3 %collective-permute-done.6.refs_1_ = bf16[4608,128]{1,0:T(8,128)(2,1)S(1)} collective-permute-done((bf16[4608,128]{1,0:T(8,128)(2,1)S(1)}, bf16[4608,128]{1,0:T(8,128)(2,1)S(1)}, u32[]{:S(2)}, u32[]{:S(2)}) %collective-permute-start.6) | collective-permute-done | bytes 1179680 | tf_op jit(solution)/shard_map/ppermute | solution.py:557
  89.2 1.0 split.4
  90.2 2.1 %collective-permute-start.7 = (bf16[2304,128]{1,0:T(8,128)(2,1)S(1)}, bf16[2304,128]{1,0:T(8,128)(2,1)S(1)}, u32[]{:S(2)}, u32[]{:S(2)}) collective-permute-start(bf16[2304,128]{1,0:T(8,128)(2,1)S(1)} %get-tuple-element.110), channel_id=1, source_target_pairs={{0,4},{1,3},{2,6},{3,1},{4,0},{5,7},{6,2},{7,5},{8,12},{9,11},{10,... | collective-permute-start | bytes 1769480 | tf_op jit(solution)/shard_map/ppermute | solution.py:557
  92.3 8.6 %attention_back.6 = (bf16[4,2,3,256,512]{4,3,2,1,0:T(8,128)(2,1)S(1)}, f32[1,3,256,512]{3,2,1,0:T(8,128)}) custom-call(s32[1]{0:T(128)} %bitcast.tens, bf16[4,8,512,512]{3,2,1,0:T(8,128)(2,1)} %get-tuple-element.97.p_ref, bf16[4,8,80,512]{3,2,1,0:T(8,128)(2,1)} %get-tuple-element.98.doa_ref, ...), custom_call_target="tpu_custom_call", output_to_operand_aliasing={{0}: (5, {})} | custom-call | flops 8999999488 | tf_op jit(solution)/shard_map/attention_back/pallas_call | solution.py:450
  101.6 3.7 %collective-permute-start.10 = (bf16[576,128]{1,0:T(8,128)(2,1)S(1)}, bf16[576,128]{1,0:T(8,128)(2,1)S(1)}, u32[]{:S(2)}, u32[]{:S(2)}) collective-permute-start(bf16[576,128]{1,0:T(8,128)(2,1)S(1)} %get-tuple-element.115), channel_id=1, source_target_pairs={{0,24},{1,25},{2,26},{3,27},{4,28},{5,29},{6,30},{7,31},{8,16},{9,... | collective-permute-start | bytes 442376 | tf_op jit(solution)/shard_map/ppermute | solution.py:557
  106.1 8.2 %attention_back.7 = (bf16[4,2,3,256,512]{4,3,2,1,0:T(8,128)(2,1)S(1)}, f32[3072,128]{1,0:T(8,128)S(1)}) custom-call(s32[1]{0:T(128)} %bitcast.tens, bf16[4,8,512,512]{3,2,1,0:T(8,128)(2,1)} %get-tuple-element.97.p_ref, bf16[4,8,80,512]{3,2,1,0:T(8,128)(2,1)} %get-tuple-element.98.doa_ref, ...), custom_call_target="tpu_custom_call", output_to_operand_aliasing={{0}: (6, {})} | custom-call | flops 8999999488 | tf_op jit(solution)/shard_map/attention_back/pallas_call | solution.py:450
  114.3 2.8 %collective-permute-done.9.refs_1_ = bf16[576,128]{1,0:T(8,128)(2,1)S(1)} collective-permute-done((bf16[576,128]{1,0:T(8,128)(2,1)S(1)}, bf16[576,128]{1,0:T(8,128)(2,1)S(1)}, u32[]{:S(2)}, u32[]{:S(2)}) %collective-permute-start.9) | collective-permute-done | bytes 147488 | tf_op jit(solution)/shard_map/ppermute | solution.py:557
  119.4 2.5 %collective-permute-start.18 = (bf16[576,128]{1,0:T(8,128)(2,1)S(1)}, bf16[576,128]{1,0:T(8,128)(2,1)S(1)}, u32[]{:S(2)}, u32[]{:S(2)}) collective-permute-start(bf16[576,128]{1,0:T(8,128)(2,1)S(1)} %settle.1.own), channel_id=1, source_target_pairs={{0,24},{1,25},{2,26},{3,27},{4,28},{5,29},{6,30},{7,31},{8,16},{9,... | collective-permute-start | bytes 442376 | tf_op jit(solution)/shard_map/ppermute | solution.py:557
  121.9 1.9 %collective-permute-start.16 = (bf16[576,128]{1,0:T(8,128)(2,1)S(1)}, bf16[576,128]{1,0:T(8,128)(2,1)S(1)}, u32[]{:S(2)}, u32[]{:S(2)}) collective-permute-start(bf16[576,128]{1,0:T(8,128)(2,1)S(1)} %settle.1.own), channel_id=1, source_target_pairs={{0,8},{1,17},{2,10},{3,19},{4,12},{5,21},{6,14},{7,23},{8,0},{9,25... | collective-permute-start | bytes 442376 | tf_op jit(solution)/shard_map/ppermute | solution.py:557
  123.8 2.2 %collective-permute-start.14 = (bf16[768,128]{1,0:T(8,128)(2,1)S(1)}, bf16[768,128]{1,0:T(8,128)(2,1)S(1)}, u32[]{:S(2)}, u32[]{:S(2)}) collective-permute-start(bf16[768,128]{1,0:T(8,128)(2,1)S(1)} %get-tuple-element.128), channel_id=1, source_target_pairs={{0,6},{1,7},{2,4},{3,5},{4,2},{5,3},{6,0},{7,1},{8,14},{9,15},{10,... | collective-permute-start | bytes 589832 | tf_op jit(solution)/shard_map/ppermute | solution.py:557
  126.6 8.0 %norm_one_back.1 = (f32[2048,512]{1,0:T(8,128)}, f32[40,128]{1,0:T(8,128)S(1)}, f32[40,128]{1,0:T(8,128)S(1)}) custom-call(s32[1]{0:T(128)} %bitcast.tens, bf16[4,2,3,256,512]{4,3,2,1,0:T(8,128)(2,1)S(1)} %get-tuple-element.130.dqkv, bf16[768,512]{1,0:T(8,128)(2,1)S(1)} %bitcast.28, bf16[768,512]{1,0:T(8,128)(2,1)S(1)} %copy-done.3, ...), custom_call_target="tpu_custom_call" | custom-call | flops 10000000000 | tf_op jit(solution)/shard_map/norm_one_back/pallas_call | solution.py:501
  135.9 1.6 collective-permute-start.23
  137.6 2.9 %collective-permute-start.19 = (bf16[192,128]{1,0:T(8,128)(2,1)S(1)}, bf16[192,128]{1,0:T(8,128)(2,1)S(1)}, u32[]{:S(2)}, u32[]{:S(2)}) collective-permute-start(bf16[192,128]{1,0:T(8,128)(2,1)S(1)} %get-tuple-element.146), channel_id=1, source_target_pairs={{0,16},{1,9},{2,18},{3,11},{4,20},{5,13},{6,22},{7,15},{8,24},{9,1... | collective-permute-start | bytes 147464 | tf_op jit(solution)/shard_map/ppermute | solution.py:557
  140.5 1.3 collective-permute-start.20
  142.6 3.8 %collective-permute-done.20.refs_2_ = bf16[192,128]{1,0:T(8,128)(2,1)S(1)} collective-permute-done((bf16[192,128]{1,0:T(8,128)(2,1)S(1)}, bf16[192,128]{1,0:T(8,128)(2,1)S(1)}, u32[]{:S(2)}, u32[]{:S(2)}) %collective-permute-start.20) | collective-permute-done | bytes 49184 | tf_op jit(solution)/shard_map/ppermute | solution.py:557
  148.5 2.1 %collective-permute-start.25 = (bf16[272,128]{1,0:T(8,128)(2,1)S(1)}, bf16[272,128]{1,0:T(8,128)(2,1)S(1)}, u32[]{:S(2)}, u32[]{:S(2)}) collective-permute-start(bf16[272,128]{1,0:T(8,128)(2,1)S(1)} %settle_cols.1.refs_0_), channel_id=1, source_target_pairs={{0,24},{1,25},{2,26},{3,27},{4,28},{5,29},{6,30},{7,31},{8,16},{9,... | collective-permute-start | bytes 208904 | tf_op jit(solution)/shard_map/ppermute | solution.py:557
  150.6 2.3 %collective-permute-start.22 = (bf16[272,128]{1,0:T(8,128)(2,1)S(1)}, bf16[272,128]{1,0:T(8,128)(2,1)S(1)}, u32[]{:S(2)}, u32[]{:S(2)}) collective-permute-start(bf16[272,128]{1,0:T(8,128)(2,1)S(1)} %settle_cols.1.refs_0_), channel_id=1, source_target_pairs={{0,8},{1,17},{2,10},{3,19},{4,12},{5,21},{6,14},{7,23},{8,0},{9,25... | collective-permute-start | bytes 208904 | tf_op jit(solution)/shard_map/ppermute | solution.py:557
  152.9 1.7 collective-permute-done.25.refs_3_
  154.6 1.5 collective-permute-done.24.refs_2_
  156.7 1.3 collective-permute-start.29
  158.0 1.5 collective-permute-start.28
  160.3 7.3 %block_out.1 = bf16[2048,512]{1,0:T(8,128)(2,1)} custom-call(s32[1]{0:T(128)} %bitcast.tens, bf16[2048,2048]{1,0:T(8,128)(2,1)S(1)} %bitcast.30, bf16[1024,512]{1,0:T(8,128)(2,1)S(1)} %copy-done, bf16[1024,512]{1,0:T(8,128)(2,1)S(1)} %collective-permute-done.3.down_oth, f32[8,512]{1,0:T(8,128)S(1)} %rows_of.1.vecs, f32[2048,512]{1,0:T(8,128)} %get-tuple-element.91.h1_ref), custom_call_target="tpu_custom_call" | custom-call | flops 7000000000 | tf_op jit(solution)/shard_map/block_out/pallas_call | solution.py:347
  167.5 1.1 collective-permute-done.27.refs_1_
  168.6 3.2 %finish_mlp.1 = (f32[1024,512]{1,0:T(8,128)}, f32[1024,512]{1,0:T(8,128)}, f32[256,512]{1,0:T(8,128)}) custom-call(s32[2]{0:T(128)S(1)} %pad_add_fusion.3.scalars, bf16[4608,128]{1,0:T(8,128)(2,1)S(1)} %join.3.refs_0_, bf16[4608,128]{1,0:T(8,128)(2,1)S(1)} %collective-permute-done.27.refs_1_), custom_call_target="tpu_custom_call" | custom-call | flops 500000000 | tf_op jit(solution)/shard_map/finish_mlp/pallas_call | solution.py:562
  171.7 1.5 collective-permute-done.26.refs_1_
  173.2 2.0 %finish_qkv.1 = (f32[3,256,512]{2,1,0:T(8,128)}, f32[40,128]{1,0:T(8,128)S(1)}) custom-call(s32[4]{0:T(128)S(1)} %pad_add_fusion.1.scalars, bf16[848,128]{1,0:T(8,128)(2,1)S(1)} %join_cols.1.refs_0_, bf16[848,128]{1,0:T(8,128)(2,1)S(1)} %collective-permute-done.26.refs_1_, bf16[848,128]{1,0:T(8,128)(2,1)S(1)} %collective-permute-done.28.refs_2_, ...), custom_call_target="tpu_custom_call" | custom-call | flops 500000000 | tf_op jit(solution)/shard_map/finish_qkv/pallas_call | solution.py:562
  (75 shorter events, 15.0 us)
Async XLA Ops:
  0.6 3.0 %collective-permute-start = (bf16[768,512]{1,0:T(8,128)(2,1)}, bf16[768,512]{1,0:T(8,128)(2,1)S(1)}, u32[]{:S(2)}, u32[]{:S(2)}) collective-permute-start(bf16[768,512]{1,0:T(8,128)(2,1)} %bitcast.26), channel_id=1, source_target_pairs={{0,1},{1,0},{2,3},{3,2},{4,5},{5,4},{6,7},{7,6},{8,9},{9,8},{10,11... | collective-permute-start | bytes 2359304 | tf_op jit(solution)/shard_map/ppermute | solution.py:529
  1.2 2.5 %collective-permute-start.1 = (bf16[256,512]{1,0:T(8,128)(2,1)}, bf16[256,512]{1,0:T(8,128)(2,1)S(1)}, u32[]{:S(2)}, u32[]{:S(2)}) collective-permute-start(bf16[256,512]{1,0:T(8,128)(2,1)} %wo_own.3), channel_id=1, source_target_pairs={{0,1},{1,0},{2,3},{3,2},{4,5},{5,4},{6,7},{7,6},{8,9},{9,8},{10,11... | collective-permute-start | bytes 786440 | tf_op jit(solution)/shard_map/ppermute | solution.py:529
  2.1 23.3 %collective-permute-start.4 = (f32[8,512]{1,0:T(8,128)S(1)}, f32[8,512]{1,0:T(8,128)S(1)}, u32[]{:S(2)}, u32[]{:S(2)}) collective-permute-start(f32[8,512]{1,0:T(8,128)S(1)} %rows_of.1.vecs), channel_id=1, source_target_pairs={{0,1},{1,0},{2,3},{3,2},{4,5},{5,4},{6,7},{7,6},{8,9},{9,8},{10,11... | collective-permute-start | bytes 49160 | tf_op jit(solution)/shard_map/ppermute | solution.py:529
  2.6 22.8 %collective-permute-start.2 = (bf16[1024,512]{1,0:T(8,128)(2,1)}, bf16[1024,512]{1,0:T(8,128)(2,1)S(1)}, u32[]{:S(2)}, u32[]{:S(2)}) collective-permute-start(bf16[1024,512]{1,0:T(8,128)(2,1)} %up_own.1), channel_id=1, source_target_pairs={{0,1},{1,0},{2,3},{3,2},{4,5},{5,4},{6,7},{7,6},{8,9},{9,8},{10,11... | collective-permute-start | bytes 3145736 | tf_op jit(solution)/shard_map/ppermute | solution.py:529
  2.7 22.8 %collective-permute-start.3 = (bf16[1024,512]{1,0:T(8,128)(2,1)}, bf16[1024,512]{1,0:T(8,128)(2,1)S(1)}, u32[]{:S(2)}, u32[]{:S(2)}) collective-permute-start(bf16[1024,512]{1,0:T(8,128)(2,1)} %down_own.3), channel_id=1, source_target_pairs={{0,1},{1,0},{2,3},{3,2},{4,5},{5,4},{6,7},{7,6},{8,9},{9,8},{10,11... | collective-permute-start | bytes 3145736 | tf_op jit(solution)/shard_map/ppermute | solution.py:529
  63.7 6.5 %collective-permute-start.5 = (bf16[9216,128]{1,0:T(8,128)(2,1)}, bf16[9216,128]{1,0:T(8,128)(2,1)S(1)}, u32[]{:S(2)}, u32[]{:S(2)}) collective-permute-start(bf16[9216,128]{1,0:T(8,128)(2,1)} %get-tuple-element.95), channel_id=1, source_target_pairs={{0,1},{1,0},{2,3},{3,2},{4,5},{5,4},{6,7},{7,6},{8,9},{9,8},{10,11... | collective-permute-start | bytes 7077896 | tf_op jit(solution)/shard_map/ppermute | solution.py:529
  72.3 16.9 %collective-permute-start.6 = (bf16[4608,128]{1,0:T(8,128)(2,1)S(1)}, bf16[4608,128]{1,0:T(8,128)(2,1)S(1)}, u32[]{:S(2)}, u32[]{:S(2)}) collective-permute-start(bf16[4608,128]{1,0:T(8,128)(2,1)S(1)} %get-tuple-element.104), channel_id=1, source_target_pairs={{0,2},{1,5},{2,0},{3,7},{4,6},{5,1},{6,4},{7,3},{8,10},{9,13},{10,... | collective-permute-start | bytes 3538952 | tf_op jit(solution)/shard_map/ppermute | solution.py:557
  85.8 32.0 %collective-permute-start.11 = (bf16[3072,128]{1,0:T(8,128)(2,1)S(1)}, bf16[3072,128]{1,0:T(8,128)(2,1)S(1)}, u32[]{:S(2)}, u32[]{:S(2)}) collective-permute-start(bf16[3072,128]{1,0:T(8,128)(2,1)S(1)} %get-tuple-element.107), channel_id=1, source_target_pairs={{0,1},{1,0},{2,3},{3,2},{4,5},{5,4},{6,7},{7,6},{8,9},{9,8},{10,11... | collective-permute-start | bytes 2359304 | tf_op jit(solution)/shard_map/ppermute | solution.py:529
  90.2 10.7 %collective-permute-start.7 = (bf16[2304,128]{1,0:T(8,128)(2,1)S(1)}, bf16[2304,128]{1,0:T(8,128)(2,1)S(1)}, u32[]{:S(2)}, u32[]{:S(2)}) collective-permute-start(bf16[2304,128]{1,0:T(8,128)(2,1)S(1)} %get-tuple-element.110), channel_id=1, source_target_pairs={{0,4},{1,3},{2,6},{3,1},{4,0},{5,7},{6,2},{7,5},{8,12},{9,11},{10,... | collective-permute-start | bytes 1769480 | tf_op jit(solution)/shard_map/ppermute | solution.py:557
  101.6 15.5 %collective-permute-start.10 = (bf16[576,128]{1,0:T(8,128)(2,1)S(1)}, bf16[576,128]{1,0:T(8,128)(2,1)S(1)}, u32[]{:S(2)}, u32[]{:S(2)}) collective-permute-start(bf16[576,128]{1,0:T(8,128)(2,1)S(1)} %get-tuple-element.115), channel_id=1, source_target_pairs={{0,24},{1,25},{2,26},{3,27},{4,28},{5,29},{6,30},{7,31},{8,16},{9,... | collective-permute-start | bytes 442376 | tf_op jit(solution)/shard_map/ppermute | solution.py:557
  105.3 9.1 %collective-permute-start.8 = (bf16[576,128]{1,0:T(8,128)(2,1)S(1)}, bf16[576,128]{1,0:T(8,128)(2,1)S(1)}, u32[]{:S(2)}, u32[]{:S(2)}) collective-permute-start(bf16[576,128]{1,0:T(8,128)(2,1)S(1)} %get-tuple-element.120), channel_id=1, source_target_pairs={{0,8},{1,17},{2,10},{3,19},{4,12},{5,21},{6,14},{7,23},{8,0},{9,25... | collective-permute-start | bytes 442376 | tf_op jit(solution)/shard_map/ppermute | solution.py:557
  105.3 11.8 %collective-permute-start.9 = (bf16[576,128]{1,0:T(8,128)(2,1)S(1)}, bf16[576,128]{1,0:T(8,128)(2,1)S(1)}, u32[]{:S(2)}, u32[]{:S(2)}) collective-permute-start(bf16[576,128]{1,0:T(8,128)(2,1)S(1)} %get-tuple-element.122), channel_id=1, source_target_pairs={{0,16},{1,9},{2,18},{3,11},{4,20},{5,13},{6,22},{7,15},{8,24},{9,1... | collective-permute-start | bytes 442376 | tf_op jit(solution)/shard_map/ppermute | solution.py:557
  117.8 42.5 %slice-start = ((s8[8388608]{0:T(1024)(128)(4,1)}), s8[4194304]{0:T(1024)(128)(4,1)S(1)}, s32[]{:S(2)}) async-start(s8[8388608]{0:T(1024)(128)(4,1)} %bitcast.29), calls=%async_computation | async-start | bytes 8388608
  118.6 7.4 %collective-permute-start.12 = (bf16[768,128]{1,0:T(8,128)(2,1)S(1)}, bf16[768,128]{1,0:T(8,128)(2,1)S(1)}, u32[]{:S(2)}, u32[]{:S(2)}) collective-permute-start(bf16[768,128]{1,0:T(8,128)(2,1)S(1)} %get-tuple-element.127), channel_id=1, source_target_pairs={{0,2},{1,5},{2,0},{3,7},{4,6},{5,1},{6,4},{7,3},{8,10},{9,13},{10,... | collective-permute-start | bytes 589832 | tf_op jit(solution)/shard_map/ppermute | solution.py:557
  119.4 15.9 %collective-permute-start.18 = (bf16[576,128]{1,0:T(8,128)(2,1)S(1)}, bf16[576,128]{1,0:T(8,128)(2,1)S(1)}, u32[]{:S(2)}, u32[]{:S(2)}) collective-permute-start(bf16[576,128]{1,0:T(8,128)(2,1)S(1)} %settle.1.own), channel_id=1, source_target_pairs={{0,24},{1,25},{2,26},{3,27},{4,28},{5,29},{6,30},{7,31},{8,16},{9,... | collective-permute-start | bytes 442376 | tf_op jit(solution)/shard_map/ppermute | solution.py:557
  121.9 13.4 %collective-permute-start.17 = (bf16[576,128]{1,0:T(8,128)(2,1)S(1)}, bf16[576,128]{1,0:T(8,128)(2,1)S(1)}, u32[]{:S(2)}, u32[]{:S(2)}) collective-permute-start(bf16[576,128]{1,0:T(8,128)(2,1)S(1)} %settle.1.own), channel_id=1, source_target_pairs={{0,16},{1,9},{2,18},{3,11},{4,20},{5,13},{6,22},{7,15},{8,24},{9,1... | collective-permute-start | bytes 442376 | tf_op jit(solution)/shard_map/ppermute | solution.py:557
  121.9 13.4 %collective-permute-start.16 = (bf16[576,128]{1,0:T(8,128)(2,1)S(1)}, bf16[576,128]{1,0:T(8,128)(2,1)S(1)}, u32[]{:S(2)}, u32[]{:S(2)}) collective-permute-start(bf16[576,128]{1,0:T(8,128)(2,1)S(1)} %settle.1.own), channel_id=1, source_target_pairs={{0,8},{1,17},{2,10},{3,19},{4,12},{5,21},{6,14},{7,23},{8,0},{9,25... | collective-permute-start | bytes 442376 | tf_op jit(solution)/shard_map/ppermute | solution.py:557
  123.8 10.8 %collective-permute-start.14 = (bf16[768,128]{1,0:T(8,128)(2,1)S(1)}, bf16[768,128]{1,0:T(8,128)(2,1)S(1)}, u32[]{:S(2)}, u32[]{:S(2)}) collective-permute-start(bf16[768,128]{1,0:T(8,128)(2,1)S(1)} %get-tuple-element.128), channel_id=1, source_target_pairs={{0,6},{1,7},{2,4},{3,5},{4,2},{5,3},{6,0},{7,1},{8,14},{9,15},{10,... | collective-permute-start | bytes 589832 | tf_op jit(solution)/shard_map/ppermute | solution.py:557
  126.0 8.6 %collective-permute-start.13 = (bf16[768,128]{1,0:T(8,128)(2,1)S(1)}, bf16[768,128]{1,0:T(8,128)(2,1)S(1)}, u32[]{:S(2)}, u32[]{:S(2)}) collective-permute-start(bf16[768,128]{1,0:T(8,128)(2,1)S(1)} %get-tuple-element.136), channel_id=1, source_target_pairs={{0,4},{1,3},{2,6},{3,1},{4,0},{5,7},{6,2},{7,5},{8,12},{9,11},{10,... | collective-permute-start | bytes 589832 | tf_op jit(solution)/shard_map/ppermute | solution.py:557
  126.6 33.7 %slice-start.1 = ((s8[8388608]{0:T(1024)(128)(4,1)}), s8[4194304]{0:T(1024)(128)(4,1)S(1)}, s32[]{:S(2)}) async-start(s8[8388608]{0:T(1024)(128)(4,1)} %bitcast.29), calls=%async_computation.1 | async-start | bytes 8388608
  135.9 11.1 %collective-permute-start.23 = (bf16[2304,128]{1,0:T(8,128)(2,1)S(1)}, bf16[2304,128]{1,0:T(8,128)(2,1)S(1)}, u32[]{:S(2)}, u32[]{:S(2)}) collective-permute-start(bf16[2304,128]{1,0:T(8,128)(2,1)S(1)} %join.2.own), channel_id=1, source_target_pairs={{0,4},{1,3},{2,6},{3,1},{4,0},{5,7},{6,2},{7,5},{8,12},{9,11},{10,... | collective-permute-start | bytes 1769480 | tf_op jit(solution)/shard_map/ppermute | solution.py:557
  137.5 4.4 %collective-permute-start.15 = (bf16[192,128]{1,0:T(8,128)(2,1)S(1)}, bf16[192,128]{1,0:T(8,128)(2,1)S(1)}, u32[]{:S(2)}, u32[]{:S(2)}) collective-permute-start(bf16[192,128]{1,0:T(8,128)(2,1)S(1)} %get-tuple-element.140), channel_id=1, source_target_pairs={{0,8},{1,17},{2,10},{3,19},{4,12},{5,21},{6,14},{7,23},{8,0},{9,25... | collective-permute-start | bytes 147464 | tf_op jit(solution)/shard_map/ppermute | solution.py:557
  137.6 5.0 %collective-permute-start.19 = (bf16[192,128]{1,0:T(8,128)(2,1)S(1)}, bf16[192,128]{1,0:T(8,128)(2,1)S(1)}, u32[]{:S(2)}, u32[]{:S(2)}) collective-permute-start(bf16[192,128]{1,0:T(8,128)(2,1)S(1)} %get-tuple-element.146), channel_id=1, source_target_pairs={{0,16},{1,9},{2,18},{3,11},{4,20},{5,13},{6,22},{7,15},{8,24},{9,1... | collective-permute-start | bytes 147464 | tf_op jit(solution)/shard_map/ppermute | solution.py:557
  140.5 5.9 %collective-permute-start.20 = (bf16[192,128]{1,0:T(8,128)(2,1)S(1)}, bf16[192,128]{1,0:T(8,128)(2,1)S(1)}, u32[]{:S(2)}, u32[]{:S(2)}) collective-permute-start(bf16[192,128]{1,0:T(8,128)(2,1)S(1)} %get-tuple-element.141), channel_id=1, source_target_pairs={{0,24},{1,25},{2,26},{3,27},{4,28},{5,29},{6,30},{7,31},{8,16},{9,... | collective-permute-start | bytes 147464 | tf_op jit(solution)/shard_map/ppermute | solution.py:557
  141.9 4.5 %collective-permute-start.21 = (f32[40,128]{1,0:T(8,128)S(1)}, f32[40,128]{1,0:T(8,128)S(1)}, u32[]{:S(2)}, u32[]{:S(2)}) collective-permute-start(f32[40,128]{1,0:T(8,128)S(1)} %get-tuple-element.149), channel_id=1, source_target_pairs={{0,1},{1,0},{2,3},{3,2},{4,5},{5,4},{6,7},{7,6},{8,9},{9,8},{10,11... | collective-permute-start | bytes 61448 | tf_op jit(solution)/shard_map/ppermute | solution.py:529
  147.7 20.9 %collective-permute-start.27 = (bf16[4608,128]{1,0:T(8,128)(2,1)S(1)}, bf16[4608,128]{1,0:T(8,128)(2,1)S(1)}, u32[]{:S(2)}, u32[]{:S(2)}) collective-permute-start(bf16[4608,128]{1,0:T(8,128)(2,1)S(1)} %join.3.refs_0_), channel_id=1, source_target_pairs={{0,2},{1,5},{2,0},{3,7},{4,6},{5,1},{6,4},{7,3},{8,10},{9,13},{10,... | collective-permute-start | bytes 3538952 | tf_op jit(solution)/shard_map/ppermute | solution.py:557
  148.5 6.1 %collective-permute-start.25 = (bf16[272,128]{1,0:T(8,128)(2,1)S(1)}, bf16[272,128]{1,0:T(8,128)(2,1)S(1)}, u32[]{:S(2)}, u32[]{:S(2)}) collective-permute-start(bf16[272,128]{1,0:T(8,128)(2,1)S(1)} %settle_cols.1.refs_0_), channel_id=1, source_target_pairs={{0,24},{1,25},{2,26},{3,27},{4,28},{5,29},{6,30},{7,31},{8,16},{9,... | collective-permute-start | bytes 208904 | tf_op jit(solution)/shard_map/ppermute | solution.py:557
  150.6 5.5 %collective-permute-start.24 = (bf16[272,128]{1,0:T(8,128)(2,1)S(1)}, bf16[272,128]{1,0:T(8,128)(2,1)S(1)}, u32[]{:S(2)}, u32[]{:S(2)}) collective-permute-start(bf16[272,128]{1,0:T(8,128)(2,1)S(1)} %settle_cols.1.refs_0_), channel_id=1, source_target_pairs={{0,16},{1,9},{2,18},{3,11},{4,20},{5,13},{6,22},{7,15},{8,24},{9,1... | collective-permute-start | bytes 208904 | tf_op jit(solution)/shard_map/ppermute | solution.py:557
  150.6 5.5 %collective-permute-start.22 = (bf16[272,128]{1,0:T(8,128)(2,1)S(1)}, bf16[272,128]{1,0:T(8,128)(2,1)S(1)}, u32[]{:S(2)}, u32[]{:S(2)}) collective-permute-start(bf16[272,128]{1,0:T(8,128)(2,1)S(1)} %settle_cols.1.refs_0_), channel_id=1, source_target_pairs={{0,8},{1,17},{2,10},{3,19},{4,12},{5,21},{6,14},{7,23},{8,0},{9,25... | collective-permute-start | bytes 208904 | tf_op jit(solution)/shard_map/ppermute | solution.py:557
  156.7 15.1 %collective-permute-start.29 = (bf16[848,128]{1,0:T(8,128)(2,1)S(1)}, bf16[848,128]{1,0:T(8,128)(2,1)S(1)}, u32[]{:S(2)}, u32[]{:S(2)}) collective-permute-start(bf16[848,128]{1,0:T(8,128)(2,1)S(1)} %join_cols.1.refs_0_), channel_id=1, source_target_pairs={{0,6},{1,7},{2,4},{3,5},{4,2},{5,3},{6,0},{7,1},{8,14},{9,15},{10,... | collective-permute-start | bytes 651272 | tf_op jit(solution)/shard_map/ppermute | solution.py:557
  158.0 13.8 %collective-permute-start.28 = (bf16[848,128]{1,0:T(8,128)(2,1)S(1)}, bf16[848,128]{1,0:T(8,128)(2,1)S(1)}, u32[]{:S(2)}, u32[]{:S(2)}) collective-permute-start(bf16[848,128]{1,0:T(8,128)(2,1)S(1)} %join_cols.1.refs_0_), channel_id=1, source_target_pairs={{0,4},{1,3},{2,6},{3,1},{4,0},{5,7},{6,2},{7,5},{8,12},{9,11},{10,... | collective-permute-start | bytes 651272 | tf_op jit(solution)/shard_map/ppermute | solution.py:557
  159.5 13.8 %collective-permute-start.26 = (bf16[848,128]{1,0:T(8,128)(2,1)S(1)}, bf16[848,128]{1,0:T(8,128)(2,1)S(1)}, u32[]{:S(2)}, u32[]{:S(2)}) collective-permute-start(bf16[848,128]{1,0:T(8,128)(2,1)S(1)} %join_cols.1.refs_0_), channel_id=1, source_target_pairs={{0,2},{1,5},{2,0},{3,7},{4,6},{5,1},{6,4},{7,3},{8,10},{9,13},{10,... | collective-permute-start | bytes 651272 | tf_op jit(solution)/shard_map/ppermute | solution.py:557
  (7 other events, 104.4 us)

commit v6 on v5

--- a/solution.py
+++ b/solution.py
@@ -435,7 +435,7 @@
     zeros = lambda i, j, *_: (0, 0, 0, 0)
     carried, specs, aliases = [], [], {}
     if not ends[0]:
-        carried.extend(hbm(partial))
+        carried.extend(vmem(partial))
         specs.append(pl.BlockSpec(sums, zeros, pipeline_mode=pl.Buffered(1)))
     if dqkv is not None:
         aliases = {5 + len(carried): 0}
@@ -445,7 +445,7 @@
         dw = jax.ShapeDtypeStruct((total_rows, 128), BF if side else F32)
         dw_spec = pl.BlockSpec((total_rows, 128), lambda i, j, *_: (0, 0), pipeline_mode=pl.Buffered(1))
     else:
-        dw = pltpu.HBM(sums, F32)
+        dw = pltpu.VMEM(sums, F32)
         dw_spec = pl.BlockSpec(sums, zeros, pipeline_mode=pl.Buffered(1))
     return pl.pallas_call(
         functools.partial(back_kernel, ends=ends),

time: 177 us -> 175 us (0.989)
  Pallas kernels: 123 us -> 119 us
    pallas_call x4, Pallas kernels: 33.2 us -> 29.7 us  [attention_back(): pl.pallas_call(functools.partial(back_kernel, ends=ends), grid_spec=pltpu...]
  transfers between devices with their start and end apart: 30 -> 30, of which waited for: 9 -> 10; matrix products, arithmetic and copies ran while one was open for 0% -> 0% of each run, Pallas kernels for 44% -> 43%
where the time goes in v6:
time: 175 us
  Pallas kernels  119 us (68%)
  starting transfers between devices  35.3 us (20%)
  waiting for transfers between devices  17.5 us (10%)
    pallas_call x1, Pallas kernels, mlp(): pl.pallas_call(mlp_kernel, grid_spec=pltpu.PrefetchScalarGridSpec(num_sca...  38.2 us
    ppermute x22, starting transfers between devices, exchange(): out.append(lax.ppermute(v, ('dp', 'tensor'), pairs))  33 us
    pallas_call x4, Pallas kernels, attention_back(): pl.pallas_call(functools.partial(back_kernel, ends=ends), grid_spec=pltpu...  29.7 us
    pallas_call x1, Pallas kernels, attention_forward(): pl.pallas_call(forward_kernel, grid_spec=pltpu.PrefetchScalarGridSpec(num...  21.7 us
    ppermute x22, waiting for transfers between devices, exchange(): out.append(lax.ppermute(v, ('dp', 'tensor'), pairs))  16.9 us
    pallas_call x12, Pallas kernels, small_call(): pl.pallas_call(kernel, in_specs=[pl.BlockSpec(memory_space=pltpu.SMEM)] +...  13.5 us
    pallas_call x1, Pallas kernels, norm_one_back(): pl.pallas_call(norm_one_back_kernel, grid_spec=pltpu.PrefetchScalarGridSp...  8.03 us
    pallas_call x1, Pallas kernels, block_out(): pl.pallas_call(block_out_kernel, grid_spec=pltpu.PrefetchScalarGridSpec(n...  7.26 us
  transfers between devices with their start and end apart: 30, of which 10 were waited for; matrix products, arithmetic and copies ran while one was open for 0% of the time, Pallas kernels for 43%

profile of v6, /device:TPU:0, one launch (start us, length us, event | category | flops | bytes accessed | tf_op | source)
XLA Modules:
  0.0 174.5 jit_solution(6436449378240418010)
XLA Ops:
  3.7 21.7 %attention_forward.1 = (bf16[2048,512]{1,0:T(8,128)(2,1)}, bf16[4,2,3,256,512]{4,3,2,1,0:T(8,128)(2,1)}, bf16[4,8,512,512]{3,2,1,0:T(8,128)(2,1)}, bf16[4,512,51...) custom-call(s32[1]{0:T(128)} %bitcast.tens, s32[8]{0:T(128)} %lens.1, ...), custom_call_target="tpu_custom_call" | custom-call | flops 23000000512 | tf_op jit(solution)/shard_map/attention_forward/pallas_call | solution.py:153
  25.4 38.2 %mlp.1 = (bf16[2048,2048]{1,0:T(8,128)(2,1)}, f32[2048,512]{1,0:T(8,128)}, bf16[4,8,80,512]{3,2,1,0:T(8,128)(2,1)}, bf16[9216,128]{1,0:T(8,128)(2,1)}, bf16[9216...) custom-call(s32[1]{0:T(128)} %bitcast.tens, bf16[2048,512]{1,0:T(8,128)(2,1)} %get-tuple-element.90.n2_ref, ...), custom_call_target="tpu_custom_call" | custom-call | flops 38999998464 | tf_op jit(solution)/shard_map/mlp/pallas_call | solution.py:299
  64.4 4.6 %attention_back.4 = (bf16[4,2,3,256,512]{4,3,2,1,0:T(8,128)(2,1)S(1)}, f32[1,3,256,512]{3,2,1,0:T(8,128)S(1)}) custom-call(s32[1]{0:T(128)} %bitcast.tens, bf16[4,8,512,512]{3,2,1,0:T(8,128)(2,1)} %get-tuple-element.97.p_ref, bf16[4,8,80,512]{3,2,1,0:T(8,128)(2,1)} %get-tuple-element.98.doa_ref, bf16[4,2,3,256,512]{4,3,2,1,0:T(8,128)(2,1)} %get-tuple-element.99.qkv_ref, ...), custom_call_target="tpu_custom_call" | custom-call | flops 4499999744 | tf_op jit(solution)/shard_map/attention_back/pallas_call | solution.py:450
  69.0 2.2 %split_mlp.1 = (f32[4608,128]{1,0:T(8,128)S(1)}, bf16[4608,128]{1,0:T(8,128)(2,1)S(1)}) custom-call(s32[2]{0:T(128)S(1)} %pad_add_fusion.3.scalars, bf16[9216,128]{1,0:T(8,128)(2,1)} %get-tuple-element.94.own, bf16[9216,128]{1,0:T(8,128)(2,1)S(1)} %collective-permute-done.5.recv), custom_call_target="tpu_custom_call" | custom-call | flops 500000000 | tf_op jit(solution)/shard_map/split_mlp/pallas_call | solution.py:562
  71.2 2.7 %collective-permute-start.6 = (bf16[4608,128]{1,0:T(8,128)(2,1)S(1)}, bf16[4608,128]{1,0:T(8,128)(2,1)S(1)}, u32[]{:S(2)}, u32[]{:S(2)}) collective-permute-start(bf16[4608,128]{1,0:T(8,128)(2,1)S(1)} %get-tuple-element.104), channel_id=1, source_target_pairs={{0,2},{1,5},{2,0},{3,7},{4,6},{5,1},{6,4},{7,3},{8,10},{9,13},{10,... | collective-permute-start | bytes 3538952 | tf_op jit(solution)/shard_map/ppermute | solution.py:557
  73.9 10.1 %attention_back.5 = (bf16[4,2,3,256,512]{4,3,2,1,0:T(8,128)(2,1)S(1)}, bf16[3072,128]{1,0:T(8,128)(2,1)S(1)}) custom-call(s32[1]{0:T(128)} %bitcast.tens, bf16[4,8,512,512]{3,2,1,0:T(8,128)(2,1)} %get-tuple-element.97.p_ref, bf16[4,8,80,512]{3,2,1,0:T(8,128)(2,1)} %get-tuple-element.98.doa_ref, ...), custom_call_target="tpu_custom_call", output_to_operand_aliasing={{0}: (6, {})} | custom-call | flops 13500000256 | tf_op jit(solution)/shard_map/attention_back/pallas_call | solution.py:450
  84.2 3.9 %collective-permute-done.6.refs_1_ = bf16[4608,128]{1,0:T(8,128)(2,1)S(1)} collective-permute-done((bf16[4608,128]{1,0:T(8,128)(2,1)S(1)}, bf16[4608,128]{1,0:T(8,128)(2,1)S(1)}, u32[]{:S(2)}, u32[]{:S(2)}) %collective-permute-start.6) | collective-permute-done | bytes 1179680 | tf_op jit(solution)/shard_map/ppermute | solution.py:557
  89.1 2.1 %collective-permute-start.7 = (bf16[2304,128]{1,0:T(8,128)(2,1)S(1)}, bf16[2304,128]{1,0:T(8,128)(2,1)S(1)}, u32[]{:S(2)}, u32[]{:S(2)}) collective-permute-start(bf16[2304,128]{1,0:T(8,128)(2,1)S(1)} %get-tuple-element.110), channel_id=1, source_target_pairs={{0,4},{1,3},{2,6},{3,1},{4,0},{5,7},{6,2},{7,5},{8,12},{9,11},{10,... | collective-permute-start | bytes 1769480 | tf_op jit(solution)/shard_map/ppermute | solution.py:557
  91.2 7.4 %attention_back.6 = (bf16[4,2,3,256,512]{4,3,2,1,0:T(8,128)(2,1)S(1)}, f32[1,3,256,512]{3,2,1,0:T(8,128)S(1)}) custom-call(s32[1]{0:T(128)} %bitcast.tens, bf16[4,8,512,512]{3,2,1,0:T(8,128)(2,1)} %get-tuple-element.97.p_ref, bf16[4,8,80,512]{3,2,1,0:T(8,128)(2,1)} %get-tuple-element.98.doa_ref, ...), custom_call_target="tpu_custom_call", output_to_operand_aliasing={{0}: (5, {})} | custom-call | flops 8999999488 | tf_op jit(solution)/shard_map/attention_back/pallas_call | solution.py:450
  99.8 4.2 %collective-permute-start.10 = (bf16[576,128]{1,0:T(8,128)(2,1)S(1)}, bf16[576,128]{1,0:T(8,128)(2,1)S(1)}, u32[]{:S(2)}, u32[]{:S(2)}) collective-permute-start(bf16[576,128]{1,0:T(8,128)(2,1)S(1)} %get-tuple-element.115), channel_id=1, source_target_pairs={{0,24},{1,25},{2,26},{3,27},{4,28},{5,29},{6,30},{7,31},{8,16},{9,... | collective-permute-start | bytes 442376 | tf_op jit(solution)/shard_map/ppermute | solution.py:557
  104.6 7.6 %attention_back.7 = (bf16[4,2,3,256,512]{4,3,2,1,0:T(8,128)(2,1)S(1)}, f32[3072,128]{1,0:T(8,128)S(1)}) custom-call(s32[1]{0:T(128)} %bitcast.tens, bf16[4,8,512,512]{3,2,1,0:T(8,128)(2,1)} %get-tuple-element.97.p_ref, bf16[4,8,80,512]{3,2,1,0:T(8,128)(2,1)} %get-tuple-element.98.doa_ref, ...), custom_call_target="tpu_custom_call", output_to_operand_aliasing={{0}: (6, {})} | custom-call | flops 8999999488 | tf_op jit(solution)/shard_map/attention_back/pallas_call | solution.py:450
  112.3 3.0 %collective-permute-done.9.refs_1_ = bf16[576,128]{1,0:T(8,128)(2,1)S(1)} collective-permute-done((bf16[576,128]{1,0:T(8,128)(2,1)S(1)}, bf16[576,128]{1,0:T(8,128)(2,1)S(1)}, u32[]{:S(2)}, u32[]{:S(2)}) %collective-permute-start.9) | collective-permute-done | bytes 147488 | tf_op jit(solution)/shard_map/ppermute | solution.py:557
  116.7 1.6 collective-permute-start.12
  118.3 2.5 %collective-permute-start.18 = (bf16[576,128]{1,0:T(8,128)(2,1)S(1)}, bf16[576,128]{1,0:T(8,128)(2,1)S(1)}, u32[]{:S(2)}, u32[]{:S(2)}) collective-permute-start(bf16[576,128]{1,0:T(8,128)(2,1)S(1)} %settle.1.own), channel_id=1, source_target_pairs={{0,24},{1,25},{2,26},{3,27},{4,28},{5,29},{6,30},{7,31},{8,16},{9,... | collective-permute-start | bytes 442376 | tf_op jit(solution)/shard_map/ppermute | solution.py:557
  120.8 1.9 %collective-permute-start.16 = (bf16[576,128]{1,0:T(8,128)(2,1)S(1)}, bf16[576,128]{1,0:T(8,128)(2,1)S(1)}, u32[]{:S(2)}, u32[]{:S(2)}) collective-permute-start(bf16[576,128]{1,0:T(8,128)(2,1)S(1)} %settle.1.own), channel_id=1, source_target_pairs={{0,8},{1,17},{2,10},{3,19},{4,12},{5,21},{6,14},{7,23},{8,0},{9,25... | collective-permute-start | bytes 442376 | tf_op jit(solution)/shard_map/ppermute | solution.py:557
  122.7 1.5 collective-permute-start.14
  124.7 8.0 %norm_one_back.1 = (f32[2048,512]{1,0:T(8,128)}, f32[40,128]{1,0:T(8,128)S(1)}, f32[40,128]{1,0:T(8,128)S(1)}) custom-call(s32[1]{0:T(128)} %bitcast.tens, bf16[4,2,3,256,512]{4,3,2,1,0:T(8,128)(2,1)S(1)} %get-tuple-element.130.dqkv, bf16[768,512]{1,0:T(8,128)(2,1)S(1)} %bitcast.28, bf16[768,512]{1,0:T(8,128)(2,1)S(1)} %copy-done.3, ...), custom_call_target="tpu_custom_call" | custom-call | flops 10000000000 | tf_op jit(solution)/shard_map/norm_one_back/pallas_call | solution.py:501
  134.1 1.6 collective-permute-start.23
  135.8 2.9 %collective-permute-start.19 = (bf16[192,128]{1,0:T(8,128)(2,1)S(1)}, bf16[192,128]{1,0:T(8,128)(2,1)S(1)}, u32[]{:S(2)}, u32[]{:S(2)}) collective-permute-start(bf16[192,128]{1,0:T(8,128)(2,1)S(1)} %get-tuple-element.146), channel_id=1, source_target_pairs={{0,16},{1,9},{2,18},{3,11},{4,20},{5,13},{6,22},{7,15},{8,24},{9,1... | collective-permute-start | bytes 147464 | tf_op jit(solution)/shard_map/ppermute | solution.py:557
  138.7 1.4 collective-permute-start.20
  140.8 3.8 %collective-permute-done.20.refs_2_ = bf16[192,128]{1,0:T(8,128)(2,1)S(1)} collective-permute-done((bf16[192,128]{1,0:T(8,128)(2,1)S(1)}, bf16[192,128]{1,0:T(8,128)(2,1)S(1)}, u32[]{:S(2)}, u32[]{:S(2)}) %collective-permute-start.20) | collective-permute-done | bytes 49184 | tf_op jit(solution)/shard_map/ppermute | solution.py:557
  145.8 1.6 collective-permute-start.27
  147.4 2.1 %collective-permute-start.25 = (bf16[272,128]{1,0:T(8,128)(2,1)S(1)}, bf16[272,128]{1,0:T(8,128)(2,1)S(1)}, u32[]{:S(2)}, u32[]{:S(2)}) collective-permute-start(bf16[272,128]{1,0:T(8,128)(2,1)S(1)} %settle_cols.1.refs_0_), channel_id=1, source_target_pairs={{0,24},{1,25},{2,26},{3,27},{4,28},{5,29},{6,30},{7,31},{8,16},{9,... | collective-permute-start | bytes 208904 | tf_op jit(solution)/shard_map/ppermute | solution.py:557
  149.5 2.3 %collective-permute-start.22 = (bf16[272,128]{1,0:T(8,128)(2,1)S(1)}, bf16[272,128]{1,0:T(8,128)(2,1)S(1)}, u32[]{:S(2)}, u32[]{:S(2)}) collective-permute-start(bf16[272,128]{1,0:T(8,128)(2,1)S(1)} %settle_cols.1.refs_0_), channel_id=1, source_target_pairs={{0,8},{1,17},{2,10},{3,19},{4,12},{5,21},{6,14},{7,23},{8,0},{9,25... | collective-permute-start | bytes 208904 | tf_op jit(solution)/shard_map/ppermute | solution.py:557
  151.8 1.7 collective-permute-done.25.refs_3_
  153.5 1.5 collective-permute-done.24.refs_2_
  155.6 1.4 collective-permute-start.29
  157.6 1.5 collective-permute-start.26
  159.1 7.3 %block_out.1 = bf16[2048,512]{1,0:T(8,128)(2,1)} custom-call(s32[1]{0:T(128)} %bitcast.tens, bf16[2048,2048]{1,0:T(8,128)(2,1)S(1)} %bitcast.30, bf16[1024,512]{1,0:T(8,128)(2,1)S(1)} %copy-done, bf16[1024,512]{1,0:T(8,128)(2,1)S(1)} %collective-permute-done.3.down_oth, f32[8,512]{1,0:T(8,128)S(1)} %rows_of.1.vecs, f32[2048,512]{1,0:T(8,128)} %get-tuple-element.91.h1_ref), custom_call_target="tpu_custom_call" | custom-call | flops 7000000000 | tf_op jit(solution)/shard_map/block_out/pallas_call | solution.py:347
  166.7 3.2 %finish_mlp.1 = (f32[1024,512]{1,0:T(8,128)}, f32[1024,512]{1,0:T(8,128)}, f32[256,512]{1,0:T(8,128)}) custom-call(s32[2]{0:T(128)S(1)} %pad_add_fusion.3.scalars, bf16[4608,128]{1,0:T(8,128)(2,1)S(1)} %join.3.refs_0_, bf16[4608,128]{1,0:T(8,128)(2,1)S(1)} %collective-permute-done.27.refs_1_), custom_call_target="tpu_custom_call" | custom-call | flops 500000000 | tf_op jit(solution)/shard_map/finish_mlp/pallas_call | solution.py:562
  169.9 1.5 collective-permute-done.26.refs_1_
  171.4 2.0 %finish_qkv.1 = (f32[3,256,512]{2,1,0:T(8,128)}, f32[40,128]{1,0:T(8,128)S(1)}) custom-call(s32[4]{0:T(128)S(1)} %pad_add_fusion.1.scalars, bf16[848,128]{1,0:T(8,128)(2,1)S(1)} %join_cols.1.refs_0_, bf16[848,128]{1,0:T(8,128)(2,1)S(1)} %collective-permute-done.26.refs_1_, bf16[848,128]{1,0:T(8,128)(2,1)S(1)} %collective-permute-done.28.refs_2_, ...), custom_call_target="tpu_custom_call" | custom-call | flops 500000000 | tf_op jit(solution)/shard_map/finish_qkv/pallas_call | solution.py:562
  (75 shorter events, 14.9 us)
Async XLA Ops:
  0.6 3.0 %collective-permute-start = (bf16[768,512]{1,0:T(8,128)(2,1)}, bf16[768,512]{1,0:T(8,128)(2,1)S(1)}, u32[]{:S(2)}, u32[]{:S(2)}) collective-permute-start(bf16[768,512]{1,0:T(8,128)(2,1)} %bitcast.26), channel_id=1, source_target_pairs={{0,1},{1,0},{2,3},{3,2},{4,5},{5,4},{6,7},{7,6},{8,9},{9,8},{10,11... | collective-permute-start | bytes 2359304 | tf_op jit(solution)/shard_map/ppermute | solution.py:529
  1.2 2.5 %collective-permute-start.1 = (bf16[256,512]{1,0:T(8,128)(2,1)}, bf16[256,512]{1,0:T(8,128)(2,1)S(1)}, u32[]{:S(2)}, u32[]{:S(2)}) collective-permute-start(bf16[256,512]{1,0:T(8,128)(2,1)} %wo_own.3), channel_id=1, source_target_pairs={{0,1},{1,0},{2,3},{3,2},{4,5},{5,4},{6,7},{7,6},{8,9},{9,8},{10,11... | collective-permute-start | bytes 786440 | tf_op jit(solution)/shard_map/ppermute | solution.py:529
  2.1 23.3 %collective-permute-start.4 = (f32[8,512]{1,0:T(8,128)S(1)}, f32[8,512]{1,0:T(8,128)S(1)}, u32[]{:S(2)}, u32[]{:S(2)}) collective-permute-start(f32[8,512]{1,0:T(8,128)S(1)} %rows_of.1.vecs), channel_id=1, source_target_pairs={{0,1},{1,0},{2,3},{3,2},{4,5},{5,4},{6,7},{7,6},{8,9},{9,8},{10,11... | collective-permute-start | bytes 49160 | tf_op jit(solution)/shard_map/ppermute | solution.py:529
  2.6 22.8 %collective-permute-start.2 = (bf16[1024,512]{1,0:T(8,128)(2,1)}, bf16[1024,512]{1,0:T(8,128)(2,1)S(1)}, u32[]{:S(2)}, u32[]{:S(2)}) collective-permute-start(bf16[1024,512]{1,0:T(8,128)(2,1)} %up_own.1), channel_id=1, source_target_pairs={{0,1},{1,0},{2,3},{3,2},{4,5},{5,4},{6,7},{7,6},{8,9},{9,8},{10,11... | collective-permute-start | bytes 3145736 | tf_op jit(solution)/shard_map/ppermute | solution.py:529
  2.7 22.8 %collective-permute-start.3 = (bf16[1024,512]{1,0:T(8,128)(2,1)}, bf16[1024,512]{1,0:T(8,128)(2,1)S(1)}, u32[]{:S(2)}, u32[]{:S(2)}) collective-permute-start(bf16[1024,512]{1,0:T(8,128)(2,1)} %down_own.3), channel_id=1, source_target_pairs={{0,1},{1,0},{2,3},{3,2},{4,5},{5,4},{6,7},{7,6},{8,9},{9,8},{10,11... | collective-permute-start | bytes 3145736 | tf_op jit(solution)/shard_map/ppermute | solution.py:529
  63.7 5.3 %collective-permute-start.5 = (bf16[9216,128]{1,0:T(8,128)(2,1)}, bf16[9216,128]{1,0:T(8,128)(2,1)S(1)}, u32[]{:S(2)}, u32[]{:S(2)}) collective-permute-start(bf16[9216,128]{1,0:T(8,128)(2,1)} %get-tuple-element.95), channel_id=1, source_target_pairs={{0,1},{1,0},{2,3},{3,2},{4,5},{5,4},{6,7},{7,6},{8,9},{9,8},{10,11... | collective-permute-start | bytes 7077896 | tf_op jit(solution)/shard_map/ppermute | solution.py:529
  71.2 16.9 %collective-permute-start.6 = (bf16[4608,128]{1,0:T(8,128)(2,1)S(1)}, bf16[4608,128]{1,0:T(8,128)(2,1)S(1)}, u32[]{:S(2)}, u32[]{:S(2)}) collective-permute-start(bf16[4608,128]{1,0:T(8,128)(2,1)S(1)} %get-tuple-element.104), channel_id=1, source_target_pairs={{0,2},{1,5},{2,0},{3,7},{4,6},{5,1},{6,4},{7,3},{8,10},{9,13},{10,... | collective-permute-start | bytes 3538952 | tf_op jit(solution)/shard_map/ppermute | solution.py:557
  84.0 31.9 %collective-permute-start.11 = (bf16[3072,128]{1,0:T(8,128)(2,1)S(1)}, bf16[3072,128]{1,0:T(8,128)(2,1)S(1)}, u32[]{:S(2)}, u32[]{:S(2)}) collective-permute-start(bf16[3072,128]{1,0:T(8,128)(2,1)S(1)} %get-tuple-element.107), channel_id=1, source_target_pairs={{0,1},{1,0},{2,3},{3,2},{4,5},{5,4},{6,7},{7,6},{8,9},{9,8},{10,11... | collective-permute-start | bytes 2359304 | tf_op jit(solution)/shard_map/ppermute | solution.py:529
  89.1 10.0 %collective-permute-start.7 = (bf16[2304,128]{1,0:T(8,128)(2,1)S(1)}, bf16[2304,128]{1,0:T(8,128)(2,1)S(1)}, u32[]{:S(2)}, u32[]{:S(2)}) collective-permute-start(bf16[2304,128]{1,0:T(8,128)(2,1)S(1)} %get-tuple-element.110), channel_id=1, source_target_pairs={{0,4},{1,3},{2,6},{3,1},{4,0},{5,7},{6,2},{7,5},{8,12},{9,11},{10,... | collective-permute-start | bytes 1769480 | tf_op jit(solution)/shard_map/ppermute | solution.py:557
  99.8 15.5 %collective-permute-start.10 = (bf16[576,128]{1,0:T(8,128)(2,1)S(1)}, bf16[576,128]{1,0:T(8,128)(2,1)S(1)}, u32[]{:S(2)}, u32[]{:S(2)}) collective-permute-start(bf16[576,128]{1,0:T(8,128)(2,1)S(1)} %get-tuple-element.115), channel_id=1, source_target_pairs={{0,24},{1,25},{2,26},{3,27},{4,28},{5,29},{6,30},{7,31},{8,16},{9,... | collective-permute-start | bytes 442376 | tf_op jit(solution)/shard_map/ppermute | solution.py:557
  104.0 8.3 %collective-permute-start.8 = (bf16[576,128]{1,0:T(8,128)(2,1)S(1)}, bf16[576,128]{1,0:T(8,128)(2,1)S(1)}, u32[]{:S(2)}, u32[]{:S(2)}) collective-permute-start(bf16[576,128]{1,0:T(8,128)(2,1)S(1)} %get-tuple-element.120), channel_id=1, source_target_pairs={{0,8},{1,17},{2,10},{3,19},{4,12},{5,21},{6,14},{7,23},{8,0},{9,25... | collective-permute-start | bytes 442376 | tf_op jit(solution)/shard_map/ppermute | solution.py:557
  104.0 11.3 %collective-permute-start.9 = (bf16[576,128]{1,0:T(8,128)(2,1)S(1)}, bf16[576,128]{1,0:T(8,128)(2,1)S(1)}, u32[]{:S(2)}, u32[]{:S(2)}) collective-permute-start(bf16[576,128]{1,0:T(8,128)(2,1)S(1)} %get-tuple-element.122), channel_id=1, source_target_pairs={{0,16},{1,9},{2,18},{3,11},{4,20},{5,13},{6,22},{7,15},{8,24},{9,1... | collective-permute-start | bytes 442376 | tf_op jit(solution)/shard_map/ppermute | solution.py:557
  115.9 43.2 %slice-start = ((s8[8388608]{0:T(1024)(128)(4,1)}), s8[4194304]{0:T(1024)(128)(4,1)S(1)}, s32[]{:S(2)}) async-start(s8[8388608]{0:T(1024)(128)(4,1)} %bitcast.29), calls=%async_computation | async-start | bytes 8388608
  116.7 7.4 %collective-permute-start.12 = (bf16[768,128]{1,0:T(8,128)(2,1)S(1)}, bf16[768,128]{1,0:T(8,128)(2,1)S(1)}, u32[]{:S(2)}, u32[]{:S(2)}) collective-permute-start(bf16[768,128]{1,0:T(8,128)(2,1)S(1)} %get-tuple-element.127), channel_id=1, source_target_pairs={{0,2},{1,5},{2,0},{3,7},{4,6},{5,1},{6,4},{7,3},{8,10},{9,13},{10,... | collective-permute-start | bytes 589832 | tf_op jit(solution)/shard_map/ppermute | solution.py:557
  118.3 15.2 %collective-permute-start.18 = (bf16[576,128]{1,0:T(8,128)(2,1)S(1)}, bf16[576,128]{1,0:T(8,128)(2,1)S(1)}, u32[]{:S(2)}, u32[]{:S(2)}) collective-permute-start(bf16[576,128]{1,0:T(8,128)(2,1)S(1)} %settle.1.own), channel_id=1, source_target_pairs={{0,24},{1,25},{2,26},{3,27},{4,28},{5,29},{6,30},{7,31},{8,16},{9,... | collective-permute-start | bytes 442376 | tf_op jit(solution)/shard_map/ppermute | solution.py:557
  120.8 12.7 %collective-permute-start.17 = (bf16[576,128]{1,0:T(8,128)(2,1)S(1)}, bf16[576,128]{1,0:T(8,128)(2,1)S(1)}, u32[]{:S(2)}, u32[]{:S(2)}) collective-permute-start(bf16[576,128]{1,0:T(8,128)(2,1)S(1)} %settle.1.own), channel_id=1, source_target_pairs={{0,16},{1,9},{2,18},{3,11},{4,20},{5,13},{6,22},{7,15},{8,24},{9,1... | collective-permute-start | bytes 442376 | tf_op jit(solution)/shard_map/ppermute | solution.py:557
  120.8 12.7 %collective-permute-start.16 = (bf16[576,128]{1,0:T(8,128)(2,1)S(1)}, bf16[576,128]{1,0:T(8,128)(2,1)S(1)}, u32[]{:S(2)}, u32[]{:S(2)}) collective-permute-start(bf16[576,128]{1,0:T(8,128)(2,1)S(1)} %settle.1.own), channel_id=1, source_target_pairs={{0,8},{1,17},{2,10},{3,19},{4,12},{5,21},{6,14},{7,23},{8,0},{9,25... | collective-permute-start | bytes 442376 | tf_op jit(solution)/shard_map/ppermute | solution.py:557
  122.7 10.1 %collective-permute-start.14 = (bf16[768,128]{1,0:T(8,128)(2,1)S(1)}, bf16[768,128]{1,0:T(8,128)(2,1)S(1)}, u32[]{:S(2)}, u32[]{:S(2)}) collective-permute-start(bf16[768,128]{1,0:T(8,128)(2,1)S(1)} %get-tuple-element.128), channel_id=1, source_target_pairs={{0,6},{1,7},{2,4},{3,5},{4,2},{5,3},{6,0},{7,1},{8,14},{9,15},{10,... | collective-permute-start | bytes 589832 | tf_op jit(solution)/shard_map/ppermute | solution.py:557
  124.2 8.6 %collective-permute-start.13 = (bf16[768,128]{1,0:T(8,128)(2,1)S(1)}, bf16[768,128]{1,0:T(8,128)(2,1)S(1)}, u32[]{:S(2)}, u32[]{:S(2)}) collective-permute-start(bf16[768,128]{1,0:T(8,128)(2,1)S(1)} %get-tuple-element.136), channel_id=1, source_target_pairs={{0,4},{1,3},{2,6},{3,1},{4,0},{5,7},{6,2},{7,5},{8,12},{9,11},{10,... | collective-permute-start | bytes 589832 | tf_op jit(solution)/shard_map/ppermute | solution.py:557
  124.7 34.4 %slice-start.1 = ((s8[8388608]{0:T(1024)(128)(4,1)}), s8[4194304]{0:T(1024)(128)(4,1)S(1)}, s32[]{:S(2)}) async-start(s8[8388608]{0:T(1024)(128)(4,1)} %bitcast.29), calls=%async_computation.1 | async-start | bytes 8388608
  134.1 11.1 %collective-permute-start.23 = (bf16[2304,128]{1,0:T(8,128)(2,1)S(1)}, bf16[2304,128]{1,0:T(8,128)(2,1)S(1)}, u32[]{:S(2)}, u32[]{:S(2)}) collective-permute-start(bf16[2304,128]{1,0:T(8,128)(2,1)S(1)} %join.2.own), channel_id=1, source_target_pairs={{0,4},{1,3},{2,6},{3,1},{4,0},{5,7},{6,2},{7,5},{8,12},{9,11},{10,... | collective-permute-start | bytes 1769480 | tf_op jit(solution)/shard_map/ppermute | solution.py:557
  135.6 4.4 %collective-permute-start.15 = (bf16[192,128]{1,0:T(8,128)(2,1)S(1)}, bf16[192,128]{1,0:T(8,128)(2,1)S(1)}, u32[]{:S(2)}, u32[]{:S(2)}) collective-permute-start(bf16[192,128]{1,0:T(8,128)(2,1)S(1)} %get-tuple-element.140), channel_id=1, source_target_pairs={{0,8},{1,17},{2,10},{3,19},{4,12},{5,21},{6,14},{7,23},{8,0},{9,25... | collective-permute-start | bytes 147464 | tf_op jit(solution)/shard_map/ppermute | solution.py:557
  135.8 5.0 %collective-permute-start.19 = (bf16[192,128]{1,0:T(8,128)(2,1)S(1)}, bf16[192,128]{1,0:T(8,128)(2,1)S(1)}, u32[]{:S(2)}, u32[]{:S(2)}) collective-permute-start(bf16[192,128]{1,0:T(8,128)(2,1)S(1)} %get-tuple-element.146), channel_id=1, source_target_pairs={{0,16},{1,9},{2,18},{3,11},{4,20},{5,13},{6,22},{7,15},{8,24},{9,1... | collective-permute-start | bytes 147464 | tf_op jit(solution)/shard_map/ppermute | solution.py:557
  138.7 5.9 %collective-permute-start.20 = (bf16[192,128]{1,0:T(8,128)(2,1)S(1)}, bf16[192,128]{1,0:T(8,128)(2,1)S(1)}, u32[]{:S(2)}, u32[]{:S(2)}) collective-permute-start(bf16[192,128]{1,0:T(8,128)(2,1)S(1)} %get-tuple-element.141), channel_id=1, source_target_pairs={{0,24},{1,25},{2,26},{3,27},{4,28},{5,29},{6,30},{7,31},{8,16},{9,... | collective-permute-start | bytes 147464 | tf_op jit(solution)/shard_map/ppermute | solution.py:557
  140.0 4.5 %collective-permute-start.21 = (f32[40,128]{1,0:T(8,128)S(1)}, f32[40,128]{1,0:T(8,128)S(1)}, u32[]{:S(2)}, u32[]{:S(2)}) collective-permute-start(f32[40,128]{1,0:T(8,128)S(1)} %get-tuple-element.149), channel_id=1, source_target_pairs={{0,1},{1,0},{2,3},{3,2},{4,5},{5,4},{6,7},{7,6},{8,9},{9,8},{10,11... | collective-permute-start | bytes 61448 | tf_op jit(solution)/shard_map/ppermute | solution.py:529
  145.8 20.9 %collective-permute-start.27 = (bf16[4608,128]{1,0:T(8,128)(2,1)S(1)}, bf16[4608,128]{1,0:T(8,128)(2,1)S(1)}, u32[]{:S(2)}, u32[]{:S(2)}) collective-permute-start(bf16[4608,128]{1,0:T(8,128)(2,1)S(1)} %join.3.refs_0_), channel_id=1, source_target_pairs={{0,2},{1,5},{2,0},{3,7},{4,6},{5,1},{6,4},{7,3},{8,10},{9,13},{10,... | collective-permute-start | bytes 3538952 | tf_op jit(solution)/shard_map/ppermute | solution.py:557
  147.4 6.1 %collective-permute-start.25 = (bf16[272,128]{1,0:T(8,128)(2,1)S(1)}, bf16[272,128]{1,0:T(8,128)(2,1)S(1)}, u32[]{:S(2)}, u32[]{:S(2)}) collective-permute-start(bf16[272,128]{1,0:T(8,128)(2,1)S(1)} %settle_cols.1.refs_0_), channel_id=1, source_target_pairs={{0,24},{1,25},{2,26},{3,27},{4,28},{5,29},{6,30},{7,31},{8,16},{9,... | collective-permute-start | bytes 208904 | tf_op jit(solution)/shard_map/ppermute | solution.py:557
  149.5 5.5 %collective-permute-start.24 = (bf16[272,128]{1,0:T(8,128)(2,1)S(1)}, bf16[272,128]{1,0:T(8,128)(2,1)S(1)}, u32[]{:S(2)}, u32[]{:S(2)}) collective-permute-start(bf16[272,128]{1,0:T(8,128)(2,1)S(1)} %settle_cols.1.refs_0_), channel_id=1, source_target_pairs={{0,16},{1,9},{2,18},{3,11},{4,20},{5,13},{6,22},{7,15},{8,24},{9,1... | collective-permute-start | bytes 208904 | tf_op jit(solution)/shard_map/ppermute | solution.py:557
  149.5 5.5 %collective-permute-start.22 = (bf16[272,128]{1,0:T(8,128)(2,1)S(1)}, bf16[272,128]{1,0:T(8,128)(2,1)S(1)}, u32[]{:S(2)}, u32[]{:S(2)}) collective-permute-start(bf16[272,128]{1,0:T(8,128)(2,1)S(1)} %settle_cols.1.refs_0_), channel_id=1, source_target_pairs={{0,8},{1,17},{2,10},{3,19},{4,12},{5,21},{6,14},{7,23},{8,0},{9,25... | collective-permute-start | bytes 208904 | tf_op jit(solution)/shard_map/ppermute | solution.py:557
  155.6 14.3 %collective-permute-start.29 = (bf16[848,128]{1,0:T(8,128)(2,1)S(1)}, bf16[848,128]{1,0:T(8,128)(2,1)S(1)}, u32[]{:S(2)}, u32[]{:S(2)}) collective-permute-start(bf16[848,128]{1,0:T(8,128)(2,1)S(1)} %join_cols.1.refs_0_), channel_id=1, source_target_pairs={{0,6},{1,7},{2,4},{3,5},{4,2},{5,3},{6,0},{7,1},{8,14},{9,15},{10,... | collective-permute-start | bytes 651272 | tf_op jit(solution)/shard_map/ppermute | solution.py:557
  156.9 13.0 %collective-permute-start.28 = (bf16[848,128]{1,0:T(8,128)(2,1)S(1)}, bf16[848,128]{1,0:T(8,128)(2,1)S(1)}, u32[]{:S(2)}, u32[]{:S(2)}) collective-permute-start(bf16[848,128]{1,0:T(8,128)(2,1)S(1)} %join_cols.1.refs_0_), channel_id=1, source_target_pairs={{0,4},{1,3},{2,6},{3,1},{4,0},{5,7},{6,2},{7,5},{8,12},{9,11},{10,... | collective-permute-start | bytes 651272 | tf_op jit(solution)/shard_map/ppermute | solution.py:557
  157.6 13.8 %collective-permute-start.26 = (bf16[848,128]{1,0:T(8,128)(2,1)S(1)}, bf16[848,128]{1,0:T(8,128)(2,1)S(1)}, u32[]{:S(2)}, u32[]{:S(2)}) collective-permute-start(bf16[848,128]{1,0:T(8,128)(2,1)S(1)} %join_cols.1.refs_0_), channel_id=1, source_target_pairs={{0,2},{1,5},{2,0},{3,7},{4,6},{5,1},{6,4},{7,3},{8,10},{9,13},{10,... | collective-permute-start | bytes 651272 | tf_op jit(solution)/shard_map/ppermute | solution.py:557
  (7 other events, 105.6 us)

commit v7 on v6

--- a/solution.py
+++ b/solution.py
@@ -751,10 +751,12 @@
 
 
 def finish_qkv_kernel(scalars, *refs):
-    (own, *recvs), (out, cols), (full, held) = refs[:-4], refs[-4:-2], refs[-2:]
+    (own, *recvs), (out, cols, dub), (full, held) = refs[:-5], refs[-5:-2], refs[-2:]
     m = full.shape[0] // (1 + len(recvs))
     fill(full, scalars, own, recvs)
-    cols[...] = sum_cols(scalars, own, recvs, m, held)
+    total = sum_cols(scalars, own, recvs, m, held)
+    cols[...] = total[:cols.shape[0]]
+    dub[...] = total[cols.shape[0]:]
     half = out.shape[1]
     for c in range(D // 128):
         for t in range(3):
@@ -766,7 +768,10 @@
     m = own.shape[0] - extra
     return small_call(
         finish_qkv_kernel,
-        [jax.ShapeDtypeStruct((3, half, D), F32), jax.ShapeDtypeStruct((extra // 2, 128), F32)],
+        [
+            jax.ShapeDtypeStruct((3, half, D), F32), jax.ShapeDtypeStruct((32, 128), F32),
+            jax.ShapeDtypeStruct((extra // 2 - 32, 128), F32),
+        ],
         "finish_qkv", stage.scalars, own, *recvs,
         scratch=[pltpu.VMEM((stage.size * m, 128), BF), pltpu.VMEM((stage.size, extra // 2, 128), F32)],
     )
@@ -888,9 +893,8 @@
             token = step(action[:3])
     while "qkv" not in results:
         token = step("qkv")
-    dwq, shared = finish_qkv(*results["qkv"], qkv_stages[0], half, extra)
-    dub = shared[32:]
-    shared = shared[:32].reshape(D // 128, 8, 128).transpose(1, 0, 2).reshape(8, D)
+    dwq, shared, dub = finish_qkv(*results["qkv"], qkv_stages[0], half, extra)
+    shared = shared.reshape(D // 128, 8, 128).transpose(1, 0, 2).reshape(8, D)
     return (
         out, grad_latents, shared[0], shared[1], dwq, dwo, shared[4],
         shared[2], shared[3], dup, dub.reshape(units), ddown, shared[5],

time: 175 us -> 174 us (level)
  no operation moved by 1% of the time
where the time goes in v7:
time: 174 us
  Pallas kernels  119 us (68%)
  starting transfers between devices  35.3 us (20%)
  waiting for transfers between devices  17.5 us (10%)
    pallas_call x1, Pallas kernels, mlp(): pl.pallas_call(mlp_kernel, grid_spec=pltpu.PrefetchScalarGridSpec(num_sca...  38.2 us
    ppermute x22, starting transfers between devices, exchange(): out.append(lax.ppermute(v, ('dp', 'tensor'), pairs))  33 us
    pallas_call x4, Pallas kernels, attention_back(): pl.pallas_call(functools.partial(back_kernel, ends=ends), grid_spec=pltpu...  29.7 us
    pallas_call x1, Pallas kernels, attention_forward(): pl.pallas_call(forward_kernel, grid_spec=pltpu.PrefetchScalarGridSpec(num...  21.7 us
    ppermute x22, waiting for transfers between devices, exchange(): out.append(lax.ppermute(v, ('dp', 'tensor'), pairs))  16.9 us
    pallas_call x12, Pallas kernels, small_call(): pl.pallas_call(kernel, in_specs=[pl.BlockSpec(memory_space=pltpu.SMEM)] +...  13.5 us
    pallas_call x1, Pallas kernels, norm_one_back(): pl.pallas_call(norm_one_back_kernel, grid_spec=pltpu.PrefetchScalarGridSp...  8.03 us
    pallas_call x1, Pallas kernels, block_out(): pl.pallas_call(block_out_kernel, grid_spec=pltpu.PrefetchScalarGridSpec(n...  7.26 us
  transfers between devices with their start and end apart: 30, of which 10 were waited for; matrix products, arithmetic and copies ran while one was open for 0% of the time, Pallas kernels for 43%

profile of v7, /device:TPU:0, one launch (start us, length us, event | category | flops | bytes accessed | tf_op | source)
XLA Modules:
  0.0 173.9 jit_solution(11921309772595054038)
XLA Ops:
  3.7 21.7 %attention_forward.1 = (bf16[2048,512]{1,0:T(8,128)(2,1)}, bf16[4,2,3,256,512]{4,3,2,1,0:T(8,128)(2,1)}, bf16[4,8,512,512]{3,2,1,0:T(8,128)(2,1)}, bf16[4,512,51...) custom-call(s32[1]{0:T(128)} %bitcast.tens, s32[8]{0:T(128)} %lens.1, ...), custom_call_target="tpu_custom_call" | custom-call | flops 23000000512 | tf_op jit(solution)/shard_map/attention_forward/pallas_call | solution.py:153
  25.4 38.2 %mlp.1 = (bf16[2048,2048]{1,0:T(8,128)(2,1)}, f32[2048,512]{1,0:T(8,128)}, bf16[4,8,80,512]{3,2,1,0:T(8,128)(2,1)}, bf16[9216,128]{1,0:T(8,128)(2,1)}, bf16[9216...) custom-call(s32[1]{0:T(128)} %bitcast.tens, bf16[2048,512]{1,0:T(8,128)(2,1)} %get-tuple-element.91.n2_ref, ...), custom_call_target="tpu_custom_call" | custom-call | flops 38999998464 | tf_op jit(solution)/shard_map/mlp/pallas_call | solution.py:299
  64.4 4.6 %attention_back.4 = (bf16[4,2,3,256,512]{4,3,2,1,0:T(8,128)(2,1)S(1)}, f32[1,3,256,512]{3,2,1,0:T(8,128)S(1)}) custom-call(s32[1]{0:T(128)} %bitcast.tens, bf16[4,8,512,512]{3,2,1,0:T(8,128)(2,1)} %get-tuple-element.98.p_ref, bf16[4,8,80,512]{3,2,1,0:T(8,128)(2,1)} %get-tuple-element.99.doa_ref, bf16[4,2,3,256,512]{4,3,2,1,0:T(8,128)(2,1)} %get-tuple-element.100.qkv_ref, ...), custom_call_target="tpu_custom_call" | custom-call | flops 4499999744 | tf_op jit(solution)/shard_map/attention_back/pallas_call | solution.py:450
  69.0 2.2 %split_mlp.1 = (f32[4608,128]{1,0:T(8,128)S(1)}, bf16[4608,128]{1,0:T(8,128)(2,1)S(1)}) custom-call(s32[2]{0:T(128)S(1)} %pad_add_fusion.3.scalars, bf16[9216,128]{1,0:T(8,128)(2,1)} %get-tuple-element.95.own, bf16[9216,128]{1,0:T(8,128)(2,1)S(1)} %collective-permute-done.5.recv), custom_call_target="tpu_custom_call" | custom-call | flops 500000000 | tf_op jit(solution)/shard_map/split_mlp/pallas_call | solution.py:562
  71.2 2.7 %collective-permute-start.6 = (bf16[4608,128]{1,0:T(8,128)(2,1)S(1)}, bf16[4608,128]{1,0:T(8,128)(2,1)S(1)}, u32[]{:S(2)}, u32[]{:S(2)}) collective-permute-start(bf16[4608,128]{1,0:T(8,128)(2,1)S(1)} %get-tuple-element.105), channel_id=1, source_target_pairs={{0,2},{1,5},{2,0},{3,7},{4,6},{5,1},{6,4},{7,3},{8,10},{9,13},{10,... | collective-permute-start | bytes 3538952 | tf_op jit(solution)/shard_map/ppermute | solution.py:557
  73.9 10.1 %attention_back.5 = (bf16[4,2,3,256,512]{4,3,2,1,0:T(8,128)(2,1)S(1)}, bf16[3072,128]{1,0:T(8,128)(2,1)S(1)}) custom-call(s32[1]{0:T(128)} %bitcast.tens, bf16[4,8,512,512]{3,2,1,0:T(8,128)(2,1)} %get-tuple-element.98.p_ref, bf16[4,8,80,512]{3,2,1,0:T(8,128)(2,1)} %get-tuple-element.99.doa_ref, ...), custom_call_target="tpu_custom_call", output_to_operand_aliasing={{0}: (6, {})} | custom-call | flops 13500000256 | tf_op jit(solution)/shard_map/attention_back/pallas_call | solution.py:450
  84.2 3.9 %collective-permute-done.6.refs_1_ = bf16[4608,128]{1,0:T(8,128)(2,1)S(1)} collective-permute-done((bf16[4608,128]{1,0:T(8,128)(2,1)S(1)}, bf16[4608,128]{1,0:T(8,128)(2,1)S(1)}, u32[]{:S(2)}, u32[]{:S(2)}) %collective-permute-start.6) | collective-permute-done | bytes 1179680 | tf_op jit(solution)/shard_map/ppermute | solution.py:557
  89.1 2.1 %collective-permute-start.7 = (bf16[2304,128]{1,0:T(8,128)(2,1)S(1)}, bf16[2304,128]{1,0:T(8,128)(2,1)S(1)}, u32[]{:S(2)}, u32[]{:S(2)}) collective-permute-start(bf16[2304,128]{1,0:T(8,128)(2,1)S(1)} %get-tuple-element.111), channel_id=1, source_target_pairs={{0,4},{1,3},{2,6},{3,1},{4,0},{5,7},{6,2},{7,5},{8,12},{9,11},{10,... | collective-permute-start | bytes 1769480 | tf_op jit(solution)/shard_map/ppermute | solution.py:557
  91.2 7.4 %attention_back.6 = (bf16[4,2,3,256,512]{4,3,2,1,0:T(8,128)(2,1)S(1)}, f32[1,3,256,512]{3,2,1,0:T(8,128)S(1)}) custom-call(s32[1]{0:T(128)} %bitcast.tens, bf16[4,8,512,512]{3,2,1,0:T(8,128)(2,1)} %get-tuple-element.98.p_ref, bf16[4,8,80,512]{3,2,1,0:T(8,128)(2,1)} %get-tuple-element.99.doa_ref, ...), custom_call_target="tpu_custom_call", output_to_operand_aliasing={{0}: (5, {})} | custom-call | flops 8999999488 | tf_op jit(solution)/shard_map/attention_back/pallas_call | solution.py:450
  99.8 4.2 %collective-permute-start.10 = (bf16[576,128]{1,0:T(8,128)(2,1)S(1)}, bf16[576,128]{1,0:T(8,128)(2,1)S(1)}, u32[]{:S(2)}, u32[]{:S(2)}) collective-permute-start(bf16[576,128]{1,0:T(8,128)(2,1)S(1)} %get-tuple-element.116), channel_id=1, source_target_pairs={{0,24},{1,25},{2,26},{3,27},{4,28},{5,29},{6,30},{7,31},{8,16},{9,... | collective-permute-start | bytes 442376 | tf_op jit(solution)/shard_map/ppermute | solution.py:557
  104.6 7.6 %attention_back.7 = (bf16[4,2,3,256,512]{4,3,2,1,0:T(8,128)(2,1)S(1)}, f32[3072,128]{1,0:T(8,128)S(1)}) custom-call(s32[1]{0:T(128)} %bitcast.tens, bf16[4,8,512,512]{3,2,1,0:T(8,128)(2,1)} %get-tuple-element.98.p_ref, bf16[4,8,80,512]{3,2,1,0:T(8,128)(2,1)} %get-tuple-element.99.doa_ref, ...), custom_call_target="tpu_custom_call", output_to_operand_aliasing={{0}: (6, {})} | custom-call | flops 8999999488 | tf_op jit(solution)/shard_map/attention_back/pallas_call | solution.py:450
  112.3 3.0 %collective-permute-done.9.refs_1_ = bf16[576,128]{1,0:T(8,128)(2,1)S(1)} collective-permute-done((bf16[576,128]{1,0:T(8,128)(2,1)S(1)}, bf16[576,128]{1,0:T(8,128)(2,1)S(1)}, u32[]{:S(2)}, u32[]{:S(2)}) %collective-permute-start.9) | collective-permute-done | bytes 147488 | tf_op jit(solution)/shard_map/ppermute | solution.py:557
  116.7 1.6 collective-permute-start.12
  118.3 2.5 %collective-permute-start.18 = (bf16[576,128]{1,0:T(8,128)(2,1)S(1)}, bf16[576,128]{1,0:T(8,128)(2,1)S(1)}, u32[]{:S(2)}, u32[]{:S(2)}) collective-permute-start(bf16[576,128]{1,0:T(8,128)(2,1)S(1)} %settle.1.own), channel_id=1, source_target_pairs={{0,24},{1,25},{2,26},{3,27},{4,28},{5,29},{6,30},{7,31},{8,16},{9,... | collective-permute-start | bytes 442376 | tf_op jit(solution)/shard_map/ppermute | solution.py:557
  120.8 1.9 %collective-permute-start.16 = (bf16[576,128]{1,0:T(8,128)(2,1)S(1)}, bf16[576,128]{1,0:T(8,128)(2,1)S(1)}, u32[]{:S(2)}, u32[]{:S(2)}) collective-permute-start(bf16[576,128]{1,0:T(8,128)(2,1)S(1)} %settle.1.own), channel_id=1, source_target_pairs={{0,8},{1,17},{2,10},{3,19},{4,12},{5,21},{6,14},{7,23},{8,0},{9,25... | collective-permute-start | bytes 442376 | tf_op jit(solution)/shard_map/ppermute | solution.py:557
  122.7 1.5 collective-permute-start.14
  124.7 8.0 %norm_one_back.1 = (f32[2048,512]{1,0:T(8,128)}, f32[40,128]{1,0:T(8,128)S(1)}, f32[40,128]{1,0:T(8,128)S(1)}) custom-call(s32[1]{0:T(128)} %bitcast.tens, bf16[4,2,3,256,512]{4,3,2,1,0:T(8,128)(2,1)S(1)} %get-tuple-element.131.dqkv, bf16[768,512]{1,0:T(8,128)(2,1)S(1)} %bitcast.27, bf16[768,512]{1,0:T(8,128)(2,1)S(1)} %copy-done.3, ...), custom_call_target="tpu_custom_call" | custom-call | flops 10000000000 | tf_op jit(solution)/shard_map/norm_one_back/pallas_call | solution.py:501
  134.1 1.6 collective-permute-start.23
  135.8 2.9 %collective-permute-start.19 = (bf16[192,128]{1,0:T(8,128)(2,1)S(1)}, bf16[192,128]{1,0:T(8,128)(2,1)S(1)}, u32[]{:S(2)}, u32[]{:S(2)}) collective-permute-start(bf16[192,128]{1,0:T(8,128)(2,1)S(1)} %get-tuple-element.147), channel_id=1, source_target_pairs={{0,16},{1,9},{2,18},{3,11},{4,20},{5,13},{6,22},{7,15},{8,24},{9,1... | collective-permute-start | bytes 147464 | tf_op jit(solution)/shard_map/ppermute | solution.py:557
  138.7 1.4 collective-permute-start.20
  140.8 3.8 %collective-permute-done.20.refs_2_ = bf16[192,128]{1,0:T(8,128)(2,1)S(1)} collective-permute-done((bf16[192,128]{1,0:T(8,128)(2,1)S(1)}, bf16[192,128]{1,0:T(8,128)(2,1)S(1)}, u32[]{:S(2)}, u32[]{:S(2)}) %collective-permute-start.20) | collective-permute-done | bytes 49184 | tf_op jit(solution)/shard_map/ppermute | solution.py:557
  145.8 1.6 collective-permute-start.27
  147.4 2.1 %collective-permute-start.25 = (bf16[272,128]{1,0:T(8,128)(2,1)S(1)}, bf16[272,128]{1,0:T(8,128)(2,1)S(1)}, u32[]{:S(2)}, u32[]{:S(2)}) collective-permute-start(bf16[272,128]{1,0:T(8,128)(2,1)S(1)} %settle_cols.1.refs_0_), channel_id=1, source_target_pairs={{0,24},{1,25},{2,26},{3,27},{4,28},{5,29},{6,30},{7,31},{8,16},{9,... | collective-permute-start | bytes 208904 | tf_op jit(solution)/shard_map/ppermute | solution.py:557
  149.5 2.3 %collective-permute-start.22 = (bf16[272,128]{1,0:T(8,128)(2,1)S(1)}, bf16[272,128]{1,0:T(8,128)(2,1)S(1)}, u32[]{:S(2)}, u32[]{:S(2)}) collective-permute-start(bf16[272,128]{1,0:T(8,128)(2,1)S(1)} %settle_cols.1.refs_0_), channel_id=1, source_target_pairs={{0,8},{1,17},{2,10},{3,19},{4,12},{5,21},{6,14},{7,23},{8,0},{9,25... | collective-permute-start | bytes 208904 | tf_op jit(solution)/shard_map/ppermute | solution.py:557
  151.8 1.7 collective-permute-done.25.refs_3_
  153.5 1.5 collective-permute-done.24.refs_2_
  155.6 1.4 collective-permute-start.29
  157.6 1.5 collective-permute-start.26
  159.1 7.3 %block_out.1 = bf16[2048,512]{1,0:T(8,128)(2,1)} custom-call(s32[1]{0:T(128)} %bitcast.tens, bf16[2048,2048]{1,0:T(8,128)(2,1)S(1)} %bitcast.29, bf16[1024,512]{1,0:T(8,128)(2,1)S(1)} %copy-done, bf16[1024,512]{1,0:T(8,128)(2,1)S(1)} %collective-permute-done.3.down_oth, f32[8,512]{1,0:T(8,128)S(1)} %rows_of.1.vecs, f32[2048,512]{1,0:T(8,128)} %get-tuple-element.92.h1_ref), custom_call_target="tpu_custom_call" | custom-call | flops 7000000000 | tf_op jit(solution)/shard_map/block_out/pallas_call | solution.py:347
  166.7 3.2 %finish_mlp.1 = (f32[1024,512]{1,0:T(8,128)}, f32[1024,512]{1,0:T(8,128)}, f32[256,512]{1,0:T(8,128)}) custom-call(s32[2]{0:T(128)S(1)} %pad_add_fusion.3.scalars, bf16[4608,128]{1,0:T(8,128)(2,1)S(1)} %join.3.refs_0_, bf16[4608,128]{1,0:T(8,128)(2,1)S(1)} %collective-permute-done.27.refs_1_), custom_call_target="tpu_custom_call" | custom-call | flops 500000000 | tf_op jit(solution)/shard_map/finish_mlp/pallas_call | solution.py:562
  169.9 1.5 collective-permute-done.26.refs_1_
  171.4 2.0 %finish_qkv.1 = (f32[3,256,512]{2,1,0:T(8,128)}, f32[32,128]{1,0:T(8,128)S(1)}, f32[8,128]{1,0:T(8,128)}) custom-call(s32[4]{0:T(128)S(1)} %pad_add_fusion.1.scalars, bf16[848,128]{1,0:T(8,128)(2,1)S(1)} %join_cols.1.refs_0_, bf16[848,128]{1,0:T(8,128)(2,1)S(1)} %collective-permute-done.26.refs_1_, bf16[848,128]{1,0:T(8,128)(2,1)S(1)} %collective-permute-done.28.refs_2_, ...), custom_call_target="tpu_custom_call" | custom-call | flops 500000000 | tf_op jit(solution)/shard_map/finish_qkv/pallas_call | solution.py:562
  (73 shorter events, 14.3 us)
Async XLA Ops:
  0.6 3.0 %collective-permute-start = (bf16[768,512]{1,0:T(8,128)(2,1)}, bf16[768,512]{1,0:T(8,128)(2,1)S(1)}, u32[]{:S(2)}, u32[]{:S(2)}) collective-permute-start(bf16[768,512]{1,0:T(8,128)(2,1)} %bitcast.25), channel_id=1, source_target_pairs={{0,1},{1,0},{2,3},{3,2},{4,5},{5,4},{6,7},{7,6},{8,9},{9,8},{10,11... | collective-permute-start | bytes 2359304 | tf_op jit(solution)/shard_map/ppermute | solution.py:529
  1.2 2.5 %collective-permute-start.1 = (bf16[256,512]{1,0:T(8,128)(2,1)}, bf16[256,512]{1,0:T(8,128)(2,1)S(1)}, u32[]{:S(2)}, u32[]{:S(2)}) collective-permute-start(bf16[256,512]{1,0:T(8,128)(2,1)} %wo_own.3), channel_id=1, source_target_pairs={{0,1},{1,0},{2,3},{3,2},{4,5},{5,4},{6,7},{7,6},{8,9},{9,8},{10,11... | collective-permute-start | bytes 786440 | tf_op jit(solution)/shard_map/ppermute | solution.py:529
  2.1 23.3 %collective-permute-start.4 = (f32[8,512]{1,0:T(8,128)S(1)}, f32[8,512]{1,0:T(8,128)S(1)}, u32[]{:S(2)}, u32[]{:S(2)}) collective-permute-start(f32[8,512]{1,0:T(8,128)S(1)} %rows_of.1.vecs), channel_id=1, source_target_pairs={{0,1},{1,0},{2,3},{3,2},{4,5},{5,4},{6,7},{7,6},{8,9},{9,8},{10,11... | collective-permute-start | bytes 49160 | tf_op jit(solution)/shard_map/ppermute | solution.py:529
  2.6 22.8 %collective-permute-start.2 = (bf16[1024,512]{1,0:T(8,128)(2,1)}, bf16[1024,512]{1,0:T(8,128)(2,1)S(1)}, u32[]{:S(2)}, u32[]{:S(2)}) collective-permute-start(bf16[1024,512]{1,0:T(8,128)(2,1)} %up_own.1), channel_id=1, source_target_pairs={{0,1},{1,0},{2,3},{3,2},{4,5},{5,4},{6,7},{7,6},{8,9},{9,8},{10,11... | collective-permute-start | bytes 3145736 | tf_op jit(solution)/shard_map/ppermute | solution.py:529
  2.7 22.8 %collective-permute-start.3 = (bf16[1024,512]{1,0:T(8,128)(2,1)}, bf16[1024,512]{1,0:T(8,128)(2,1)S(1)}, u32[]{:S(2)}, u32[]{:S(2)}) collective-permute-start(bf16[1024,512]{1,0:T(8,128)(2,1)} %down_own.3), channel_id=1, source_target_pairs={{0,1},{1,0},{2,3},{3,2},{4,5},{5,4},{6,7},{7,6},{8,9},{9,8},{10,11... | collective-permute-start | bytes 3145736 | tf_op jit(solution)/shard_map/ppermute | solution.py:529
  63.7 5.3 %collective-permute-start.5 = (bf16[9216,128]{1,0:T(8,128)(2,1)}, bf16[9216,128]{1,0:T(8,128)(2,1)S(1)}, u32[]{:S(2)}, u32[]{:S(2)}) collective-permute-start(bf16[9216,128]{1,0:T(8,128)(2,1)} %get-tuple-element.96), channel_id=1, source_target_pairs={{0,1},{1,0},{2,3},{3,2},{4,5},{5,4},{6,7},{7,6},{8,9},{9,8},{10,11... | collective-permute-start | bytes 7077896 | tf_op jit(solution)/shard_map/ppermute | solution.py:529
  71.2 16.9 %collective-permute-start.6 = (bf16[4608,128]{1,0:T(8,128)(2,1)S(1)}, bf16[4608,128]{1,0:T(8,128)(2,1)S(1)}, u32[]{:S(2)}, u32[]{:S(2)}) collective-permute-start(bf16[4608,128]{1,0:T(8,128)(2,1)S(1)} %get-tuple-element.105), channel_id=1, source_target_pairs={{0,2},{1,5},{2,0},{3,7},{4,6},{5,1},{6,4},{7,3},{8,10},{9,13},{10,... | collective-permute-start | bytes 3538952 | tf_op jit(solution)/shard_map/ppermute | solution.py:557
  84.0 31.9 %collective-permute-start.11 = (bf16[3072,128]{1,0:T(8,128)(2,1)S(1)}, bf16[3072,128]{1,0:T(8,128)(2,1)S(1)}, u32[]{:S(2)}, u32[]{:S(2)}) collective-permute-start(bf16[3072,128]{1,0:T(8,128)(2,1)S(1)} %get-tuple-element.108), channel_id=1, source_target_pairs={{0,1},{1,0},{2,3},{3,2},{4,5},{5,4},{6,7},{7,6},{8,9},{9,8},{10,11... | collective-permute-start | bytes 2359304 | tf_op jit(solution)/shard_map/ppermute | solution.py:529
  89.1 10.0 %collective-permute-start.7 = (bf16[2304,128]{1,0:T(8,128)(2,1)S(1)}, bf16[2304,128]{1,0:T(8,128)(2,1)S(1)}, u32[]{:S(2)}, u32[]{:S(2)}) collective-permute-start(bf16[2304,128]{1,0:T(8,128)(2,1)S(1)} %get-tuple-element.111), channel_id=1, source_target_pairs={{0,4},{1,3},{2,6},{3,1},{4,0},{5,7},{6,2},{7,5},{8,12},{9,11},{10,... | collective-permute-start | bytes 1769480 | tf_op jit(solution)/shard_map/ppermute | solution.py:557
  99.8 15.5 %collective-permute-start.10 = (bf16[576,128]{1,0:T(8,128)(2,1)S(1)}, bf16[576,128]{1,0:T(8,128)(2,1)S(1)}, u32[]{:S(2)}, u32[]{:S(2)}) collective-permute-start(bf16[576,128]{1,0:T(8,128)(2,1)S(1)} %get-tuple-element.116), channel_id=1, source_target_pairs={{0,24},{1,25},{2,26},{3,27},{4,28},{5,29},{6,30},{7,31},{8,16},{9,... | collective-permute-start | bytes 442376 | tf_op jit(solution)/shard_map/ppermute | solution.py:557
  104.0 8.3 %collective-permute-start.8 = (bf16[576,128]{1,0:T(8,128)(2,1)S(1)}, bf16[576,128]{1,0:T(8,128)(2,1)S(1)}, u32[]{:S(2)}, u32[]{:S(2)}) collective-permute-start(bf16[576,128]{1,0:T(8,128)(2,1)S(1)} %get-tuple-element.121), channel_id=1, source_target_pairs={{0,8},{1,17},{2,10},{3,19},{4,12},{5,21},{6,14},{7,23},{8,0},{9,25... | collective-permute-start | bytes 442376 | tf_op jit(solution)/shard_map/ppermute | solution.py:557
  104.0 11.3 %collective-permute-start.9 = (bf16[576,128]{1,0:T(8,128)(2,1)S(1)}, bf16[576,128]{1,0:T(8,128)(2,1)S(1)}, u32[]{:S(2)}, u32[]{:S(2)}) collective-permute-start(bf16[576,128]{1,0:T(8,128)(2,1)S(1)} %get-tuple-element.123), channel_id=1, source_target_pairs={{0,16},{1,9},{2,18},{3,11},{4,20},{5,13},{6,22},{7,15},{8,24},{9,1... | collective-permute-start | bytes 442376 | tf_op jit(solution)/shard_map/ppermute | solution.py:557
  115.9 43.2 %slice-start = ((s8[8388608]{0:T(1024)(128)(4,1)}), s8[4194304]{0:T(1024)(128)(4,1)S(1)}, s32[]{:S(2)}) async-start(s8[8388608]{0:T(1024)(128)(4,1)} %bitcast.28), calls=%async_computation | async-start | bytes 8388608
  116.7 7.4 %collective-permute-start.12 = (bf16[768,128]{1,0:T(8,128)(2,1)S(1)}, bf16[768,128]{1,0:T(8,128)(2,1)S(1)}, u32[]{:S(2)}, u32[]{:S(2)}) collective-permute-start(bf16[768,128]{1,0:T(8,128)(2,1)S(1)} %get-tuple-element.128), channel_id=1, source_target_pairs={{0,2},{1,5},{2,0},{3,7},{4,6},{5,1},{6,4},{7,3},{8,10},{9,13},{10,... | collective-permute-start | bytes 589832 | tf_op jit(solution)/shard_map/ppermute | solution.py:557
  118.3 15.2 %collective-permute-start.18 = (bf16[576,128]{1,0:T(8,128)(2,1)S(1)}, bf16[576,128]{1,0:T(8,128)(2,1)S(1)}, u32[]{:S(2)}, u32[]{:S(2)}) collective-permute-start(bf16[576,128]{1,0:T(8,128)(2,1)S(1)} %settle.1.own), channel_id=1, source_target_pairs={{0,24},{1,25},{2,26},{3,27},{4,28},{5,29},{6,30},{7,31},{8,16},{9,... | collective-permute-start | bytes 442376 | tf_op jit(solution)/shard_map/ppermute | solution.py:557
  120.8 12.7 %collective-permute-start.17 = (bf16[576,128]{1,0:T(8,128)(2,1)S(1)}, bf16[576,128]{1,0:T(8,128)(2,1)S(1)}, u32[]{:S(2)}, u32[]{:S(2)}) collective-permute-start(bf16[576,128]{1,0:T(8,128)(2,1)S(1)} %settle.1.own), channel_id=1, source_target_pairs={{0,16},{1,9},{2,18},{3,11},{4,20},{5,13},{6,22},{7,15},{8,24},{9,1... | collective-permute-start | bytes 442376 | tf_op jit(solution)/shard_map/ppermute | solution.py:557
  120.8 12.7 %collective-permute-start.16 = (bf16[576,128]{1,0:T(8,128)(2,1)S(1)}, bf16[576,128]{1,0:T(8,128)(2,1)S(1)}, u32[]{:S(2)}, u32[]{:S(2)}) collective-permute-start(bf16[576,128]{1,0:T(8,128)(2,1)S(1)} %settle.1.own), channel_id=1, source_target_pairs={{0,8},{1,17},{2,10},{3,19},{4,12},{5,21},{6,14},{7,23},{8,0},{9,25... | collective-permute-start | bytes 442376 | tf_op jit(solution)/shard_map/ppermute | solution.py:557
  122.7 10.1 %collective-permute-start.14 = (bf16[768,128]{1,0:T(8,128)(2,1)S(1)}, bf16[768,128]{1,0:T(8,128)(2,1)S(1)}, u32[]{:S(2)}, u32[]{:S(2)}) collective-permute-start(bf16[768,128]{1,0:T(8,128)(2,1)S(1)} %get-tuple-element.129), channel_id=1, source_target_pairs={{0,6},{1,7},{2,4},{3,5},{4,2},{5,3},{6,0},{7,1},{8,14},{9,15},{10,... | collective-permute-start | bytes 589832 | tf_op jit(solution)/shard_map/ppermute | solution.py:557
  124.2 8.6 %collective-permute-start.13 = (bf16[768,128]{1,0:T(8,128)(2,1)S(1)}, bf16[768,128]{1,0:T(8,128)(2,1)S(1)}, u32[]{:S(2)}, u32[]{:S(2)}) collective-permute-start(bf16[768,128]{1,0:T(8,128)(2,1)S(1)} %get-tuple-element.137), channel_id=1, source_target_pairs={{0,4},{1,3},{2,6},{3,1},{4,0},{5,7},{6,2},{7,5},{8,12},{9,11},{10,... | collective-permute-start | bytes 589832 | tf_op jit(solution)/shard_map/ppermute | solution.py:557
  124.7 34.4 %slice-start.1 = ((s8[8388608]{0:T(1024)(128)(4,1)}), s8[4194304]{0:T(1024)(128)(4,1)S(1)}, s32[]{:S(2)}) async-start(s8[8388608]{0:T(1024)(128)(4,1)} %bitcast.28), calls=%async_computation.1 | async-start | bytes 8388608
  134.1 11.1 %collective-permute-start.23 = (bf16[2304,128]{1,0:T(8,128)(2,1)S(1)}, bf16[2304,128]{1,0:T(8,128)(2,1)S(1)}, u32[]{:S(2)}, u32[]{:S(2)}) collective-permute-start(bf16[2304,128]{1,0:T(8,128)(2,1)S(1)} %join.2.own), channel_id=1, source_target_pairs={{0,4},{1,3},{2,6},{3,1},{4,0},{5,7},{6,2},{7,5},{8,12},{9,11},{10,... | collective-permute-start | bytes 1769480 | tf_op jit(solution)/shard_map/ppermute | solution.py:557
  135.6 4.4 %collective-permute-start.15 = (bf16[192,128]{1,0:T(8,128)(2,1)S(1)}, bf16[192,128]{1,0:T(8,128)(2,1)S(1)}, u32[]{:S(2)}, u32[]{:S(2)}) collective-permute-start(bf16[192,128]{1,0:T(8,128)(2,1)S(1)} %get-tuple-element.141), channel_id=1, source_target_pairs={{0,8},{1,17},{2,10},{3,19},{4,12},{5,21},{6,14},{7,23},{8,0},{9,25... | collective-permute-start | bytes 147464 | tf_op jit(solution)/shard_map/ppermute | solution.py:557
  135.8 5.0 %collective-permute-start.19 = (bf16[192,128]{1,0:T(8,128)(2,1)S(1)}, bf16[192,128]{1,0:T(8,128)(2,1)S(1)}, u32[]{:S(2)}, u32[]{:S(2)}) collective-permute-start(bf16[192,128]{1,0:T(8,128)(2,1)S(1)} %get-tuple-element.147), channel_id=1, source_target_pairs={{0,16},{1,9},{2,18},{3,11},{4,20},{5,13},{6,22},{7,15},{8,24},{9,1... | collective-permute-start | bytes 147464 | tf_op jit(solution)/shard_map/ppermute | solution.py:557
  138.7 5.9 %collective-permute-start.20 = (bf16[192,128]{1,0:T(8,128)(2,1)S(1)}, bf16[192,128]{1,0:T(8,128)(2,1)S(1)}, u32[]{:S(2)}, u32[]{:S(2)}) collective-permute-start(bf16[192,128]{1,0:T(8,128)(2,1)S(1)} %get-tuple-element.142), channel_id=1, source_target_pairs={{0,24},{1,25},{2,26},{3,27},{4,28},{5,29},{6,30},{7,31},{8,16},{9,... | collective-permute-start | bytes 147464 | tf_op jit(solution)/shard_map/ppermute | solution.py:557
  140.0 4.5 %collective-permute-start.21 = (f32[40,128]{1,0:T(8,128)S(1)}, f32[40,128]{1,0:T(8,128)S(1)}, u32[]{:S(2)}, u32[]{:S(2)}) collective-permute-start(f32[40,128]{1,0:T(8,128)S(1)} %get-tuple-element.150), channel_id=1, source_target_pairs={{0,1},{1,0},{2,3},{3,2},{4,5},{5,4},{6,7},{7,6},{8,9},{9,8},{10,11... | collective-permute-start | bytes 61448 | tf_op jit(solution)/shard_map/ppermute | solution.py:529
  145.8 20.9 %collective-permute-start.27 = (bf16[4608,128]{1,0:T(8,128)(2,1)S(1)}, bf16[4608,128]{1,0:T(8,128)(2,1)S(1)}, u32[]{:S(2)}, u32[]{:S(2)}) collective-permute-start(bf16[4608,128]{1,0:T(8,128)(2,1)S(1)} %join.3.refs_0_), channel_id=1, source_target_pairs={{0,2},{1,5},{2,0},{3,7},{4,6},{5,1},{6,4},{7,3},{8,10},{9,13},{10,... | collective-permute-start | bytes 3538952 | tf_op jit(solution)/shard_map/ppermute | solution.py:557
  147.4 6.1 %collective-permute-start.25 = (bf16[272,128]{1,0:T(8,128)(2,1)S(1)}, bf16[272,128]{1,0:T(8,128)(2,1)S(1)}, u32[]{:S(2)}, u32[]{:S(2)}) collective-permute-start(bf16[272,128]{1,0:T(8,128)(2,1)S(1)} %settle_cols.1.refs_0_), channel_id=1, source_target_pairs={{0,24},{1,25},{2,26},{3,27},{4,28},{5,29},{6,30},{7,31},{8,16},{9,... | collective-permute-start | bytes 208904 | tf_op jit(solution)/shard_map/ppermute | solution.py:557
  149.5 5.5 %collective-permute-start.24 = (bf16[272,128]{1,0:T(8,128)(2,1)S(1)}, bf16[272,128]{1,0:T(8,128)(2,1)S(1)}, u32[]{:S(2)}, u32[]{:S(2)}) collective-permute-start(bf16[272,128]{1,0:T(8,128)(2,1)S(1)} %settle_cols.1.refs_0_), channel_id=1, source_target_pairs={{0,16},{1,9},{2,18},{3,11},{4,20},{5,13},{6,22},{7,15},{8,24},{9,1... | collective-permute-start | bytes 208904 | tf_op jit(solution)/shard_map/ppermute | solution.py:557
  149.5 5.5 %collective-permute-start.22 = (bf16[272,128]{1,0:T(8,128)(2,1)S(1)}, bf16[272,128]{1,0:T(8,128)(2,1)S(1)}, u32[]{:S(2)}, u32[]{:S(2)}) collective-permute-start(bf16[272,128]{1,0:T(8,128)(2,1)S(1)} %settle_cols.1.refs_0_), channel_id=1, source_target_pairs={{0,8},{1,17},{2,10},{3,19},{4,12},{5,21},{6,14},{7,23},{8,0},{9,25... | collective-permute-start | bytes 208904 | tf_op jit(solution)/shard_map/ppermute | solution.py:557
  155.6 14.3 %collective-permute-start.29 = (bf16[848,128]{1,0:T(8,128)(2,1)S(1)}, bf16[848,128]{1,0:T(8,128)(2,1)S(1)}, u32[]{:S(2)}, u32[]{:S(2)}) collective-permute-start(bf16[848,128]{1,0:T(8,128)(2,1)S(1)} %join_cols.1.refs_0_), channel_id=1, source_target_pairs={{0,6},{1,7},{2,4},{3,5},{4,2},{5,3},{6,0},{7,1},{8,14},{9,15},{10,... | collective-permute-start | bytes 651272 | tf_op jit(solution)/shard_map/ppermute | solution.py:557
  156.9 13.0 %collective-permute-start.28 = (bf16[848,128]{1,0:T(8,128)(2,1)S(1)}, bf16[848,128]{1,0:T(8,128)(2,1)S(1)}, u32[]{:S(2)}, u32[]{:S(2)}) collective-permute-start(bf16[848,128]{1,0:T(8,128)(2,1)S(1)} %join_cols.1.refs_0_), channel_id=1, source_target_pairs={{0,4},{1,3},{2,6},{3,1},{4,0},{5,7},{6,2},{7,5},{8,12},{9,11},{10,... | collective-permute-start | bytes 651272 | tf_op jit(solution)/shard_map/ppermute | solution.py:557
  157.6 13.8 %collective-permute-start.26 = (bf16[848,128]{1,0:T(8,128)(2,1)S(1)}, bf16[848,128]{1,0:T(8,128)(2,1)S(1)}, u32[]{:S(2)}, u32[]{:S(2)}) collective-permute-start(bf16[848,128]{1,0:T(8,128)(2,1)S(1)} %join_cols.1.refs_0_), channel_id=1, source_target_pairs={{0,2},{1,5},{2,0},{3,7},{4,6},{5,1},{6,4},{7,3},{8,10},{9,13},{10,... | collective-permute-start | bytes 651272 | tf_op jit(solution)/shard_map/ppermute | solution.py:557
  (7 other events, 105.6 us)
